TPU v7x, 256 devices: a whole 4x4x8 slice. The times are simulated.
256 devices in a mesh: island: 16 (over z_hi, x, core), zero: 16 (over y, z_lo).
Axes of the slice: x: 4, y: 4, z: 8 (z_hi: 2, z_lo: 4; z = z_hi * 4 + z_lo), core: 2. Of those that a mesh axis runs over, the one named last changes fastest.
Arguments:
- tokens: bfloat16 [131072, 8192], P(('island', 'zero')), may hold values from -6 to 6
- norm_gain: float32 [8192], replicated, may hold values from 0.1 to 1.9
- outer_params: float32 [8192, 512], P('zero'), may hold values from -6 to 6
- momentum: float32 [8192, 512], P('zero'), may hold values from -3 to 3
- local_weights: float32 [16, 8192, 512], P('island', 'zero'), may hold values from -6 to 6
Outputs:
- keys: bfloat16 [131072, 512], P(('island', 'zero'))
- params_out: float32 [8192, 512], P('zero')
- momentum_out: float32 [8192, 512], P('zero')
- mixed: float32 [16, 8192, 512], P('island', 'zero')
All inputs are finite; a program needn't handle non-finite values.
Results may differ from a plain program's by a relative error of at most 0.0057.
Values may be sent and summed in bfloat16 or wider, within the bound.
No kernel may reach another device: no remote copies, remote signals or barrier semaphores. Data moves between devices by JAX's collectives and lax.ppermute only.
A program may use at most 64 MiB of HBM per device.

v0:
```python
import math

import jax
import jax.numpy as jnp
from jax import lax
from jax.sharding import PartitionSpec as P

D = 8192


epsilon = 1e-05
outer_momentum = 0.9
outer_rate = 0.7
mix_share = 0.5


def outer_update(params_part, momentum_part, delta):
    momentum_new = outer_momentum * momentum_part + delta
    params_new = params_part - outer_rate * (delta + outer_momentum * momentum_new)
    return (params_new, momentum_new)


def body(tokens, norm_gain, outer_params, momentum, local_weights):
    values = tokens.astype(jnp.float32)
    scale = lax.rsqrt(jnp.mean(values * values, axis=-1, keepdims=True) + epsilon)
    normed = (values * scale * norm_gain).astype(jnp.bfloat16)
    own_copy = local_weights[0]
    copy_bf = own_copy.astype(jnp.bfloat16)
    summed = jnp.dot(
        normed,
        lax.all_gather(copy_bf, "zero", axis=0, tiled=True),
        preferred_element_type=jnp.float32,
    )
    keys = (summed * (1.0 / math.sqrt(D))).astype(jnp.bfloat16)
    islands = lax.axis_size("island")
    total = lax.psum(outer_params - own_copy, "island")
    params_out, momentum_out = outer_update(outer_params, momentum, total / islands)
    mixed = mix_share * local_weights + (1.0 - mix_share) * params_out[None]
    return (keys, params_out, momentum_out, mixed)


def solution(mesh):
    placed = (
        P(("island", "zero"), None),
        P(),
        P("zero", None),
        P("zero", None),
        P("island", "zero", None),
    )
    return jax.shard_map(
        body,
        mesh=mesh,
        in_specs=placed,
        out_specs=(
            P(("island", "zero"), None),
            P("zero", None),
            P("zero", None),
            P("island", "zero", None),
        ),
        check_vma=False,
    )
```

profile of v0, /device:TPU:34, one launch (start us, length us, event | category | flops | bytes accessed | tf_op | source)
XLA Modules:
  0.0 399.5 jit_solution(17289244942633690979)
XLA Ops:
  7.2 0.0 all-reduce.2.cloned.1.call-start
  7.2 2.7 bitcast_subtract_fusion
  9.9 0.0 all-reduce.2.cloned.1.call-update
  10.0 0.0 copy-start
  10.0 0.0 all-gather.2.cloned.1.call-start
  10.0 175.7 %all-reduce.2.cloned.1.call-done = f32[512,512]{1,0:T(8,128)} async-done(((f32[512,512]{1,0:T(8,128)}), f32[512,512]{1,0:T(8,128)}) %all-reduce.2.cloned.1.call-update) | async-done | bytes 1048592 | tf_op jit(solution)/shard_map/psum | solution.py:36
  185.7 4.4 %fusion.13 = (f32[1,512,512]{2,1,0:T(8,128)}, f32[512,512]{1,0:T(8,128)}, f32[512,512]{1,0:T(8,128)}, bf16[512,512]{1,0:T(8,128)(2,1)}) fusion(f32[1,512,512]{2,1,0:T(8,128)} %param.9, f32[512,512]{1,0:T(8,128)} %param.7, f32[512,512]{1,0:T(8,128)} %all-reduce.2.cloned.1.call-done, f32[512,512]{1,0:T(8,128)} %param.8), kind=kLoop, calls=%fused_computation.11 | loop fusion | flops 2621440 | bytes 7864320 | tf_op jit(solution)/shard_map/add | solution.py:38
  190.1 0.0 all-gather.2.cloned.1.call-update
  190.1 5.1 %fusion = f32[512]{0:T(512)S(1)} fusion(bf16[512,8192]{1,0:T(8,128)(2,1)} %param.5), kind=kLoop, calls=%fused_computation.2 | loop fusion | flops 12582400 | bytes 8390656 | tf_op jit(solution)/shard_map/reduce_sum | solution.py:25
  195.2 186.3 %all-gather.2.cloned.1.call-done = bf16[8192,512]{1,0:T(8,128)(2,1)} async-done(((bf16[512,512]{1,0:T(8,128)(2,1)}), bf16[8192,512]{1,0:T(8,128)(2,1)}) %all-gather.2.cloned.1.call-update) | async-done | bytes 8388624 | tf_op jit(solution)/shard_map/all_gather | solution.py:31
  381.5 0.0 copy-done
  381.5 11.1 %fusion.10 = bf16[512,512]{1,0:T(8,128)(2,1)} fusion(bf16[8192,512]{1,0:T(8,128)(2,1)} %all-gather.2.cloned.1.call-done, bf16[512,8192]{1,0:T(8,128)(2,1)} %param.5, f32[8192]{0:T(1024)S(1)} %copy-done, f32[512]{0:T(512)S(1)} %add_rsqrt_fusion), kind=kOutput, calls=%fused_computation.9 | convolution fusion | flops 4312268800 | bytes 17336320 | tf_op jit(solution)/shard_map/dot_general | solution.py:29
  (1 shorter events, 0.0 us)
Async XLA Ops:
  7.2 178.5 %all-reduce.2.cloned.1.call-start = ((), (), s32[]{:S(2)}) async-start(), calls=%async_computation.1 | async-start | bytes 2097152 | tf_op jit(solution)/shard_map/psum | solution.py:36
  10.0 371.6 %copy-start = (f32[8192]{0:T(1024)S(1)}, f32[8192]{0:T(1024)}, u32[]{:S(2)}) copy-start(f32[8192]{0:T(1024)} %param.6) | copy-start | bytes 98308
  10.0 371.6 %all-gather.2.cloned.1.call-start = ((), (), s32[]{:S(2)}) async-start(), calls=%async_computation | async-start | bytes 8912896 | tf_op jit(solution)/shard_map/all_gather | solution.py:31
Sparse Core Ops, SparseCore 0:
  11.2 174.4 all-reduce.1
  190.3 191.2 all-gather.1
where the time goes:
time: 406 us; the launch traced here: 399 us
  waiting for transfers between devices  362 us (89%)
  between operations  14 us (3%)
  other arithmetic  12.3 us (3%)
  matrix products  11.1 us (3%)
    all_gather x1, waiting for transfers between devices, body(): lax.all_gather(copy_bf, 'zero', axis=0, tiled=True)  186 us
    psum x1, waiting for transfers between devices, body(): total = lax.psum(outer_params - own_copy, 'island')  176 us
    dot_general x1, matrix products, body(): jnp.dot(normed, lax.all_gather(copy_bf, 'zero', axis=0, tiled=True), pref...  11.1 us
  transfers between devices with their start and end apart: 2, of which 2 were waited for; matrix products, arithmetic and copies ran while one was open for 1% of the time, Pallas kernels for 0%

commit v1 on v0

v1 whole, which is shorter than its diff:
```python
import math

import jax
import jax.numpy as jnp
from jax import lax
from jax.experimental import pallas as pl
from jax.experimental.pallas import tpu as pltpu
from jax.sharding import PartitionSpec as P

D = 8192
ROWS = 512

epsilon = 1e-05
outer_momentum = 0.9
outer_rate = 0.7
mix_share = 0.5


def ring_pairs(first):
    pairs = []
    for island in range(16):
        for zero in range(16):
            y, z = divmod(zero, 4)
            partner = y ^ 1 if (island % 2 == 0) == first else 3 - y
            pairs.append((island * 16 + zero, island * 16 + partner * 4 + z))
    return pairs


def swap(bits):
    return [(i, i ^ bits) for i in range(16)]


BOTH = ("island", "zero")


class Order:
    def __init__(self):
        self.last = None

    def __call__(self, value):
        if self.last is not None:
            value = lax.optimization_barrier((value, self.last))[0]
        self.last = value
        return value


def outer_update(params_part, momentum_part, delta):
    momentum_new = outer_momentum * momentum_part + delta
    params_new = params_part - outer_rate * (delta + outer_momentum * momentum_new)
    return (params_new, momentum_new)


CHUNK = 64


def scale_kernel(tokens_ref, scale_ref, held, arrived):
    chunks = tokens_ref.shape[0] // CHUNK

    def fetch(i):
        rows = pl.ds(pl.multiple_of(i * CHUNK, CHUNK), CHUNK)
        return pltpu.make_async_copy(
            tokens_ref.at[rows, :], held.at[lax.rem(i, 2)], arrived.at[lax.rem(i, 2)]
        )

    fetch(0).start()

    @pl.loop(0, chunks)
    def _(i):
        @pl.when(i + 1 < chunks)
        def _():
            fetch(i + 1).start()

        fetch(i).wait()
        values = held[lax.rem(i, 2)].astype(jnp.float32)
        mean = jnp.sum(values * values, axis=-1, keepdims=True) * (1.0 / D)
        rows = pl.ds(pl.multiple_of(i * CHUNK, CHUNK), CHUNK)
        scale_ref[rows, :] = lax.rsqrt(mean + epsilon)


def token_scale(tokens):
    count, width = tokens.shape
    return pl.pallas_call(
        scale_kernel,
        out_shape=jax.ShapeDtypeStruct((count, 1), jnp.float32),
        in_specs=[pl.BlockSpec(memory_space=pltpu.HBM)],
        out_specs=pl.BlockSpec(memory_space=pltpu.VMEM),
        scratch_shapes=[
            pltpu.VMEM((2, CHUNK, width), tokens.dtype),
            pltpu.SemaphoreType.DMA((2,)),
        ],
        compiler_params=pltpu.CompilerParams(vmem_limit_bytes=8 * 1024 * 1024),
        cost_estimate=pl.CostEstimate(
            flops=3 * count * width, bytes_accessed=2 * count * width, transcendentals=0
        ),
        name="token_scale",
    )(tokens)


def send(name, value, axis, pairs):
    with jax.named_scope(name):
        return lax.ppermute(value, axis, pairs)


def split(value, high):
    half = value.shape[0] // 2
    low_part, high_part = value[:half], value[half:]
    return jnp.where(high, high_part, low_part), jnp.where(high, low_part, high_part)


def join(mine, other, high):
    return jnp.concatenate([jnp.where(high, other, mine), jnp.where(high, mine, other)])


def body(tokens, norm_gain, outer_params, momentum, local_weights):
    own_copy = local_weights[0]
    me = lax.axis_index("zero")
    y, z = me // 4, me % 4
    island = lax.axis_index("island")
    core, x = island % 2, island // 2 % 4
    near_y = jnp.where(core == 0, y ^ 1, 3 - y)
    far_y = jnp.where(core == 0, 3 - y, y ^ 1)
    order = Order()
    summed = [0.0]

    def add_product(name, block, row, column):
        start = (row * 4 + column) * ROWS
        with jax.named_scope(name):
            part = lax.dynamic_slice(tokens, (0, start), (tokens.shape[0], ROWS))
            gain = lax.dynamic_slice(norm_gain, (start,), (ROWS,))
            part = (part.astype(jnp.float32) * scale * gain).astype(jnp.bfloat16)
            summed[0] = order(
                summed[0] + jnp.dot(part, block, preferred_element_type=jnp.float32)
            )

    def add_pair(name, pair, column):
        add_product(name, pair[:ROWS], far_y, column)
        add_product(name, pair[ROWS:], y ^ 2, column)

    def pair(block, near):
        return order(jnp.concatenate([block, near]))

    first, second = ring_pairs(True), ring_pairs(False)
    own = order(own_copy.astype(jnp.bfloat16))
    a0 = send("A0", own, BOTH, first)
    z2 = send("Z2", own, "zero", swap(2))
    z1 = send("Z1", own, "zero", swap(1))
    keep, give = split(order(outer_params - own_copy), core == 1)
    k1 = send("K1", order(give), "island", swap(1))

    a0 = order(a0)
    f0 = send("F0", pair(own, a0), BOTH, second)
    total = order(keep + order(k1))
    keep, give = split(total, x % 2 == 1)
    k2 = send("K2", order(give), "island", swap(2))

    scale = order(token_scale(order(tokens)))

    total = order(keep + order(k2))
    keep, give = split(total, x // 2 == 1)
    k3 = send("K3", order(give), "island", swap(4))

    z1 = order(z1)
    a1 = send("A1", z1, BOTH, first)
    z2 = order(z2)
    a2 = send("A2", z2, BOTH, first)
    total = order(keep + order(k3))
    high = send("HIGH", total, "island", swap(8))
    z3 = send("Z3", order(own), "zero", swap(3))
    f0 = order(f0)
    zf = send("ZF", f0, "zero", swap(1))

    add_product("dot0", own, y, z)
    add_product("dot0", a0, near_y, z)
    add_pair("dot0", f0, z)
    add_product("dot1", z1, y, z ^ 1)
    add_product("dot2", z2, y, z ^ 2)

    a1 = order(a1)
    a2 = order(a2)
    f2 = send("F2", pair(z2, a2), BOTH, second)
    add_product("dot1", a1, near_y, z ^ 1)
    add_product("dot2", a2, near_y, z ^ 2)

    total = order(total + order(high))
    k4 = send("K4", total, "island", swap(4))

    z3 = order(z3)
    a3 = send("A3", z3, BOTH, first)
    add_product("dot3", z3, y, z ^ 3)
    total = order(join(total, order(k4), x // 2 == 1))
    k5 = send("K5", total, "island", swap(2))

    f2 = order(f2)
    add_pair("dot2", f2, z ^ 2)

    a3 = order(a3)
    f3 = send("F3", pair(z3, a3), BOTH, second)
    add_product("dot3", a3, near_y, z ^ 3)

    total = order(join(total, order(k5), x % 2 == 1))
    k6 = send("K6", total, "island", swap(1))

    add_pair("dot1", order(zf), z ^ 1)

    total = order(join(total, order(k6), core == 1))
    islands = lax.axis_size("island")
    params_out, momentum_out = outer_update(outer_params, momentum, total / islands)
    mixed = mix_share * local_weights + (1.0 - mix_share) * params_out[None]
    params_out, momentum_out, mixed = lax.optimization_barrier(
        (params_out, momentum_out, mixed)
    )
    order.last = (order.last, params_out)

    add_pair("dot3", order(f3), z ^ 3)
    keys = (summed[0] * (1.0 / math.sqrt(D))).astype(jnp.bfloat16)
    return (keys, params_out, momentum_out, mixed)


def solution(mesh):
    placed = (
        P(("island", "zero"), None),
        P(),
        P("zero", None),
        P("zero", None),
        P("island", "zero", None),
    )
    return jax.shard_map(
        body,
        mesh=mesh,
        in_specs=placed,
        out_specs=(
            P(("island", "zero"), None),
            P("zero", None),
            P("zero", None),
            P("island", "zero", None),
        ),
        check_vma=False,
    )
```

time: 406 us -> 105 us (0.26); the launches traced: 399 us -> 103 us
  waiting for transfers between devices: 362 us -> 40.7 us
  starting transfers between devices: 0.08 us -> 30.7 us
  between operations: 14 us -> 1.01 us
    all_gather x1 -> x0, waiting for transfers between devices: 186 us -> none  [body(): lax.all_gather(copy_bf, 'zero', axis=0, tiled=True)]
    psum x1 -> x0, waiting for transfers between devices: 176 us -> none  [body(): total = lax.psum(outer_params - own_copy, 'island')]
    ppermute x0 -> x18, waiting for transfers between devices: none -> 40.7 us  [send(): return lax.ppermute(value, axis, pairs)]
    ppermute x0 -> x18, starting transfers between devices: none -> 30.7 us  [send(): return lax.ppermute(value, axis, pairs)]
    reduce_sum x1 -> x0, other arithmetic: 5.1 us -> none  [body(): jnp.mean(values * values, axis=-1, keepdims=True) + epsilon]
    dot_general x1 -> x16, matrix products: 11.1 us -> 13.5 us  [add_product(): jnp.dot(part, block, preferred_element_type=jnp.float32)]
  transfers between devices with their start and end apart: 2 -> 18, of which waited for: 2 -> 7; matrix products, arithmetic and copies ran while one was open for 1% -> 20% of each run, Pallas kernels for 0% -> 3%
where the time goes in v1:
time: 105 us; the launch traced here: 103 us
  waiting for transfers between devices  40.7 us (39%)
  starting transfers between devices  30.7 us (29%)
  matrix products  13.5 us (13%)
  other arithmetic  10.8 us (10%)
  local copies, waits for them, and re-layouts  3.55 us (3%)
  Pallas kernels  3.13 us (3%)
    ppermute x18, waiting for transfers between devices, send(): return lax.ppermute(value, axis, pairs)  40.7 us
    ppermute x18, starting transfers between devices, send(): return lax.ppermute(value, axis, pairs)  30.7 us
    dot_general x16, matrix products, add_product(): jnp.dot(part, block, preferred_element_type=jnp.float32)  13.5 us
    unnamed x14, local copies, waits for them, and re-layouts  3.42 us
    pallas_call x1, Pallas kernels, token_scale(): pl.pallas_call(scale_kernel, out_shape=jax.ShapeDtypeStruct((count, 1), j...  3.13 us
  transfers between devices with their start and end apart: 18, of which 7 were waited for; matrix products, arithmetic and copies ran while one was open for 20% of the time, Pallas kernels for 3%

profile of v1, /device:TPU:34, one launch (start us, length us, event | category | flops | bytes accessed | tf_op | source)
XLA Modules:
  0.0 103.5 jit_solution(2148964401373220119)
XLA Ops:
  0.6 1.3 %bitcast_convert_fusion = bf16[512,512]{1,0:T(8,128)(2,1)S(1)} fusion(f32[1,512,512]{2,1,0:T(8,128)} %param.9), kind=kLoop, calls=%fused_computation.21 | loop fusion | flops 262144 | bytes 1572864 | tf_op jit(solution)/shard_map/convert_element_type | solution.py:143
  1.9 1.7 %collective-permute-start.1 = (bf16[512,512]{1,0:T(8,128)(2,1)S(1)}, bf16[512,512]{1,0:T(8,128)(2,1)S(1)}, u32[]{:S(2)}, u32[]{:S(2)}) collective-permute-start(bf16[512,512]{1,0:T(8,128)(2,1)S(1)} %bitcast_convert_fusion), channel_id=1, source_target_pairs={{0,4},{1,5},{2,6},{3,7},{4,0},{5,1},{6,2},{7,3},{8,12},{9,13},{10,... | collective-permute-start | bytes 1572872 | tf_op jit(solution)/shard_map/A0/ppermute | solution.py:101
  3.6 1.7 %bitcast_subtract_fusion = f32[512,512]{1,0:T(8,128)S(1)} fusion(f32[512,512]{1,0:T(8,128)} %param.7, f32[1,512,512]{2,1,0:T(8,128)} %param.9), kind=kLoop, calls=%fused_computation.22 | loop fusion | flops 262144 | bytes 3145728 | tf_op jit(solution)/shard_map/sub | solution.py:147
  5.5 1.1 %collective-permute-start = (f32[256,512]{1,0:T(8,128)S(1)}, f32[256,512]{1,0:T(8,128)S(1)}, u32[]{:S(2)}, u32[]{:S(2)}) collective-permute-start(f32[256,512]{1,0:T(8,128)S(1)} %slice_select_fusion), channel_id=1, source_target_pairs={{0,16},{16,0},{32,48},{48,32},{64,80},{80,64},{96,112},{112,96},{1... | collective-permute-start | bytes 1572872 | tf_op jit(solution)/shard_map/K1/ppermute | solution.py:101
  6.5 4.7 %collective-permute-done.1 = bf16[512,512]{1,0:T(8,128)(2,1)S(1)} collective-permute-done((bf16[512,512]{1,0:T(8,128)(2,1)S(1)}, bf16[512,512]{1,0:T(8,128)(2,1)S(1)}, u32[]{:S(2)}, u32[]{:S(2)}) %collective-permute-start.1) | collective-permute-done | bytes 524320 | tf_op jit(solution)/shard_map/A0/ppermute | solution.py:101
  11.2 1.0 %pad_maximum_fusion = bf16[1024,512]{1,0:T(8,128)(2,1)} fusion(bf16[512,512]{1,0:T(8,128)(2,1)S(1)} %collective-permute-done.1, bf16[512,512]{1,0:T(8,128)(2,1)S(1)} %bitcast_convert_fusion), kind=kLoop, calls=%fused_computation.15 | loop fusion | flops 2097152 | bytes 2097152 | tf_op jit(solution)/shard_map/concatenate | solution.py:140
  12.4 0.7 slice_select_fusion.1
  13.1 0.5 collective-permute-start.3
  13.7 3.3 %collective-permute-start.5 = (bf16[512,512]{1,0:T(8,128)(2,1)S(1)}, bf16[512,512]{1,0:T(8,128)(2,1)S(1)}, u32[]{:S(2)}, u32[]{:S(2)}) collective-permute-start(bf16[512,512]{1,0:T(8,128)(2,1)S(1)} %bitcast_convert_fusion), channel_id=1, source_target_pairs={{0,2},{1,3},{2,0},{3,1},{4,6},{5,7},{6,4},{7,5},{8,10},{9,11},{10,... | collective-permute-start | bytes 1572872 | tf_op jit(solution)/shard_map/Z2/ppermute | solution.py:101
  17.1 3.0 %collective-permute-start.2 = (bf16[1024,512]{1,0:T(8,128)(2,1)}, bf16[1024,512]{1,0:T(8,128)(2,1)S(1)}, u32[]{:S(2)}, u32[]{:S(2)}) collective-permute-start(bf16[1024,512]{1,0:T(8,128)(2,1)} %pad_maximum_fusion), channel_id=1, source_target_pairs={{0,12},{1,13},{2,14},{3,15},{4,8},{5,9},{6,10},{7,11},{8,4},{9,5},... | collective-permute-start | bytes 3145736 | tf_op jit(solution)/shard_map/F0/ppermute | solution.py:101
  20.2 3.4 %copy-done = bf16[512,8192]{1,0:T(8,128)(2,1)S(1)} copy-done((bf16[512,8192]{1,0:T(8,128)(2,1)S(1)}, bf16[512,8192]{1,0:T(8,128)(2,1)}, u32[]{:S(2)}) %copy-start) | copy-done | bytes 8388632
  23.6 3.1 %token_scale.1 = f32[512,1]{1,0:T(8,128)S(1)} custom-call(bf16[512,8192]{1,0:T(8,128)(2,1)S(1)} %copy-done), custom_call_target="tpu_custom_call" | custom-call | flops 12582912 | bytes 8388608 | tf_op jit(solution)/shard_map/token_scale/pallas_call | solution.py:82
  26.9 1.2 %select_add_fusion.1 = f32[128,512]{1,0:T(8,128)S(1)} fusion(f32[128,512]{1,0:T(8,128)} %collective-permute-done.3, f32[256,512]{1,0:T(8,128)S(1)} %select_add_fusion, pred[]{:T(512)S(6)} %eq.22), kind=kLoop, calls=%fused_computation.103 | loop fusion | flops 131072 | bytes 1048577 | tf_op jit(solution)/shard_map/add | solution.py:158
  28.1 2.5 %collective-permute-start.4 = (f32[64,512]{1,0:T(8,128)S(1)}, f32[64,512]{1,0:T(8,128)S(1)}, u32[]{:S(2)}, u32[]{:S(2)}) collective-permute-start(f32[64,512]{1,0:T(8,128)S(1)} %slice_select_fusion.2), channel_id=1, source_target_pairs={{0,64},{16,80},{32,96},{48,112},{64,0},{80,16},{96,32},{112,48},{1... | collective-permute-start | bytes 393224 | tf_op jit(solution)/shard_map/K3/ppermute | solution.py:101
  30.6 1.5 %fusion.1 = f32[512,512]{1,0:T(8,128)S(1)} fusion(bf16[512,512]{1,0:T(8,128)(2,1)S(1)} %bitcast_convert_fusion, f32[512]{0:T(512)S(1)} %get-tuple-element.134, f32[512]{0:T(512)S(1)} %reduce, bf16[512,8192]{1,0:T(8,128)(2,1)} %tokens_ref, s32[]{:T(128)S(6)} %select_n.164), kind=kOutput, calls=%fused_computation.42 | convolution fusion | flops 269484032 | bytes 2101252 | tf_op jit(solution)/shard_map/dot0/dot_general | solution.py:132
  32.1 7.8 %collective-permute-done.6 = bf16[512,512]{1,0:T(8,128)(2,1)} collective-permute-done((bf16[512,512]{1,0:T(8,128)(2,1)S(1)}, bf16[512,512]{1,0:T(8,128)(2,1)}, u32[]{:S(2)}, u32[]{:S(2)}) %collective-permute-start.6) | collective-permute-done | bytes 524320 | tf_op jit(solution)/shard_map/Z1/ppermute | solution.py:101
  39.9 0.6 collective-permute-start.7
  40.5 1.4 %collective-permute-start.8 = (bf16[512,512]{1,0:T(8,128)(2,1)S(1)}, bf16[512,512]{1,0:T(8,128)(2,1)S(1)}, u32[]{:S(2)}, u32[]{:S(2)}) collective-permute-start(bf16[512,512]{1,0:T(8,128)(2,1)S(1)} %collective-permute-done.5), channel_id=1, source_target_pairs={{0,4},{1,5},{2,6},{3,7},{4,0},{5,1},{6,2},{7,3},{8,12},{9,13},{10,... | collective-permute-start | bytes 1572872 | tf_op jit(solution)/shard_map/A2/ppermute | solution.py:101
  42.0 5.5 %collective-permute-start.10 = (f32[64,512]{1,0:T(8,128)S(1)}, f32[64,512]{1,0:T(8,128)S(1)}, u32[]{:S(2)}, u32[]{:S(2)}) collective-permute-start(f32[64,512]{1,0:T(8,128)S(1)} %select_add_fusion.2), channel_id=1, source_target_pairs={{0,128},{16,144},{32,160},{48,176},{64,192},{80,208},{96,224},{112... | collective-permute-start | bytes 393224 | tf_op jit(solution)/shard_map/HIGH/ppermute | solution.py:101
  47.5 1.0 collective-permute-start.9
  48.5 0.8 collective-permute-start.14
  49.3 1.5 %convolution_add_fusion.14 = f32[512,512]{1,0:T(8,128)S(1)} fusion(f32[512,512]{1,0:T(8,128)S(1)} %fusion.1, bf16[512,512]{1,0:T(8,128)(2,1)S(1)} %collective-permute-done.1, f32[512]{0:T(512)S(1)} %get-tuple-element.133, bf16[512,8192]{1,0:T(8,128)(2,1)} %tokens_ref, s32[]{:T(128)S(6)} %select_n.180, f32[512]{0:T(512)S(1)} %reduce), kind=kOutput, calls=%fused_computation.14 | convolution fusion | flops 269746176 | bytes 3149828 | tf_op jit(solution)/shard_map/dot0/dot_general | solution.py:132
  50.8 1.7 %convolution_add_fusion.13 = f32[512,512]{1,0:T(8,128)S(1)} fusion(f32[512,512]{1,0:T(8,128)S(1)} %convolution_add_fusion.14, bf16[1024,512]{1,0:T(8,128)(2,1)S(1)} %collective-permute-done.2, f32[512]{0:T(512)S(1)} %get-tuple-element.132, bf16[512,8192]{1,0:T(8,128)(2,1)} %tokens_ref, s32[]{:T(128)S(6)} %select_n.182, f32[512]{0:T(512)S(1)} %reduce), kind=kOutput, calls=%fused_computation.13 | convolution fusion | flops 269746176 | bytes 3149828 | tf_op jit(solution)/shard_map/dot0/dot_general | solution.py:132
  52.5 1.5 %convolution_add_fusion.12 = f32[512,512]{1,0:T(8,128)S(1)} fusion(f32[512,512]{1,0:T(8,128)S(1)} %convolution_add_fusion.13, bf16[1024,512]{1,0:T(8,128)(2,1)S(1)} %collective-permute-done.2, f32[512]{0:T(512)S(1)} %get-tuple-element.131, bf16[512,8192]{1,0:T(8,128)(2,1)} %tokens_ref, s32[]{:T(128)S(6)} %select_n.183, f32[512]{0:T(512)S(1)} %reduce), kind=kOutput, calls=%fused_computation.12 | convolution fusion | flops 269746176 | bytes 3149828 | tf_op jit(solution)/shard_map/dot0/dot_general | solution.py:132
  54.1 1.7 %convolution_add_fusion.11 = f32[512,512]{1,0:T(8,128)S(1)} fusion(f32[512,512]{1,0:T(8,128)S(1)} %convolution_add_fusion.12, bf16[512,512]{1,0:T(8,128)(2,1)} %collective-permute-done.6, f32[512]{0:T(512)S(1)} %get-tuple-element.130, bf16[512,8192]{1,0:T(8,128)(2,1)} %tokens_ref, s32[]{:T(128)S(6)} %select_n.184, f32[512]{0:T(512)S(1)} %reduce), kind=kOutput, calls=%fused_computation.11 | convolution fusion | flops 269746176 | bytes 3149828 | tf_op jit(solution)/shard_map/dot1/dot_general | solution.py:132
  55.8 0.5 convolution_add_fusion.10
  56.4 2.6 %collective-permute-start.11 = (bf16[1024,512]{1,0:T(8,128)(2,1)S(1)}, bf16[1024,512]{1,0:T(8,128)(2,1)S(1)}, u32[]{:S(2)}, u32[]{:S(2)}) collective-permute-start(bf16[1024,512]{1,0:T(8,128)(2,1)S(1)} %pad_maximum_fusion.1), channel_id=1, source_target_pairs={{0,12},{1,13},{2,14},{3,15},{4,8},{5,9},{6,10},{7,11},{8,4},{9,5},... | collective-permute-start | bytes 3145736 | tf_op jit(solution)/shard_map/F2/ppermute | solution.py:101
  59.0 0.5 convolution_add_fusion.9
  59.5 0.5 convolution_add_fusion.8
  60.0 4.6 %collective-permute-done.10 = f32[64,512]{1,0:T(8,128)S(1)} collective-permute-done((f32[64,512]{1,0:T(8,128)S(1)}, f32[64,512]{1,0:T(8,128)S(1)}, u32[]{:S(2)}, u32[]{:S(2)}) %collective-permute-start.10) | collective-permute-done | bytes 131104 | tf_op jit(solution)/shard_map/HIGH/ppermute | solution.py:101
  64.7 2.7 %collective-permute-start.12 = (f32[64,512]{1,0:T(8,128)S(1)}, f32[64,512]{1,0:T(8,128)S(1)}, u32[]{:S(2)}, u32[]{:S(2)}) collective-permute-start(f32[64,512]{1,0:T(8,128)S(1)} %add.228), channel_id=1, source_target_pairs={{0,64},{16,80},{32,96},{48,112},{64,0},{80,16},{96,32},{112,48},{1... | collective-permute-start | bytes 393224 | tf_op jit(solution)/shard_map/K4/ppermute | solution.py:101
  67.4 8.8 %collective-permute-done.9 = bf16[512,512]{1,0:T(8,128)(2,1)S(1)} collective-permute-done((bf16[512,512]{1,0:T(8,128)(2,1)S(1)}, bf16[512,512]{1,0:T(8,128)(2,1)S(1)}, u32[]{:S(2)}, u32[]{:S(2)}) %collective-permute-start.9) | collective-permute-done | bytes 524320 | tf_op jit(solution)/shard_map/Z3/ppermute | solution.py:101
  76.2 0.5 convolution_add_fusion.7
  76.7 1.6 %collective-permute-start.15 = (f32[128,512]{1,0:T(8,128)S(1)}, f32[128,512]{1,0:T(8,128)S(1)}, u32[]{:S(2)}, u32[]{:S(2)}) collective-permute-start(f32[128,512]{1,0:T(8,128)S(1)} %pad_maximum_fusion.5), channel_id=1, source_target_pairs={{0,32},{16,48},{32,0},{48,16},{64,96},{80,112},{96,64},{112,80},{1... | collective-permute-start | bytes 786440 | tf_op jit(solution)/shard_map/K5/ppermute | solution.py:101
  78.3 0.5 convolution_add_fusion.6
  78.8 0.5 convolution_add_fusion.5
  79.3 6.0 %collective-permute-done.13 = bf16[512,512]{1,0:T(8,128)(2,1)S(1)} collective-permute-done((bf16[512,512]{1,0:T(8,128)(2,1)S(1)}, bf16[512,512]{1,0:T(8,128)(2,1)S(1)}, u32[]{:S(2)}, u32[]{:S(2)}) %collective-permute-start.13) | collective-permute-done | bytes 524320 | tf_op jit(solution)/shard_map/A3/ppermute | solution.py:101
  85.4 2.3 %collective-permute-start.16 = (bf16[1024,512]{1,0:T(8,128)(2,1)S(1)}, bf16[1024,512]{1,0:T(8,128)(2,1)S(1)}, u32[]{:S(2)}, u32[]{:S(2)}) collective-permute-start(bf16[1024,512]{1,0:T(8,128)(2,1)S(1)} %pad_maximum_fusion.2), channel_id=1, source_target_pairs={{0,12},{1,13},{2,14},{3,15},{4,8},{5,9},{6,10},{7,11},{8,4},{9,5},... | collective-permute-start | bytes 3145736 | tf_op jit(solution)/shard_map/F3/ppermute | solution.py:101
  87.7 0.5 convolution_add_fusion.4
  88.5 0.5 convolution_add_fusion.3
  89.0 0.5 convolution_add_fusion.2
  89.5 0.9 collective-permute-done.17
  90.5 1.2 %multiply_add_fusion = f32[512,512]{1,0:T(8,128)} fusion(f32[512,512]{1,0:T(8,128)S(1)} %copy-done.3, f32[512,512]{1,0:T(8,128)S(1)} %pad_maximum_fusion.3), kind=kLoop, calls=%fused_computation.26 | loop fusion | flops 786432 | bytes 3145728 | tf_op jit(solution)/shard_map/add | solution.py:48
  91.7 1.8 %fusion = (f32[1,512,512]{2,1,0:T(8,128)}, f32[512,512]{1,0:T(8,128)}) fusion(f32[1,512,512]{2,1,0:T(8,128)S(1)} %copy-done.1, f32[512,512]{1,0:T(8,128)S(1)} %copy-done.2, f32[512,512]{1,0:T(8,128)S(1)} %copy-done.3, f32[512,512]{1,0:T(8,128)S(1)} %pad_maximum_fusion.3), kind=kLoop, calls=%fused_computation.20 | loop fusion | flops 2359296 | bytes 6291456 | tf_op jit(solution)/shard_map/add | solution.py:208
  93.6 8.0 %collective-permute-done.16 = bf16[1024,512]{1,0:T(8,128)(2,1)S(1)} collective-permute-done((bf16[1024,512]{1,0:T(8,128)(2,1)S(1)}, bf16[1024,512]{1,0:T(8,128)(2,1)S(1)}, u32[]{:S(2)}, u32[]{:S(2)}) %collective-permute-start.16) | collective-permute-done | bytes 1048608 | tf_op jit(solution)/shard_map/F3/ppermute | solution.py:101
  101.5 0.5 convolution_add_fusion.1
  102.0 0.5 convolution_add_fusion
  102.5 0.9 multiply_convert_fusion
  (43 shorter events, 1.3 us)
Async XLA Ops:
  0.6 19.4 %copy-start.4 = (f32[8192]{0:T(1024)S(1)}, f32[8192]{0:T(1024)}, u32[]{:S(2)}) copy-start(f32[8192]{0:T(1024)} %param.6) | copy-start | bytes 98308
  1.9 9.3 %collective-permute-start.1 = (bf16[512,512]{1,0:T(8,128)(2,1)S(1)}, bf16[512,512]{1,0:T(8,128)(2,1)S(1)}, u32[]{:S(2)}, u32[]{:S(2)}) collective-permute-start(bf16[512,512]{1,0:T(8,128)(2,1)S(1)} %bitcast_convert_fusion), channel_id=1, source_target_pairs={{0,4},{1,5},{2,6},{3,7},{4,0},{5,1},{6,2},{7,3},{8,12},{9,13},{10,... | collective-permute-start | bytes 1572872 | tf_op jit(solution)/shard_map/A0/ppermute | solution.py:101
  5.5 6.8 %collective-permute-start = (f32[256,512]{1,0:T(8,128)S(1)}, f32[256,512]{1,0:T(8,128)S(1)}, u32[]{:S(2)}, u32[]{:S(2)}) collective-permute-start(f32[256,512]{1,0:T(8,128)S(1)} %slice_select_fusion), channel_id=1, source_target_pairs={{0,16},{16,0},{32,48},{48,32},{64,80},{80,64},{96,112},{112,96},{1... | collective-permute-start | bytes 1572872 | tf_op jit(solution)/shard_map/K1/ppermute | solution.py:101
  13.1 13.7 %collective-permute-start.3 = (f32[128,512]{1,0:T(8,128)}, f32[128,512]{1,0:T(8,128)}, u32[]{:S(2)}, u32[]{:S(2)}) collective-permute-start(f32[128,512]{1,0:T(8,128)} %slice_select_fusion.1), channel_id=1, source_target_pairs={{0,32},{16,48},{32,0},{48,16},{64,96},{80,112},{96,64},{112,80},{1... | collective-permute-start | bytes 786440 | tf_op jit(solution)/shard_map/K2/ppermute | solution.py:101
  13.7 26.8 %collective-permute-start.5 = (bf16[512,512]{1,0:T(8,128)(2,1)S(1)}, bf16[512,512]{1,0:T(8,128)(2,1)S(1)}, u32[]{:S(2)}, u32[]{:S(2)}) collective-permute-start(bf16[512,512]{1,0:T(8,128)(2,1)S(1)} %bitcast_convert_fusion), channel_id=1, source_target_pairs={{0,2},{1,3},{2,0},{3,1},{4,6},{5,7},{6,4},{7,5},{8,10},{9,11},{10,... | collective-permute-start | bytes 1572872 | tf_op jit(solution)/shard_map/Z2/ppermute | solution.py:101
  16.9 23.0 %collective-permute-start.6 = (bf16[512,512]{1,0:T(8,128)(2,1)S(1)}, bf16[512,512]{1,0:T(8,128)(2,1)}, u32[]{:S(2)}, u32[]{:S(2)}) collective-permute-start(bf16[512,512]{1,0:T(8,128)(2,1)S(1)} %bitcast_convert_fusion), channel_id=1, source_target_pairs={{0,1},{1,0},{2,3},{3,2},{4,5},{5,4},{6,7},{7,6},{8,9},{9,8},{10,11... | collective-permute-start | bytes 1572872 | tf_op jit(solution)/shard_map/Z1/ppermute | solution.py:101
  17.1 31.4 %collective-permute-start.2 = (bf16[1024,512]{1,0:T(8,128)(2,1)}, bf16[1024,512]{1,0:T(8,128)(2,1)S(1)}, u32[]{:S(2)}, u32[]{:S(2)}) collective-permute-start(bf16[1024,512]{1,0:T(8,128)(2,1)} %pad_maximum_fusion), channel_id=1, source_target_pairs={{0,12},{1,13},{2,14},{3,15},{4,8},{5,9},{6,10},{7,11},{8,4},{9,5},... | collective-permute-start | bytes 3145736 | tf_op jit(solution)/shard_map/F0/ppermute | solution.py:101
  20.2 3.4 %copy-start = (bf16[512,8192]{1,0:T(8,128)(2,1)S(1)}, bf16[512,8192]{1,0:T(8,128)(2,1)}, u32[]{:S(2)}) copy-start(bf16[512,8192]{1,0:T(8,128)(2,1)} %tokens_ref) | copy-start | bytes 25165828
  26.9 28.9 %slice-start = ((s8[8388608]{0:T(1024)(128)(4,1)}), s8[4194304]{0:T(1024)(128)(4,1)S(1)}, s32[]{:S(2)}) async-start(s8[8388608]{0:T(1024)(128)(4,1)} %bitcast.15), calls=%async_computation | async-start | bytes 8388608
  28.1 13.9 %collective-permute-start.4 = (f32[64,512]{1,0:T(8,128)S(1)}, f32[64,512]{1,0:T(8,128)S(1)}, u32[]{:S(2)}, u32[]{:S(2)}) collective-permute-start(f32[64,512]{1,0:T(8,128)S(1)} %slice_select_fusion.2), channel_id=1, source_target_pairs={{0,64},{16,80},{32,96},{48,112},{64,0},{80,16},{96,32},{112,48},{1... | collective-permute-start | bytes 393224 | tf_op jit(solution)/shard_map/K3/ppermute | solution.py:101
  39.9 16.4 %collective-permute-start.7 = (bf16[512,512]{1,0:T(8,128)(2,1)}, bf16[512,512]{1,0:T(8,128)(2,1)S(1)}, u32[]{:S(2)}, u32[]{:S(2)}) collective-permute-start(bf16[512,512]{1,0:T(8,128)(2,1)} %collective-permute-done.6), channel_id=1, source_target_pairs={{0,4},{1,5},{2,6},{3,7},{4,0},{5,1},{6,2},{7,3},{8,12},{9,13},{10,... | collective-permute-start | bytes 1572872 | tf_op jit(solution)/shard_map/A1/ppermute | solution.py:101
  40.5 15.8 %collective-permute-start.8 = (bf16[512,512]{1,0:T(8,128)(2,1)S(1)}, bf16[512,512]{1,0:T(8,128)(2,1)S(1)}, u32[]{:S(2)}, u32[]{:S(2)}) collective-permute-start(bf16[512,512]{1,0:T(8,128)(2,1)S(1)} %collective-permute-done.5), channel_id=1, source_target_pairs={{0,4},{1,5},{2,6},{3,7},{4,0},{5,1},{6,2},{7,3},{8,12},{9,13},{10,... | collective-permute-start | bytes 1572872 | tf_op jit(solution)/shard_map/A2/ppermute | solution.py:101
  42.0 22.7 %collective-permute-start.10 = (f32[64,512]{1,0:T(8,128)S(1)}, f32[64,512]{1,0:T(8,128)S(1)}, u32[]{:S(2)}, u32[]{:S(2)}) collective-permute-start(f32[64,512]{1,0:T(8,128)S(1)} %select_add_fusion.2), channel_id=1, source_target_pairs={{0,128},{16,144},{32,160},{48,176},{64,192},{80,208},{96,224},{112... | collective-permute-start | bytes 393224 | tf_op jit(solution)/shard_map/HIGH/ppermute | solution.py:101
  47.5 28.7 %collective-permute-start.9 = (bf16[512,512]{1,0:T(8,128)(2,1)S(1)}, bf16[512,512]{1,0:T(8,128)(2,1)S(1)}, u32[]{:S(2)}, u32[]{:S(2)}) collective-permute-start(bf16[512,512]{1,0:T(8,128)(2,1)S(1)} %bitcast_convert_fusion), channel_id=1, source_target_pairs={{0,3},{1,2},{2,1},{3,0},{4,7},{5,6},{6,5},{7,4},{8,11},{9,10},{10,... | collective-permute-start | bytes 1572872 | tf_op jit(solution)/shard_map/Z3/ppermute | solution.py:101
  48.5 40.0 %collective-permute-start.14 = (bf16[1024,512]{1,0:T(8,128)(2,1)S(1)}, bf16[1024,512]{1,0:T(8,128)(2,1)S(1)}, u32[]{:S(2)}, u32[]{:S(2)}) collective-permute-start(bf16[1024,512]{1,0:T(8,128)(2,1)S(1)} %collective-permute-done.2), channel_id=1, source_target_pairs={{0,1},{1,0},{2,3},{3,2},{4,5},{5,4},{6,7},{7,6},{8,9},{9,8},{10,11... | collective-permute-start | bytes 3145736 | tf_op jit(solution)/shard_map/ZF/ppermute | solution.py:101
  50.8 5.0 %slice-start.1 = ((s8[8388608]{0:T(1024)(128)(4,1)}), s8[4194304]{0:T(1024)(128)(4,1)S(1)}, s32[]{:S(2)}) async-start(s8[8388608]{0:T(1024)(128)(4,1)} %bitcast.15), calls=%async_computation.1 | async-start | bytes 8388608
  56.4 21.9 %collective-permute-start.11 = (bf16[1024,512]{1,0:T(8,128)(2,1)S(1)}, bf16[1024,512]{1,0:T(8,128)(2,1)S(1)}, u32[]{:S(2)}, u32[]{:S(2)}) collective-permute-start(bf16[1024,512]{1,0:T(8,128)(2,1)S(1)} %pad_maximum_fusion.1), channel_id=1, source_target_pairs={{0,12},{1,13},{2,14},{3,15},{4,8},{5,9},{6,10},{7,11},{8,4},{9,5},... | collective-permute-start | bytes 3145736 | tf_op jit(solution)/shard_map/F2/ppermute | solution.py:101
  64.7 12.0 %collective-permute-start.12 = (f32[64,512]{1,0:T(8,128)S(1)}, f32[64,512]{1,0:T(8,128)S(1)}, u32[]{:S(2)}, u32[]{:S(2)}) collective-permute-start(f32[64,512]{1,0:T(8,128)S(1)} %add.228), channel_id=1, source_target_pairs={{0,64},{16,80},{32,96},{48,112},{64,0},{80,16},{96,32},{112,48},{1... | collective-permute-start | bytes 393224 | tf_op jit(solution)/shard_map/K4/ppermute | solution.py:101
  76.2 9.2 %collective-permute-start.13 = (bf16[512,512]{1,0:T(8,128)(2,1)S(1)}, bf16[512,512]{1,0:T(8,128)(2,1)S(1)}, u32[]{:S(2)}, u32[]{:S(2)}) collective-permute-start(bf16[512,512]{1,0:T(8,128)(2,1)S(1)} %collective-permute-done.9), channel_id=1, source_target_pairs={{0,4},{1,5},{2,6},{3,7},{4,0},{5,1},{6,2},{7,3},{8,12},{9,13},{10,... | collective-permute-start | bytes 1572872 | tf_op jit(solution)/shard_map/A3/ppermute | solution.py:101
  76.7 11.5 %collective-permute-start.15 = (f32[128,512]{1,0:T(8,128)S(1)}, f32[128,512]{1,0:T(8,128)S(1)}, u32[]{:S(2)}, u32[]{:S(2)}) collective-permute-start(f32[128,512]{1,0:T(8,128)S(1)} %pad_maximum_fusion.5), channel_id=1, source_target_pairs={{0,32},{16,48},{32,0},{48,16},{64,96},{80,112},{96,64},{112,80},{1... | collective-permute-start | bytes 786440 | tf_op jit(solution)/shard_map/K5/ppermute | solution.py:101
  85.4 5.1 %copy-start.3 = (f32[512,512]{1,0:T(8,128)S(1)}, f32[512,512]{1,0:T(8,128)}, u32[]{:S(2)}) copy-start(f32[512,512]{1,0:T(8,128)} %param.8) | copy-start | bytes 3145732
  85.4 16.1 %collective-permute-start.16 = (bf16[1024,512]{1,0:T(8,128)(2,1)S(1)}, bf16[1024,512]{1,0:T(8,128)(2,1)S(1)}, u32[]{:S(2)}, u32[]{:S(2)}) collective-permute-start(bf16[1024,512]{1,0:T(8,128)(2,1)S(1)} %pad_maximum_fusion.2), channel_id=1, source_target_pairs={{0,12},{1,13},{2,14},{3,15},{4,8},{5,9},{6,10},{7,11},{8,4},{9,5},... | collective-permute-start | bytes 3145736 | tf_op jit(solution)/shard_map/F3/ppermute | solution.py:101
  88.2 3.5 %copy-start.1 = (f32[1,512,512]{2,1,0:T(8,128)S(1)}, f32[1,512,512]{2,1,0:T(8,128)}, u32[]{:S(2)}) copy-start(f32[1,512,512]{2,1,0:T(8,128)} %param.9) | copy-start | bytes 3145732
  88.2 3.5 %copy-start.2 = (f32[512,512]{1,0:T(8,128)S(1)}, f32[512,512]{1,0:T(8,128)}, u32[]{:S(2)}) copy-start(f32[512,512]{1,0:T(8,128)} %param.7) | copy-start | bytes 3145732
  88.3 2.0 %collective-permute-start.17 = (f32[256,512]{1,0:T(8,128)S(1)}, f32[256,512]{1,0:T(8,128)S(1)}, u32[]{:S(2)}, u32[]{:S(2)}) collective-permute-start(f32[256,512]{1,0:T(8,128)S(1)} %pad_maximum_fusion.4), channel_id=1, source_target_pairs={{0,16},{16,0},{32,48},{48,32},{64,80},{80,64},{96,112},{112,96},{1... | collective-permute-start | bytes 1572872 | tf_op jit(solution)/shard_map/K6/ppermute | solution.py:101

commit v2 on v1

v2 whole, which is shorter than its diff:
```python
import math

import jax
import jax.numpy as jnp
from jax import lax
from jax.experimental import pallas as pl
from jax.experimental.pallas import tpu as pltpu
from jax.sharding import PartitionSpec as P

D = 8192
ROWS = 512

epsilon = 1e-05
outer_momentum = 0.9
outer_rate = 0.7
mix_share = 0.5


def ring_pairs(first):
    pairs = []
    for island in range(16):
        for zero in range(16):
            y, z = divmod(zero, 4)
            partner = y ^ 1 if (island % 2 == 0) == first else 3 - y
            pairs.append((island * 16 + zero, island * 16 + partner * 4 + z))
    return pairs


def swap(bits):
    return [(i, i ^ bits) for i in range(16)]


def middle_swap():
    pairs = []
    for island in range(16):
        for zero in range(16):
            y, z = divmod(zero, 4)
            there = island if z in (1, 2) else island ^ 8
            pairs.append((island * 16 + zero, there * 16 + y * 4 + 3 - z))
    return pairs


BOTH = ("island", "zero")


class Order:
    def __init__(self):
        self.last = None

    def __call__(self, value):
        if self.last is not None:
            value = lax.optimization_barrier((value, self.last))[0]
        self.last = value
        return value


def outer_update(params_part, momentum_part, delta):
    momentum_new = outer_momentum * momentum_part + delta
    params_new = params_part - outer_rate * (delta + outer_momentum * momentum_new)
    return (params_new, momentum_new)


CHUNK = 64
DEPTH = 4


def norm_kernel(tokens_ref, gain_ref, normed_ref, held, arrived):
    step, steps = pl.program_id(0), pl.num_programs(0)

    def fetch(i):
        rows = pl.ds(pl.multiple_of(i * CHUNK, CHUNK), CHUNK)
        slot = lax.rem(i, DEPTH)
        return pltpu.make_async_copy(tokens_ref.at[rows, :], held.at[slot], arrived.at[slot])

    @pl.when(step == 0)
    def _():
        for i in range(DEPTH - 1):
            fetch(i).start()

    @pl.when(step + DEPTH - 1 < steps)
    def _():
        fetch(step + DEPTH - 1).start()

    fetch(step).wait()
    values = held[lax.rem(step, DEPTH)].astype(jnp.float32)
    mean = jnp.sum(values * values, axis=-1, keepdims=True) * (1.0 / D)
    scale = lax.rsqrt(mean + epsilon)
    normed_ref[...] = (values * scale * gain_ref[...]).astype(jnp.bfloat16)


def normalise(tokens, gain):
    count, width = tokens.shape
    return pl.pallas_call(
        norm_kernel,
        out_shape=jax.ShapeDtypeStruct(tokens.shape, tokens.dtype),
        grid=(count // CHUNK,),
        in_specs=[
            pl.BlockSpec(memory_space=pltpu.HBM),
            pl.BlockSpec((1, width), lambda i: (0, 0)),
        ],
        out_specs=pl.BlockSpec((CHUNK, width), lambda i: (i, 0)),
        scratch_shapes=[
            pltpu.VMEM((DEPTH, CHUNK, width), tokens.dtype),
            pltpu.SemaphoreType.DMA((DEPTH,)),
        ],
        compiler_params=pltpu.CompilerParams(vmem_limit_bytes=12 * 1024 * 1024),
        cost_estimate=pl.CostEstimate(
            flops=6 * count * width, bytes_accessed=4 * count * width, transcendentals=0
        ),
        name="normalise",
    )(pltpu.with_memory_space_constraint(tokens, pltpu.HBM), gain)


def send(name, value, axis, pairs):
    with jax.named_scope(name):
        return lax.ppermute(value, axis, pairs)


def split(value, high):
    half = value.shape[0] // 2
    low_part, high_part = value[:half], value[half:]
    return jnp.where(high, high_part, low_part), jnp.where(high, low_part, high_part)


def join(mine, other, high):
    return jnp.concatenate([jnp.where(high, other, mine), jnp.where(high, mine, other)])


def body(tokens, norm_gain, outer_params, momentum, local_weights):
    own_copy = local_weights[0]
    me = lax.axis_index("zero")
    y, z = me // 4, me % 4
    island = lax.axis_index("island")
    core, x = island % 2, island // 2 % 4
    near_y = jnp.where(core == 0, y ^ 1, 3 - y)
    far_y = jnp.where(core == 0, 3 - y, y ^ 1)
    order = Order()
    summed = [0.0]

    def add_product(name, block, row, column):
        start = (row * 4 + column) * ROWS
        with jax.named_scope(name):
            part = lax.dynamic_slice(normed, (0, start), (normed.shape[0], ROWS))
            summed[0] = order(
                summed[0] + jnp.dot(part, block, preferred_element_type=jnp.float32)
            )

    first, second = ring_pairs(True), ring_pairs(False)
    inner = (z == 1) | (z == 2)

    own = order(own_copy.astype(jnp.bfloat16))
    z1 = send("Z1", own, "zero", swap(1))
    m1 = send("M1", own, BOTH, middle_swap())
    a0 = send("A0", own, BOTH, first)
    b0 = send("B0", own, BOTH, second)
    keep, give = split(order(outer_params - own_copy), core == 1)
    k1 = send("K1", order(give), "island", swap(1))
    a0 = order(a0)
    c0 = send("C0", a0, BOTH, second)
    b0 = order(b0)
    m1 = order(m1)
    e2 = send("E2", m1, "zero", swap(1))
    z1 = order(z1)
    m2 = send("M2", z1, BOTH, middle_swap())
    a1 = send("A1", z1, BOTH, first)
    total = order(keep + order(k1))
    keep, give = split(total, x % 2 == 1)
    k2 = send("K2", order(give), "island", swap(2))
    normed = order(normalise(tokens, order(norm_gain[None])))
    total = order(keep + order(k2))
    b1 = send("B1", order(z1), BOTH, second)
    keep, give = split(total, x // 2 == 1)
    k3 = send("K3", order(give), "island", swap(4))
    c0 = order(c0)
    m2 = order(m2)
    s2 = order(jnp.where(inner, m2, order(e2)))
    a2 = send("A2", s2, BOTH, first)
    b2 = send("B2", s2, BOTH, second)
    e3 = send("E3", m2, "zero", swap(1))
    a1 = order(a1)
    total = order(keep + order(k3))
    high = send("HIGH", order(total), "island", swap(8))
    add_product("dot0", own, y, z)
    add_product("dot0", a0, near_y, z)
    a2 = order(a2)
    c2 = send("C2", a2, BOTH, second)
    s3 = order(jnp.where(inner, m1, order(e3)))
    a3 = send("A3", s3, BOTH, first)
    b3 = send("B3", s3, BOTH, second)
    b1 = order(b1)
    c1 = send("ZC", order(c0), "zero", swap(1))
    add_product("dot0", b0, far_y, z)
    add_product("dot0", c0, y ^ 2, z)
    add_product("dot1", z1, y, z ^ 1)
    add_product("dot1", a1, near_y, z ^ 1)
    add_product("dot1", b1, far_y, z ^ 1)
    add_product("dot2", s2, y, z ^ 2)
    total = order(total + order(high))
    k4 = send("K4", total, "island", swap(4))
    b2 = order(b2)
    add_product("dot2", a2, near_y, z ^ 2)
    add_product("dot2", b2, far_y, z ^ 2)
    add_product("dot3", s3, y, z ^ 3)
    c2 = order(c2)
    total = order(join(total, order(k4), x // 2 == 1))
    k5 = send("K5", total, "island", swap(2))
    a3 = order(a3)
    c3 = send("C3", a3, BOTH, second)
    add_product("dot2", c2, y ^ 2, z ^ 2)
    add_product("dot3", a3, near_y, z ^ 3)
    add_product("dot3", order(b3), far_y, z ^ 3)
    total = order(join(total, order(k5), x % 2 == 1))
    k6 = send("K6", total, "island", swap(1))
    add_product("dot1", order(c1), y ^ 2, z ^ 1)
    add_product("dot3", order(c3), y ^ 2, z ^ 3)
    keys = order((summed[0] * (1.0 / math.sqrt(D))).astype(jnp.bfloat16))
    total = order(join(total, order(k6), core == 1))
    islands = lax.axis_size("island")
    params_out, momentum_out = outer_update(outer_params, momentum, total / islands)
    mixed = mix_share * local_weights + (1.0 - mix_share) * params_out[None]
    return (keys, params_out, momentum_out, mixed)


def solution(mesh):
    placed = (
        P(("island", "zero"), None),
        P(),
        P("zero", None),
        P("zero", None),
        P("island", "zero", None),
    )
    return jax.shard_map(
        body,
        mesh=mesh,
        in_specs=placed,
        out_specs=(
            P(("island", "zero"), None),
            P("zero", None),
            P("zero", None),
            P("island", "zero", None),
        ),
        check_vma=False,
    )
```

time: 105 us -> 83.9 us (0.80)
  waiting for transfers between devices: 40.7 us -> 14.6 us
  starting transfers between devices: 30.7 us -> 42.9 us
  other arithmetic: 10.8 us -> 6.81 us
  local copies, waits for them, and re-layouts: 3.55 us -> 0.02 us
  Pallas kernels: 3.13 us -> 6.49 us
  matrix products: 13.5 us -> 10.2 us
    ppermute x18 -> x24, waiting for transfers between devices: 40.7 us -> 14.6 us  [send(): return lax.ppermute(value, axis, pairs)]
    ppermute x18 -> x24, starting transfers between devices: 30.7 us -> 42.9 us  [send(): return lax.ppermute(value, axis, pairs)]
    unnamed x14 -> x8, local copies, waits for them, and re-layouts: 3.42 us -> 0.02 us
    pallas_call x1, Pallas kernels: 3.13 us -> 6.49 us  [normalise(): pl.pallas_call(norm_kernel, out_shape=jax.ShapeDtypeStruct(tokens.shape,...]
    dot_general x16, matrix products: 13.5 us -> 10.2 us  [add_product(): jnp.dot(part, block, preferred_element_type=jnp.float32)]
    add x1 -> x0, other arithmetic: 1.2 us -> none  [outer_update(): momentum_new = outer_momentum * momentum_part + delta]
    concatenate x3 -> x0, other arithmetic: 1.18 us -> none  [pair(): return order(jnp.concatenate([block, near]))]
    add x1, other arithmetic: 1.16 us -> 0.05 us  [body(): total = order(keep + order(k2))]
  transfers between devices with their start and end apart: 18 -> 24, of which waited for: 7 -> 7; matrix products, arithmetic and copies ran while one was open for 20% -> 16% of each run, Pallas kernels for 3% -> 8%
where the time goes in v2:
time: 83.9 us; the launch traced here: 82.3 us
  starting transfers between devices  42.9 us (51%)
  waiting for transfers between devices  14.6 us (17%)
  matrix products  10.2 us (12%)
  other arithmetic  6.81 us (8%)
  Pallas kernels  6.49 us (8%)
  between operations  1.2 us (1%)
    ppermute x24, starting transfers between devices, send(): return lax.ppermute(value, axis, pairs)  42.9 us
    ppermute x24, waiting for transfers between devices, send(): return lax.ppermute(value, axis, pairs)  14.6 us
    dot_general x16, matrix products, add_product(): jnp.dot(part, block, preferred_element_type=jnp.float32)  10.2 us
    pallas_call x1, Pallas kernels, normalise(): pl.pallas_call(norm_kernel, out_shape=jax.ShapeDtypeStruct(tokens.shape,...  6.49 us
    add x1, other arithmetic, body(): mixed = mix_share * local_weights + (1.0 - mix_share) * params_out[None]  2.06 us
    sub x1, other arithmetic, body(): keep, give = split(order(outer_params - own_copy), core == 1)  1.75 us
  transfers between devices with their start and end apart: 24, of which 7 were waited for; matrix products, arithmetic and copies ran while one was open for 16% of the time, Pallas kernels for 8%

profile of v2, /device:TPU:34, one launch (start us, length us, event | category | flops | bytes accessed | tf_op | source)
XLA Modules:
  0.0 82.3 jit_solution(3493886635670522779)
XLA Ops:
  0.6 1.3 %bitcast_convert_fusion = bf16[512,512]{1,0:T(8,128)(2,1)S(1)} fusion(f32[1,512,512]{2,1,0:T(8,128)} %param.9), kind=kLoop, calls=%fused_computation.18 | loop fusion | flops 262144 | bytes 1572864 | tf_op jit(solution)/shard_map/convert_element_type | solution.py:151
  1.9 1.7 %collective-permute-start.4 = (bf16[512,512]{1,0:T(8,128)(2,1)S(1)}, bf16[512,512]{1,0:T(8,128)(2,1)}, u32[]{:S(2)}, u32[]{:S(2)}) collective-permute-start(bf16[512,512]{1,0:T(8,128)(2,1)S(1)} %bitcast_convert_fusion), channel_id=1, source_target_pairs={{0,4},{1,5},{2,6},{3,7},{4,0},{5,1},{6,2},{7,3},{8,12},{9,13},{10,... | collective-permute-start | bytes 1572872 | tf_op jit(solution)/shard_map/A0/ppermute | solution.py:116
  3.6 2.2 %collective-permute-start.3 = (bf16[512,512]{1,0:T(8,128)(2,1)S(1)}, bf16[512,512]{1,0:T(8,128)(2,1)}, u32[]{:S(2)}, u32[]{:S(2)}) collective-permute-start(bf16[512,512]{1,0:T(8,128)(2,1)S(1)} %bitcast_convert_fusion), channel_id=1, source_target_pairs={{0,12},{1,13},{2,14},{3,15},{4,8},{5,9},{6,10},{7,11},{8,4},{9,5},... | collective-permute-start | bytes 1572872 | tf_op jit(solution)/shard_map/B0/ppermute | solution.py:116
  5.8 1.9 %collective-permute-start.2 = (bf16[512,512]{1,0:T(8,128)(2,1)S(1)}, bf16[512,512]{1,0:T(8,128)(2,1)S(1)}, u32[]{:S(2)}, u32[]{:S(2)}) collective-permute-start(bf16[512,512]{1,0:T(8,128)(2,1)S(1)} %bitcast_convert_fusion), channel_id=1, source_target_pairs={{0,131},{1,2},{2,1},{3,128},{4,135},{5,6},{6,5},{7,132},{8,139},{9... | collective-permute-start | bytes 1572872 | tf_op jit(solution)/shard_map/M1/ppermute | solution.py:116
  7.7 4.0 %collective-permute-start.1 = (bf16[512,512]{1,0:T(8,128)(2,1)S(1)}, bf16[512,512]{1,0:T(8,128)(2,1)}, u32[]{:S(2)}, u32[]{:S(2)}) collective-permute-start(bf16[512,512]{1,0:T(8,128)(2,1)S(1)} %bitcast_convert_fusion), channel_id=1, source_target_pairs={{0,1},{1,0},{2,3},{3,2},{4,5},{5,4},{6,7},{7,6},{8,9},{9,8},{10,11... | collective-permute-start | bytes 1572872 | tf_op jit(solution)/shard_map/Z1/ppermute | solution.py:116
  11.8 1.7 %bitcast_subtract_fusion = f32[512,512]{1,0:T(8,128)S(1)} fusion(f32[512,512]{1,0:T(8,128)} %param.7, f32[1,512,512]{2,1,0:T(8,128)} %param.9), kind=kLoop, calls=%fused_computation.19 | loop fusion | flops 262144 | bytes 3145728 | tf_op jit(solution)/shard_map/sub | solution.py:156
  13.9 1.7 %collective-permute-done.4 = bf16[512,512]{1,0:T(8,128)(2,1)} collective-permute-done((bf16[512,512]{1,0:T(8,128)(2,1)S(1)}, bf16[512,512]{1,0:T(8,128)(2,1)}, u32[]{:S(2)}, u32[]{:S(2)}) %collective-permute-start.4) | collective-permute-done | bytes 524320 | tf_op jit(solution)/shard_map/A0/ppermute | solution.py:116
  15.6 3.3 %collective-permute-start.9 = (bf16[512,512]{1,0:T(8,128)(2,1)}, bf16[512,512]{1,0:T(8,128)(2,1)S(1)}, u32[]{:S(2)}, u32[]{:S(2)}) collective-permute-start(bf16[512,512]{1,0:T(8,128)(2,1)} %collective-permute-done.4), channel_id=1, source_target_pairs={{0,12},{1,13},{2,14},{3,15},{4,8},{5,9},{6,10},{7,11},{8,4},{9,5},... | collective-permute-start | bytes 1572872 | tf_op jit(solution)/shard_map/C0/ppermute | solution.py:116
  18.9 3.7 %collective-permute-start.10 = (bf16[512,512]{1,0:T(8,128)(2,1)S(1)}, bf16[512,512]{1,0:T(8,128)(2,1)S(1)}, u32[]{:S(2)}, u32[]{:S(2)}) collective-permute-start(bf16[512,512]{1,0:T(8,128)(2,1)S(1)} %collective-permute-done.2), channel_id=1, source_target_pairs={{0,1},{1,0},{2,3},{3,2},{4,5},{5,4},{6,7},{7,6},{8,9},{9,8},{10,11... | collective-permute-start | bytes 1572872 | tf_op jit(solution)/shard_map/E2/ppermute | solution.py:116
  22.7 0.4 collective-permute-done.1
  23.1 1.1 %collective-permute-start.8 = (bf16[512,512]{1,0:T(8,128)(2,1)}, bf16[512,512]{1,0:T(8,128)(2,1)S(1)}, u32[]{:S(2)}, u32[]{:S(2)}) collective-permute-start(bf16[512,512]{1,0:T(8,128)(2,1)} %collective-permute-done.1), channel_id=1, source_target_pairs={{0,131},{1,2},{2,1},{3,128},{4,135},{5,6},{6,5},{7,132},{8,139},{9... | collective-permute-start | bytes 1572872 | tf_op jit(solution)/shard_map/M2/ppermute | solution.py:116
  24.2 1.2 %collective-permute-start.7 = (bf16[512,512]{1,0:T(8,128)(2,1)}, bf16[512,512]{1,0:T(8,128)(2,1)S(1)}, u32[]{:S(2)}, u32[]{:S(2)}) collective-permute-start(bf16[512,512]{1,0:T(8,128)(2,1)} %collective-permute-done.1), channel_id=1, source_target_pairs={{0,4},{1,5},{2,6},{3,7},{4,0},{5,1},{6,2},{7,3},{8,12},{9,13},{10,... | collective-permute-start | bytes 1572872 | tf_op jit(solution)/shard_map/A1/ppermute | solution.py:116
  25.6 0.6 collective-permute-start.5
  26.2 6.5 %normalise.1 = bf16[512,8192]{1,0:T(8,128)(2,1)S(1)} custom-call(bf16[512,8192]{1,0:T(8,128)(2,1)} %tokens_ref.1, f32[1,8192]{1,0:T(1,128)S(1)} %bitcast.24), custom_call_target="tpu_custom_call" | custom-call | flops 25165824 | bytes 16777216 | tf_op jit(solution)/shard_map/normalise/pallas_call | solution.py:93
  33.2 0.5 collective-permute-start.11
  33.7 2.5 %collective-permute-start.6 = (f32[64,512]{1,0:T(8,128)S(1)}, f32[64,512]{1,0:T(8,128)S(1)}, u32[]{:S(2)}, u32[]{:S(2)}) collective-permute-start(f32[64,512]{1,0:T(8,128)S(1)} %slice_select_fusion.2), channel_id=1, source_target_pairs={{0,64},{16,80},{32,96},{48,112},{64,0},{80,16},{96,32},{112,48},{1... | collective-permute-start | bytes 393224 | tf_op jit(solution)/shard_map/K3/ppermute | solution.py:116
  36.2 2.0 %collective-permute-start.12 = (bf16[512,512]{1,0:T(8,128)(2,1)S(1)}, bf16[512,512]{1,0:T(8,128)(2,1)S(1)}, u32[]{:S(2)}, u32[]{:S(2)}) collective-permute-start(bf16[512,512]{1,0:T(8,128)(2,1)S(1)} %collective-permute-done.8), channel_id=1, source_target_pairs={{0,1},{1,0},{2,3},{3,2},{4,5},{5,4},{6,7},{7,6},{8,9},{9,8},{10,11... | collective-permute-start | bytes 1572872 | tf_op jit(solution)/shard_map/E3/ppermute | solution.py:116
  38.3 1.7 %collective-permute-start.13 = (bf16[512,512]{1,0:T(8,128)(2,1)S(1)}, bf16[512,512]{1,0:T(8,128)(2,1)S(1)}, u32[]{:S(2)}, u32[]{:S(2)}) collective-permute-start(bf16[512,512]{1,0:T(8,128)(2,1)S(1)} %broadcast_select_fusion.1), channel_id=1, source_target_pairs={{0,4},{1,5},{2,6},{3,7},{4,0},{5,1},{6,2},{7,3},{8,12},{9,13},{10,... | collective-permute-start | bytes 1572872 | tf_op jit(solution)/shard_map/A2/ppermute | solution.py:116
  40.1 1.2 %collective-permute-start.14 = (bf16[512,512]{1,0:T(8,128)(2,1)S(1)}, bf16[512,512]{1,0:T(8,128)(2,1)S(1)}, u32[]{:S(2)}, u32[]{:S(2)}) collective-permute-start(bf16[512,512]{1,0:T(8,128)(2,1)S(1)} %broadcast_select_fusion.1), channel_id=1, source_target_pairs={{0,12},{1,13},{2,14},{3,15},{4,8},{5,9},{6,10},{7,11},{8,4},{9,5},... | collective-permute-start | bytes 1572872 | tf_op jit(solution)/shard_map/B2/ppermute | solution.py:116
  41.3 3.6 %collective-permute-start.15 = (f32[64,512]{1,0:T(8,128)S(1)}, f32[64,512]{1,0:T(8,128)S(1)}, u32[]{:S(2)}, u32[]{:S(2)}) collective-permute-start(f32[64,512]{1,0:T(8,128)S(1)} %select_add_fusion.2), channel_id=1, source_target_pairs={{0,128},{16,144},{32,160},{48,176},{64,192},{80,208},{96,224},{112... | collective-permute-start | bytes 393224 | tf_op jit(solution)/shard_map/HIGH/ppermute | solution.py:116
  44.9 1.5 %convolution_add_fusion.14 = f32[512,512]{1,0:T(8,128)S(1)} fusion(f32[512,512]{1,0:T(8,128)S(1)} %fusion.16, bf16[512,512]{1,0:T(8,128)(2,1)} %collective-permute-done.4, bf16[512,8192]{1,0:T(8,128)(2,1)S(1)} %normalise.1, s32[]{:T(128)S(6)} %select_n.178), kind=kOutput, calls=%fused_computation.14 | convolution fusion | flops 268697600 | bytes 3145732 | tf_op jit(solution)/shard_map/dot0/dot_general | solution.py:145
  46.4 1.5 %convolution_add_fusion.13 = f32[512,512]{1,0:T(8,128)S(1)} fusion(f32[512,512]{1,0:T(8,128)S(1)} %convolution_add_fusion.14, bf16[512,512]{1,0:T(8,128)(2,1)} %collective-permute-done.3, bf16[512,8192]{1,0:T(8,128)(2,1)S(1)} %normalise.1, s32[]{:T(128)S(6)} %select_n.180), kind=kOutput, calls=%fused_computation.13 | convolution fusion | flops 268697600 | bytes 3145732 | tf_op jit(solution)/shard_map/dot0/dot_general | solution.py:145
  47.9 3.6 %collective-permute-done.13 = bf16[512,512]{1,0:T(8,128)(2,1)S(1)} collective-permute-done((bf16[512,512]{1,0:T(8,128)(2,1)S(1)}, bf16[512,512]{1,0:T(8,128)(2,1)S(1)}, u32[]{:S(2)}, u32[]{:S(2)}) %collective-permute-start.13) | collective-permute-done | bytes 524320 | tf_op jit(solution)/shard_map/A2/ppermute | solution.py:116
  51.5 0.9 %collective-permute-start.16 = (bf16[512,512]{1,0:T(8,128)(2,1)S(1)}, bf16[512,512]{1,0:T(8,128)(2,1)S(1)}, u32[]{:S(2)}, u32[]{:S(2)}) collective-permute-start(bf16[512,512]{1,0:T(8,128)(2,1)S(1)} %collective-permute-done.13), channel_id=1, source_target_pairs={{0,12},{1,13},{2,14},{3,15},{4,8},{5,9},{6,10},{7,11},{8,4},{9,5},... | collective-permute-start | bytes 1572872 | tf_op jit(solution)/shard_map/C2/ppermute | solution.py:116
  52.4 0.8 %collective-permute-start.17 = (bf16[512,512]{1,0:T(8,128)(2,1)S(1)}, bf16[512,512]{1,0:T(8,128)(2,1)S(1)}, u32[]{:S(2)}, u32[]{:S(2)}) collective-permute-start(bf16[512,512]{1,0:T(8,128)(2,1)S(1)} %broadcast_select_fusion), channel_id=1, source_target_pairs={{0,4},{1,5},{2,6},{3,7},{4,0},{5,1},{6,2},{7,3},{8,12},{9,13},{10,... | collective-permute-start | bytes 1572872 | tf_op jit(solution)/shard_map/A3/ppermute | solution.py:116
  53.3 1.7 %collective-permute-start.19 = (bf16[512,512]{1,0:T(8,128)(2,1)S(1)}, bf16[512,512]{1,0:T(8,128)(2,1)S(1)}, u32[]{:S(2)}, u32[]{:S(2)}) collective-permute-start(bf16[512,512]{1,0:T(8,128)(2,1)S(1)} %broadcast_select_fusion), channel_id=1, source_target_pairs={{0,12},{1,13},{2,14},{3,15},{4,8},{5,9},{6,10},{7,11},{8,4},{9,5},... | collective-permute-start | bytes 1572872 | tf_op jit(solution)/shard_map/B3/ppermute | solution.py:116
  55.0 0.4 convolution_add_fusion.12
  55.4 1.5 %convolution_add_fusion.11 = f32[512,512]{1,0:T(8,128)S(1)} fusion(f32[512,512]{1,0:T(8,128)S(1)} %convolution_add_fusion.12, bf16[512,512]{1,0:T(8,128)(2,1)} %collective-permute-done.1, bf16[512,8192]{1,0:T(8,128)(2,1)S(1)} %normalise.1, s32[]{:T(128)S(6)} %select_n.183), kind=kOutput, calls=%fused_computation.11 | convolution fusion | flops 268697600 | bytes 3145732 | tf_op jit(solution)/shard_map/dot1/dot_general | solution.py:145
  56.9 0.4 convolution_add_fusion.10
  57.4 0.4 convolution_add_fusion.9
  58.3 1.5 %collective-permute-start.20 = (bf16[512,512]{1,0:T(8,128)(2,1)S(1)}, bf16[512,512]{1,0:T(8,128)(2,1)S(1)}, u32[]{:S(2)}, u32[]{:S(2)}) collective-permute-start(bf16[512,512]{1,0:T(8,128)(2,1)S(1)} %collective-permute-done.9), channel_id=1, source_target_pairs={{0,1},{1,0},{2,3},{3,2},{4,5},{5,4},{6,7},{7,6},{8,9},{9,8},{10,11... | collective-permute-start | bytes 1572872 | tf_op jit(solution)/shard_map/ZC/ppermute | solution.py:116
  59.8 2.3 %collective-permute-start.18 = (f32[64,512]{1,0:T(8,128)S(1)}, f32[64,512]{1,0:T(8,128)S(1)}, u32[]{:S(2)}, u32[]{:S(2)}) collective-permute-start(f32[64,512]{1,0:T(8,128)S(1)} %add.213), channel_id=1, source_target_pairs={{0,64},{16,80},{32,96},{48,112},{64,0},{80,16},{96,32},{112,48},{1... | collective-permute-start | bytes 393224 | tf_op jit(solution)/shard_map/K4/ppermute | solution.py:116
  62.1 0.4 convolution_add_fusion.7
  62.5 0.4 convolution_add_fusion.6
  63.0 0.4 convolution_add_fusion.5
  63.4 3.0 %collective-permute-done.16 = bf16[512,512]{1,0:T(8,128)(2,1)S(1)} collective-permute-done((bf16[512,512]{1,0:T(8,128)(2,1)S(1)}, bf16[512,512]{1,0:T(8,128)(2,1)S(1)}, u32[]{:S(2)}, u32[]{:S(2)}) %collective-permute-start.16) | collective-permute-done | bytes 524320 | tf_op jit(solution)/shard_map/C2/ppermute | solution.py:116
  66.5 0.6 collective-permute-done.18
  67.1 1.2 %collective-permute-start.21 = (f32[128,512]{1,0:T(8,128)S(1)}, f32[128,512]{1,0:T(8,128)S(1)}, u32[]{:S(2)}, u32[]{:S(2)}) collective-permute-start(f32[128,512]{1,0:T(8,128)S(1)} %pad_maximum_fusion.2), channel_id=1, source_target_pairs={{0,32},{16,48},{32,0},{48,16},{64,96},{80,112},{96,64},{112,80},{1... | collective-permute-start | bytes 786440 | tf_op jit(solution)/shard_map/K5/ppermute | solution.py:116
  68.3 3.1 %collective-permute-start.22 = (bf16[512,512]{1,0:T(8,128)(2,1)S(1)}, bf16[512,512]{1,0:T(8,128)(2,1)S(1)}, u32[]{:S(2)}, u32[]{:S(2)}) collective-permute-start(bf16[512,512]{1,0:T(8,128)(2,1)S(1)} %collective-permute-done.17), channel_id=1, source_target_pairs={{0,12},{1,13},{2,14},{3,15},{4,8},{5,9},{6,10},{7,11},{8,4},{9,5},... | collective-permute-start | bytes 1572872 | tf_op jit(solution)/shard_map/C3/ppermute | solution.py:116
  71.3 0.4 convolution_add_fusion.4
  71.8 0.4 convolution_add_fusion.3
  72.3 0.4 convolution_add_fusion.2
  72.7 0.8 %collective-permute-done.21 = f32[128,512]{1,0:T(8,128)S(1)} collective-permute-done((f32[128,512]{1,0:T(8,128)S(1)}, f32[128,512]{1,0:T(8,128)S(1)}, u32[]{:S(2)}, u32[]{:S(2)}) %collective-permute-start.21) | collective-permute-done | bytes 262176 | tf_op jit(solution)/shard_map/K5/ppermute | solution.py:116
  73.8 0.5 convolution_add_fusion.1
  74.2 4.4 %collective-permute-done.22 = bf16[512,512]{1,0:T(8,128)(2,1)S(1)} collective-permute-done((bf16[512,512]{1,0:T(8,128)(2,1)S(1)}, bf16[512,512]{1,0:T(8,128)(2,1)S(1)}, u32[]{:S(2)}, u32[]{:S(2)}) %collective-permute-start.22) | collective-permute-done | bytes 524320 | tf_op jit(solution)/shard_map/C3/ppermute | solution.py:116
  78.6 0.4 convolution_add_fusion
  79.1 0.9 %multiply_convert_fusion = bf16[512,512]{1,0:T(8,128)(2,1)} fusion(f32[512,512]{1,0:T(8,128)S(1)} %convolution_add_fusion), kind=kLoop, calls=%fused_computation.22 | loop fusion | flops 524288 | bytes 1572864 | tf_op jit(solution)/shard_map/convert_element_type | solution.py:216
  80.2 2.1 %fusion = (f32[1,512,512]{2,1,0:T(8,128)}, f32[512,512]{1,0:T(8,128)}, f32[512,512]{1,0:T(8,128)}) fusion(f32[1,512,512]{2,1,0:T(8,128)S(1)} %copy-done.1, f32[512,512]{1,0:T(8,128)S(1)} %copy-done.2, f32[512,512]{1,0:T(8,128)S(1)} %pad_maximum_fusion, f32[512,512]{1,0:T(8,128)S(1)} %copy-done.3), kind=kLoop, calls=%fused_computation.17 | loop fusion | flops 2359296 | bytes 7340032 | tf_op jit(solution)/shard_map/add | solution.py:220
  (44 shorter events, 1.9 us)
Async XLA Ops:
  0.6 25.6 %copy-start = (f32[8192]{0:T(1024)S(1)}, f32[8192]{0:T(1024)}, u32[]{:S(2)}) copy-start(f32[8192]{0:T(1024)} %param.6) | copy-start | bytes 98308
  1.9 13.7 %collective-permute-start.4 = (bf16[512,512]{1,0:T(8,128)(2,1)S(1)}, bf16[512,512]{1,0:T(8,128)(2,1)}, u32[]{:S(2)}, u32[]{:S(2)}) collective-permute-start(bf16[512,512]{1,0:T(8,128)(2,1)S(1)} %bitcast_convert_fusion), channel_id=1, source_target_pairs={{0,4},{1,5},{2,6},{3,7},{4,0},{5,1},{6,2},{7,3},{8,12},{9,13},{10,... | collective-permute-start | bytes 1572872 | tf_op jit(solution)/shard_map/A0/ppermute | solution.py:116
  3.6 15.3 %collective-permute-start.3 = (bf16[512,512]{1,0:T(8,128)(2,1)S(1)}, bf16[512,512]{1,0:T(8,128)(2,1)}, u32[]{:S(2)}, u32[]{:S(2)}) collective-permute-start(bf16[512,512]{1,0:T(8,128)(2,1)S(1)} %bitcast_convert_fusion), channel_id=1, source_target_pairs={{0,12},{1,13},{2,14},{3,15},{4,8},{5,9},{6,10},{7,11},{8,4},{9,5},... | collective-permute-start | bytes 1572872 | tf_op jit(solution)/shard_map/B0/ppermute | solution.py:116
  5.8 13.1 %collective-permute-start.2 = (bf16[512,512]{1,0:T(8,128)(2,1)S(1)}, bf16[512,512]{1,0:T(8,128)(2,1)S(1)}, u32[]{:S(2)}, u32[]{:S(2)}) collective-permute-start(bf16[512,512]{1,0:T(8,128)(2,1)S(1)} %bitcast_convert_fusion), channel_id=1, source_target_pairs={{0,131},{1,2},{2,1},{3,128},{4,135},{5,6},{6,5},{7,132},{8,139},{9... | collective-permute-start | bytes 1572872 | tf_op jit(solution)/shard_map/M1/ppermute | solution.py:116
  7.7 15.4 %collective-permute-start.1 = (bf16[512,512]{1,0:T(8,128)(2,1)S(1)}, bf16[512,512]{1,0:T(8,128)(2,1)}, u32[]{:S(2)}, u32[]{:S(2)}) collective-permute-start(bf16[512,512]{1,0:T(8,128)(2,1)S(1)} %bitcast_convert_fusion), channel_id=1, source_target_pairs={{0,1},{1,0},{2,3},{3,2},{4,5},{5,4},{6,7},{7,6},{8,9},{9,8},{10,11... | collective-permute-start | bytes 1572872 | tf_op jit(solution)/shard_map/Z1/ppermute | solution.py:116
  13.6 11.8 %collective-permute-start = (f32[256,512]{1,0:T(8,128)S(1)}, f32[256,512]{1,0:T(8,128)S(1)}, u32[]{:S(2)}, u32[]{:S(2)}) collective-permute-start(f32[256,512]{1,0:T(8,128)S(1)} %slice_select_fusion), channel_id=1, source_target_pairs={{0,16},{16,0},{32,48},{48,32},{64,80},{80,64},{96,112},{112,96},{1... | collective-permute-start | bytes 1572872 | tf_op jit(solution)/shard_map/K1/ppermute | solution.py:116
  15.6 18.1 %collective-permute-start.9 = (bf16[512,512]{1,0:T(8,128)(2,1)}, bf16[512,512]{1,0:T(8,128)(2,1)S(1)}, u32[]{:S(2)}, u32[]{:S(2)}) collective-permute-start(bf16[512,512]{1,0:T(8,128)(2,1)} %collective-permute-done.4), channel_id=1, source_target_pairs={{0,12},{1,13},{2,14},{3,15},{4,8},{5,9},{6,10},{7,11},{8,4},{9,5},... | collective-permute-start | bytes 1572872 | tf_op jit(solution)/shard_map/C0/ppermute | solution.py:116
  18.9 19.4 %collective-permute-start.10 = (bf16[512,512]{1,0:T(8,128)(2,1)S(1)}, bf16[512,512]{1,0:T(8,128)(2,1)S(1)}, u32[]{:S(2)}, u32[]{:S(2)}) collective-permute-start(bf16[512,512]{1,0:T(8,128)(2,1)S(1)} %collective-permute-done.2), channel_id=1, source_target_pairs={{0,1},{1,0},{2,3},{3,2},{4,5},{5,4},{6,7},{7,6},{8,9},{9,8},{10,11... | collective-permute-start | bytes 1572872 | tf_op jit(solution)/shard_map/E2/ppermute | solution.py:116
  23.1 13.1 %collective-permute-start.8 = (bf16[512,512]{1,0:T(8,128)(2,1)}, bf16[512,512]{1,0:T(8,128)(2,1)S(1)}, u32[]{:S(2)}, u32[]{:S(2)}) collective-permute-start(bf16[512,512]{1,0:T(8,128)(2,1)} %collective-permute-done.1), channel_id=1, source_target_pairs={{0,131},{1,2},{2,1},{3,128},{4,135},{5,6},{6,5},{7,132},{8,139},{9... | collective-permute-start | bytes 1572872 | tf_op jit(solution)/shard_map/M2/ppermute | solution.py:116
  24.2 15.9 %collective-permute-start.7 = (bf16[512,512]{1,0:T(8,128)(2,1)}, bf16[512,512]{1,0:T(8,128)(2,1)S(1)}, u32[]{:S(2)}, u32[]{:S(2)}) collective-permute-start(bf16[512,512]{1,0:T(8,128)(2,1)} %collective-permute-done.1), channel_id=1, source_target_pairs={{0,4},{1,5},{2,6},{3,7},{4,0},{5,1},{6,2},{7,3},{8,12},{9,13},{10,... | collective-permute-start | bytes 1572872 | tf_op jit(solution)/shard_map/A1/ppermute | solution.py:116
  25.6 7.6 %collective-permute-start.5 = (f32[128,512]{1,0:T(8,128)S(1)}, f32[128,512]{1,0:T(8,128)S(1)}, u32[]{:S(2)}, u32[]{:S(2)}) collective-permute-start(f32[128,512]{1,0:T(8,128)S(1)} %slice_select_fusion.1), channel_id=1, source_target_pairs={{0,32},{16,48},{32,0},{48,16},{64,96},{80,112},{96,64},{112,80},{1... | collective-permute-start | bytes 786440 | tf_op jit(solution)/shard_map/K2/ppermute | solution.py:116
  33.2 20.1 %collective-permute-start.11 = (bf16[512,512]{1,0:T(8,128)(2,1)}, bf16[512,512]{1,0:T(8,128)(2,1)S(1)}, u32[]{:S(2)}, u32[]{:S(2)}) collective-permute-start(bf16[512,512]{1,0:T(8,128)(2,1)} %collective-permute-done.1), channel_id=1, source_target_pairs={{0,12},{1,13},{2,14},{3,15},{4,8},{5,9},{6,10},{7,11},{8,4},{9,5},... | collective-permute-start | bytes 1572872 | tf_op jit(solution)/shard_map/B1/ppermute | solution.py:116
  33.7 7.6 %collective-permute-start.6 = (f32[64,512]{1,0:T(8,128)S(1)}, f32[64,512]{1,0:T(8,128)S(1)}, u32[]{:S(2)}, u32[]{:S(2)}) collective-permute-start(f32[64,512]{1,0:T(8,128)S(1)} %slice_select_fusion.2), channel_id=1, source_target_pairs={{0,64},{16,80},{32,96},{48,112},{64,0},{80,16},{96,32},{112,48},{1... | collective-permute-start | bytes 393224 | tf_op jit(solution)/shard_map/K3/ppermute | solution.py:116
  36.2 16.1 %collective-permute-start.12 = (bf16[512,512]{1,0:T(8,128)(2,1)S(1)}, bf16[512,512]{1,0:T(8,128)(2,1)S(1)}, u32[]{:S(2)}, u32[]{:S(2)}) collective-permute-start(bf16[512,512]{1,0:T(8,128)(2,1)S(1)} %collective-permute-done.8), channel_id=1, source_target_pairs={{0,1},{1,0},{2,3},{3,2},{4,5},{5,4},{6,7},{7,6},{8,9},{9,8},{10,11... | collective-permute-start | bytes 1572872 | tf_op jit(solution)/shard_map/E3/ppermute | solution.py:116
  38.3 13.1 %collective-permute-start.13 = (bf16[512,512]{1,0:T(8,128)(2,1)S(1)}, bf16[512,512]{1,0:T(8,128)(2,1)S(1)}, u32[]{:S(2)}, u32[]{:S(2)}) collective-permute-start(bf16[512,512]{1,0:T(8,128)(2,1)S(1)} %broadcast_select_fusion.1), channel_id=1, source_target_pairs={{0,4},{1,5},{2,6},{3,7},{4,0},{5,1},{6,2},{7,3},{8,12},{9,13},{10,... | collective-permute-start | bytes 1572872 | tf_op jit(solution)/shard_map/A2/ppermute | solution.py:116
  40.1 19.7 %collective-permute-start.14 = (bf16[512,512]{1,0:T(8,128)(2,1)S(1)}, bf16[512,512]{1,0:T(8,128)(2,1)S(1)}, u32[]{:S(2)}, u32[]{:S(2)}) collective-permute-start(bf16[512,512]{1,0:T(8,128)(2,1)S(1)} %broadcast_select_fusion.1), channel_id=1, source_target_pairs={{0,12},{1,13},{2,14},{3,15},{4,8},{5,9},{6,10},{7,11},{8,4},{9,5},... | collective-permute-start | bytes 1572872 | tf_op jit(solution)/shard_map/B2/ppermute | solution.py:116
  41.3 16.9 %collective-permute-start.15 = (f32[64,512]{1,0:T(8,128)S(1)}, f32[64,512]{1,0:T(8,128)S(1)}, u32[]{:S(2)}, u32[]{:S(2)}) collective-permute-start(f32[64,512]{1,0:T(8,128)S(1)} %select_add_fusion.2), channel_id=1, source_target_pairs={{0,128},{16,144},{32,160},{48,176},{64,192},{80,208},{96,224},{112... | collective-permute-start | bytes 393224 | tf_op jit(solution)/shard_map/HIGH/ppermute | solution.py:116
  51.5 15.0 %collective-permute-start.16 = (bf16[512,512]{1,0:T(8,128)(2,1)S(1)}, bf16[512,512]{1,0:T(8,128)(2,1)S(1)}, u32[]{:S(2)}, u32[]{:S(2)}) collective-permute-start(bf16[512,512]{1,0:T(8,128)(2,1)S(1)} %collective-permute-done.13), channel_id=1, source_target_pairs={{0,12},{1,13},{2,14},{3,15},{4,8},{5,9},{6,10},{7,11},{8,4},{9,5},... | collective-permute-start | bytes 1572872 | tf_op jit(solution)/shard_map/C2/ppermute | solution.py:116
  52.4 15.8 %collective-permute-start.17 = (bf16[512,512]{1,0:T(8,128)(2,1)S(1)}, bf16[512,512]{1,0:T(8,128)(2,1)S(1)}, u32[]{:S(2)}, u32[]{:S(2)}) collective-permute-start(bf16[512,512]{1,0:T(8,128)(2,1)S(1)} %broadcast_select_fusion), channel_id=1, source_target_pairs={{0,4},{1,5},{2,6},{3,7},{4,0},{5,1},{6,2},{7,3},{8,12},{9,13},{10,... | collective-permute-start | bytes 1572872 | tf_op jit(solution)/shard_map/A3/ppermute | solution.py:116
  53.3 19.0 %collective-permute-start.19 = (bf16[512,512]{1,0:T(8,128)(2,1)S(1)}, bf16[512,512]{1,0:T(8,128)(2,1)S(1)}, u32[]{:S(2)}, u32[]{:S(2)}) collective-permute-start(bf16[512,512]{1,0:T(8,128)(2,1)S(1)} %broadcast_select_fusion), channel_id=1, source_target_pairs={{0,12},{1,13},{2,14},{3,15},{4,8},{5,9},{6,10},{7,11},{8,4},{9,5},... | collective-permute-start | bytes 1572872 | tf_op jit(solution)/shard_map/B3/ppermute | solution.py:116
  58.3 15.5 %collective-permute-start.20 = (bf16[512,512]{1,0:T(8,128)(2,1)S(1)}, bf16[512,512]{1,0:T(8,128)(2,1)S(1)}, u32[]{:S(2)}, u32[]{:S(2)}) collective-permute-start(bf16[512,512]{1,0:T(8,128)(2,1)S(1)} %collective-permute-done.9), channel_id=1, source_target_pairs={{0,1},{1,0},{2,3},{3,2},{4,5},{5,4},{6,7},{7,6},{8,9},{9,8},{10,11... | collective-permute-start | bytes 1572872 | tf_op jit(solution)/shard_map/ZC/ppermute | solution.py:116
  59.8 7.2 %collective-permute-start.18 = (f32[64,512]{1,0:T(8,128)S(1)}, f32[64,512]{1,0:T(8,128)S(1)}, u32[]{:S(2)}, u32[]{:S(2)}) collective-permute-start(f32[64,512]{1,0:T(8,128)S(1)} %add.213), channel_id=1, source_target_pairs={{0,64},{16,80},{32,96},{48,112},{64,0},{80,16},{96,32},{112,48},{1... | collective-permute-start | bytes 393224 | tf_op jit(solution)/shard_map/K4/ppermute | solution.py:116
  67.1 6.5 %collective-permute-start.21 = (f32[128,512]{1,0:T(8,128)S(1)}, f32[128,512]{1,0:T(8,128)S(1)}, u32[]{:S(2)}, u32[]{:S(2)}) collective-permute-start(f32[128,512]{1,0:T(8,128)S(1)} %pad_maximum_fusion.2), channel_id=1, source_target_pairs={{0,32},{16,48},{32,0},{48,16},{64,96},{80,112},{96,64},{112,80},{1... | collective-permute-start | bytes 786440 | tf_op jit(solution)/shard_map/K5/ppermute | solution.py:116
  68.3 10.4 %collective-permute-start.22 = (bf16[512,512]{1,0:T(8,128)(2,1)S(1)}, bf16[512,512]{1,0:T(8,128)(2,1)S(1)}, u32[]{:S(2)}, u32[]{:S(2)}) collective-permute-start(bf16[512,512]{1,0:T(8,128)(2,1)S(1)} %collective-permute-done.17), channel_id=1, source_target_pairs={{0,12},{1,13},{2,14},{3,15},{4,8},{5,9},{6,10},{7,11},{8,4},{9,5},... | collective-permute-start | bytes 1572872 | tf_op jit(solution)/shard_map/C3/ppermute | solution.py:116
  72.2 8.0 %copy-start.1 = (f32[1,512,512]{2,1,0:T(8,128)S(1)}, f32[1,512,512]{2,1,0:T(8,128)}, u32[]{:S(2)}) copy-start(f32[1,512,512]{2,1,0:T(8,128)} %param.9) | copy-start | bytes 3145732
  72.2 8.0 %copy-start.2 = (f32[512,512]{1,0:T(8,128)S(1)}, f32[512,512]{1,0:T(8,128)}, u32[]{:S(2)}) copy-start(f32[512,512]{1,0:T(8,128)} %param.7) | copy-start | bytes 3145732
  72.2 8.0 %copy-start.3 = (f32[512,512]{1,0:T(8,128)S(1)}, f32[512,512]{1,0:T(8,128)}, u32[]{:S(2)}) copy-start(f32[512,512]{1,0:T(8,128)} %param.8) | copy-start | bytes 3145732
  73.7 6.4 %collective-permute-start.23 = (f32[256,512]{1,0:T(8,128)S(1)}, f32[256,512]{1,0:T(8,128)S(1)}, u32[]{:S(2)}, u32[]{:S(2)}) collective-permute-start(f32[256,512]{1,0:T(8,128)S(1)} %pad_maximum_fusion.1), channel_id=1, source_target_pairs={{0,16},{16,0},{32,48},{48,32},{64,80},{80,64},{96,112},{112,96},{1... | collective-permute-start | bytes 1572872 | tf_op jit(solution)/shard_map/K6/ppermute | solution.py:116

commit v3 on v2

--- a/solution.py
+++ b/solution.py
@@ -35,8 +35,9 @@
     for island in range(16):
         for zero in range(16):
             y, z = divmod(zero, 4)
-            there = island if z in (1, 2) else island ^ 8
-            pairs.append((island * 16 + zero, there * 16 + y * 4 + 3 - z))
+            inner = z in (1, 2)
+            target = (island, y * 4 + 3 - z) if inner else (island ^ 1, zero)
+            pairs.append((island * 16 + zero, target[0] * 16 + target[1]))
     return pairs
 
 
@@ -168,9 +169,6 @@
     k2 = send("K2", order(give), "island", swap(2))
     normed = order(normalise(tokens, order(norm_gain[None])))
     total = order(keep + order(k2))
-    b1 = send("B1", order(z1), BOTH, second)
-    keep, give = split(total, x // 2 == 1)
-    k3 = send("K3", order(give), "island", swap(4))
     c0 = order(c0)
     m2 = order(m2)
     s2 = order(jnp.where(inner, m2, order(e2)))
@@ -178,22 +176,23 @@
     b2 = send("B2", s2, BOTH, second)
     e3 = send("E3", m2, "zero", swap(1))
     a1 = order(a1)
+    keep, give = split(total, x // 2 == 1)
+    k3 = send("K3", order(give), "island", swap(4))
+    add_product("dot0", own, y, z)
+    add_product("dot0", a0, near_y, z)
     total = order(keep + order(k3))
     high = send("HIGH", order(total), "island", swap(8))
-    add_product("dot0", own, y, z)
-    add_product("dot0", a0, near_y, z)
+    rest = order(jnp.concatenate([b0, c0]))
     a2 = order(a2)
     c2 = send("C2", a2, BOTH, second)
     s3 = order(jnp.where(inner, m1, order(e3)))
     a3 = send("A3", s3, BOTH, first)
     b3 = send("B3", s3, BOTH, second)
-    b1 = order(b1)
-    c1 = send("ZC", order(c0), "zero", swap(1))
+    rest = send("ZBC", order(rest), "zero", swap(1))
     add_product("dot0", b0, far_y, z)
     add_product("dot0", c0, y ^ 2, z)
     add_product("dot1", z1, y, z ^ 1)
     add_product("dot1", a1, near_y, z ^ 1)
-    add_product("dot1", b1, far_y, z ^ 1)
     add_product("dot2", s2, y, z ^ 2)
     total = order(total + order(high))
     k4 = send("K4", total, "island", swap(4))
@@ -201,17 +200,18 @@
     add_product("dot2", a2, near_y, z ^ 2)
     add_product("dot2", b2, far_y, z ^ 2)
     add_product("dot3", s3, y, z ^ 3)
-    c2 = order(c2)
     total = order(join(total, order(k4), x // 2 == 1))
     k5 = send("K5", total, "island", swap(2))
     a3 = order(a3)
     c3 = send("C3", a3, BOTH, second)
-    add_product("dot2", c2, y ^ 2, z ^ 2)
     add_product("dot3", a3, near_y, z ^ 3)
+    add_product("dot2", order(c2), y ^ 2, z ^ 2)
     add_product("dot3", order(b3), far_y, z ^ 3)
     total = order(join(total, order(k5), x % 2 == 1))
     k6 = send("K6", total, "island", swap(1))
-    add_product("dot1", order(c1), y ^ 2, z ^ 1)
+    rest = order(rest)
+    add_product("dot1", rest[:ROWS], far_y, z ^ 1)
+    add_product("dot1", rest[ROWS:], y ^ 2, z ^ 1)
     add_product("dot3", order(c3), y ^ 2, z ^ 3)
     keys = order((summed[0] * (1.0 / math.sqrt(D))).astype(jnp.bfloat16))
     total = order(join(total, order(k6), core == 1))

time: 83.9 us -> 82.6 us (0.985)
  starting transfers between devices: 42.9 us -> 30.7 us
  waiting for transfers between devices: 14.6 us -> 26.7 us
  matrix products: 10.2 us -> 9.11 us
  other arithmetic: 6.81 us -> 7.69 us
    ppermute x24 -> x23, starting transfers between devices: 42.9 us -> 30.7 us  [send(): return lax.ppermute(value, axis, pairs)]
    ppermute x24 -> x23, waiting for transfers between devices: 14.6 us -> 26.7 us  [send(): return lax.ppermute(value, axis, pairs)]
    dot_general x16, matrix products: 10.2 us -> 9.11 us  [add_product(): jnp.dot(part, block, preferred_element_type=jnp.float32)]
  transfers between devices with their start and end apart: 24 -> 23, of which waited for: 7 -> 9; matrix products, arithmetic and copies ran while one was open for 16% -> 16% of each run, Pallas kernels for 8% -> 8%
where the time goes in v3:
time: 82.6 us; the launch traced here: 81.8 us
  starting transfers between devices  30.7 us (37%)
  waiting for transfers between devices  26.7 us (32%)
  matrix products  9.11 us (11%)
  other arithmetic  7.69 us (9%)
  Pallas kernels  6.49 us (8%)
  between operations  0.97 us (1%)
    ppermute x23, starting transfers between devices, send(): return lax.ppermute(value, axis, pairs)  30.7 us
    ppermute x23, waiting for transfers between devices, send(): return lax.ppermute(value, axis, pairs)  26.7 us
    dot_general x16, matrix products, add_product(): jnp.dot(part, block, preferred_element_type=jnp.float32)  9.11 us
    pallas_call x1, Pallas kernels, normalise(): pl.pallas_call(norm_kernel, out_shape=jax.ShapeDtypeStruct(tokens.shape,...  6.49 us
    add x1, other arithmetic, body(): mixed = mix_share * local_weights + (1.0 - mix_share) * params_out[None]  2.06 us
    sub x1, other arithmetic, body(): keep, give = split(order(outer_params - own_copy), core == 1)  1.75 us
  transfers between devices with their start and end apart: 23, of which 9 were waited for; matrix products, arithmetic and copies ran while one was open for 16% of the time, Pallas kernels for 8%

profile of v3, /device:TPU:34, one launch (start us, length us, event | category | flops | bytes accessed | tf_op | source)
XLA Modules:
  0.0 81.8 jit_solution(5092937711026038736)
XLA Ops:
  0.6 1.3 %bitcast_convert_fusion = bf16[512,512]{1,0:T(8,128)(2,1)S(1)} fusion(f32[1,512,512]{2,1,0:T(8,128)} %param.9), kind=kLoop, calls=%fused_computation.19 | loop fusion | flops 262144 | bytes 1572864 | tf_op jit(solution)/shard_map/convert_element_type | solution.py:152
  1.9 1.7 %collective-permute-start.4 = (bf16[512,512]{1,0:T(8,128)(2,1)S(1)}, bf16[512,512]{1,0:T(8,128)(2,1)}, u32[]{:S(2)}, u32[]{:S(2)}) collective-permute-start(bf16[512,512]{1,0:T(8,128)(2,1)S(1)} %bitcast_convert_fusion), channel_id=1, source_target_pairs={{0,4},{1,5},{2,6},{3,7},{4,0},{5,1},{6,2},{7,3},{8,12},{9,13},{10,... | collective-permute-start | bytes 1572872 | tf_op jit(solution)/shard_map/A0/ppermute | solution.py:117
  3.6 2.2 %collective-permute-start.3 = (bf16[512,512]{1,0:T(8,128)(2,1)S(1)}, bf16[512,512]{1,0:T(8,128)(2,1)S(1)}, u32[]{:S(2)}, u32[]{:S(2)}) collective-permute-start(bf16[512,512]{1,0:T(8,128)(2,1)S(1)} %bitcast_convert_fusion), channel_id=1, source_target_pairs={{0,12},{1,13},{2,14},{3,15},{4,8},{5,9},{6,10},{7,11},{8,4},{9,5},... | collective-permute-start | bytes 1572872 | tf_op jit(solution)/shard_map/B0/ppermute | solution.py:117
  5.8 1.9 %collective-permute-start.2 = (bf16[512,512]{1,0:T(8,128)(2,1)S(1)}, bf16[512,512]{1,0:T(8,128)(2,1)S(1)}, u32[]{:S(2)}, u32[]{:S(2)}) collective-permute-start(bf16[512,512]{1,0:T(8,128)(2,1)S(1)} %bitcast_convert_fusion), channel_id=1, source_target_pairs={{0,16},{1,2},{2,1},{3,19},{4,20},{5,6},{6,5},{7,23},{8,24},{9,10},... | collective-permute-start | bytes 1572872 | tf_op jit(solution)/shard_map/M1/ppermute | solution.py:117
  7.7 1.7 %bitcast_subtract_fusion = f32[512,512]{1,0:T(8,128)S(1)} fusion(f32[512,512]{1,0:T(8,128)} %param.7, f32[1,512,512]{2,1,0:T(8,128)} %param.9), kind=kLoop, calls=%fused_computation.20 | loop fusion | flops 262144 | bytes 3145728 | tf_op jit(solution)/shard_map/sub | solution.py:157
  9.5 0.9 %slice_select_fusion = f32[256,512]{1,0:T(8,128)} fusion(f32[512,512]{1,0:T(8,128)S(1)} %bitcast_subtract_fusion, pred[]{:T(512)S(6)} %eq.29), kind=kLoop, calls=%fused_computation.47 | loop fusion | flops 131072 | bytes 1572865 | tf_op jit(solution)/shard_map/jit(_where)/select_n | solution.py:123
  10.3 5.3 %collective-permute-done.4 = bf16[512,512]{1,0:T(8,128)(2,1)} collective-permute-done((bf16[512,512]{1,0:T(8,128)(2,1)S(1)}, bf16[512,512]{1,0:T(8,128)(2,1)}, u32[]{:S(2)}, u32[]{:S(2)}) %collective-permute-start.4) | collective-permute-done | bytes 524320 | tf_op jit(solution)/shard_map/A0/ppermute | solution.py:117
  15.6 3.3 %collective-permute-start.8 = (bf16[512,512]{1,0:T(8,128)(2,1)}, bf16[512,512]{1,0:T(8,128)(2,1)S(1)}, u32[]{:S(2)}, u32[]{:S(2)}) collective-permute-start(bf16[512,512]{1,0:T(8,128)(2,1)} %collective-permute-done.4), channel_id=1, source_target_pairs={{0,12},{1,13},{2,14},{3,15},{4,8},{5,9},{6,10},{7,11},{8,4},{9,5},... | collective-permute-start | bytes 1572872 | tf_op jit(solution)/shard_map/C0/ppermute | solution.py:117
  19.0 1.5 %collective-permute-done.1 = bf16[512,512]{1,0:T(8,128)(2,1)} collective-permute-done((bf16[512,512]{1,0:T(8,128)(2,1)S(1)}, bf16[512,512]{1,0:T(8,128)(2,1)}, u32[]{:S(2)}, u32[]{:S(2)}) %collective-permute-start.1) | collective-permute-done | bytes 524320 | tf_op jit(solution)/shard_map/Z1/ppermute | solution.py:117
  20.5 2.2 %collective-permute-start.7 = (bf16[512,512]{1,0:T(8,128)(2,1)}, bf16[512,512]{1,0:T(8,128)(2,1)S(1)}, u32[]{:S(2)}, u32[]{:S(2)}) collective-permute-start(bf16[512,512]{1,0:T(8,128)(2,1)} %collective-permute-done.1), channel_id=1, source_target_pairs={{0,16},{1,2},{2,1},{3,19},{4,20},{5,6},{6,5},{7,23},{8,24},{9,10},... | collective-permute-start | bytes 1572872 | tf_op jit(solution)/shard_map/M2/ppermute | solution.py:117
  23.2 0.6 collective-permute-start.5
  23.8 6.5 %normalise.1 = bf16[512,8192]{1,0:T(8,128)(2,1)S(1)} custom-call(bf16[512,8192]{1,0:T(8,128)(2,1)} %tokens_ref.1, f32[1,8192]{1,0:T(1,128)S(1)} %bitcast.22), custom_call_target="tpu_custom_call" | custom-call | flops 25165824 | bytes 16777216 | tf_op jit(solution)/shard_map/normalise/pallas_call | solution.py:94
  30.3 0.4 fusion.18
  30.8 0.4 collective-permute-done.5
  31.2 3.2 %collective-permute-done.7 = bf16[512,512]{1,0:T(8,128)(2,1)S(1)} collective-permute-done((bf16[512,512]{1,0:T(8,128)(2,1)}, bf16[512,512]{1,0:T(8,128)(2,1)S(1)}, u32[]{:S(2)}, u32[]{:S(2)}) %collective-permute-start.7) | collective-permute-done | bytes 524320 | tf_op jit(solution)/shard_map/M2/ppermute | solution.py:117
  34.5 0.8 collective-permute-start.12
  35.3 0.6 collective-permute-start.13
  35.9 2.1 %collective-permute-start.10 = (f32[64,512]{1,0:T(8,128)S(1)}, f32[64,512]{1,0:T(8,128)S(1)}, u32[]{:S(2)}, u32[]{:S(2)}) collective-permute-start(f32[64,512]{1,0:T(8,128)S(1)} %slice_select_fusion.2), channel_id=1, source_target_pairs={{0,64},{16,80},{32,96},{48,112},{64,0},{80,16},{96,32},{112,48},{1... | collective-permute-start | bytes 393224 | tf_op jit(solution)/shard_map/K3/ppermute | solution.py:117
  38.0 1.5 %convolution_add_fusion.14 = f32[512,512]{1,0:T(8,128)S(1)} fusion(f32[512,512]{1,0:T(8,128)S(1)} %fusion.18, bf16[512,512]{1,0:T(8,128)(2,1)} %collective-permute-done.4, bf16[512,8192]{1,0:T(8,128)(2,1)S(1)} %normalise.1, s32[]{:T(128)S(6)} %select_n.177), kind=kOutput, calls=%fused_computation.14 | convolution fusion | flops 268697600 | bytes 3145732 | tf_op jit(solution)/shard_map/dot0/dot_general | solution.py:146
  39.5 0.4 convolution_add_fusion.13
  40.0 2.3 %collective-permute-done.10 = f32[64,512]{1,0:T(8,128)S(1)} collective-permute-done((f32[64,512]{1,0:T(8,128)S(1)}, f32[64,512]{1,0:T(8,128)S(1)}, u32[]{:S(2)}, u32[]{:S(2)}) %collective-permute-start.10) | collective-permute-done | bytes 131104 | tf_op jit(solution)/shard_map/K3/ppermute | solution.py:117
  42.4 5.6 %collective-permute-start.14 = (f32[64,512]{1,0:T(8,128)S(1)}, f32[64,512]{1,0:T(8,128)S(1)}, u32[]{:S(2)}, u32[]{:S(2)}) collective-permute-start(f32[64,512]{1,0:T(8,128)S(1)} %select_add_fusion.2), channel_id=1, source_target_pairs={{0,128},{16,144},{32,160},{48,176},{64,192},{80,208},{96,224},{112... | collective-permute-start | bytes 393224 | tf_op jit(solution)/shard_map/HIGH/ppermute | solution.py:117
  48.0 0.9 %collective-permute-done.11 = bf16[512,512]{1,0:T(8,128)(2,1)S(1)} collective-permute-done((bf16[512,512]{1,0:T(8,128)(2,1)S(1)}, bf16[512,512]{1,0:T(8,128)(2,1)S(1)}, u32[]{:S(2)}, u32[]{:S(2)}) %collective-permute-start.11) | collective-permute-done | bytes 524320 | tf_op jit(solution)/shard_map/E3/ppermute | solution.py:117
  49.0 0.5 collective-permute-start.15
  49.5 1.1 %collective-permute-start.17 = (bf16[512,512]{1,0:T(8,128)(2,1)S(1)}, bf16[512,512]{1,0:T(8,128)(2,1)S(1)}, u32[]{:S(2)}, u32[]{:S(2)}) collective-permute-start(bf16[512,512]{1,0:T(8,128)(2,1)S(1)} %collective-permute-done.12), channel_id=1, source_target_pairs={{0,12},{1,13},{2,14},{3,15},{4,8},{5,9},{6,10},{7,11},{8,4},{9,5},... | collective-permute-start | bytes 1572872 | tf_op jit(solution)/shard_map/C2/ppermute | solution.py:117
  50.6 2.1 %collective-permute-start.18 = (bf16[512,512]{1,0:T(8,128)(2,1)S(1)}, bf16[512,512]{1,0:T(8,128)(2,1)S(1)}, u32[]{:S(2)}, u32[]{:S(2)}) collective-permute-start(bf16[512,512]{1,0:T(8,128)(2,1)S(1)} %broadcast_select_fusion), channel_id=1, source_target_pairs={{0,12},{1,13},{2,14},{3,15},{4,8},{5,9},{6,10},{7,11},{8,4},{9,5},... | collective-permute-start | bytes 1572872 | tf_op jit(solution)/shard_map/B3/ppermute | solution.py:117
  52.7 0.4 convolution_add_fusion.12
  53.1 1.5 %convolution_add_fusion.11 = f32[512,512]{1,0:T(8,128)S(1)} fusion(f32[512,512]{1,0:T(8,128)S(1)} %convolution_add_fusion.12, bf16[512,512]{1,0:T(8,128)(2,1)} %collective-permute-done.1, bf16[512,8192]{1,0:T(8,128)(2,1)S(1)} %normalise.1, s32[]{:T(128)S(6)} %select_n.183), kind=kOutput, calls=%fused_computation.11 | convolution fusion | flops 268697600 | bytes 3145732 | tf_op jit(solution)/shard_map/dot1/dot_general | solution.py:146
  54.6 0.4 convolution_add_fusion.10
  55.1 0.4 convolution_add_fusion.9
  55.5 2.1 %collective-permute-start.19 = (bf16[1024,512]{1,0:T(8,128)(2,1)S(1)}, bf16[1024,512]{1,0:T(8,128)(2,1)S(1)}, u32[]{:S(2)}, u32[]{:S(2)}) collective-permute-start(bf16[1024,512]{1,0:T(8,128)(2,1)S(1)} %pad_maximum_fusion), channel_id=1, source_target_pairs={{0,1},{1,0},{2,3},{3,2},{4,5},{5,4},{6,7},{7,6},{8,9},{9,8},{10,11... | collective-permute-start | bytes 3145736 | tf_op jit(solution)/shard_map/ZBC/ppermute | solution.py:117
  57.7 2.2 %collective-permute-start.16 = (f32[64,512]{1,0:T(8,128)S(1)}, f32[64,512]{1,0:T(8,128)S(1)}, u32[]{:S(2)}, u32[]{:S(2)}) collective-permute-start(f32[64,512]{1,0:T(8,128)S(1)} %add.210), channel_id=1, source_target_pairs={{0,64},{16,80},{32,96},{48,112},{64,0},{80,16},{96,32},{112,48},{1... | collective-permute-start | bytes 393224 | tf_op jit(solution)/shard_map/K4/ppermute | solution.py:117
  59.9 0.4 convolution_add_fusion.8
  60.3 0.4 convolution_add_fusion.7
  60.8 0.4 convolution_add_fusion.6
  61.2 4.4 %collective-permute-done.16 = f32[64,512]{1,0:T(8,128)S(1)} collective-permute-done((f32[64,512]{1,0:T(8,128)S(1)}, f32[64,512]{1,0:T(8,128)S(1)}, u32[]{:S(2)}, u32[]{:S(2)}) %collective-permute-start.16) | collective-permute-done | bytes 131104 | tf_op jit(solution)/shard_map/K4/ppermute | solution.py:117
  65.7 0.5 collective-permute-start.20
  66.2 0.7 collective-permute-start.21
  66.9 0.4 convolution_add_fusion.5
  67.3 0.4 convolution_add_fusion.4
  67.8 0.4 convolution_add_fusion.3
  68.2 3.9 %collective-permute-done.20 = f32[128,512]{1,0:T(8,128)S(1)} collective-permute-done((f32[128,512]{1,0:T(8,128)S(1)}, f32[128,512]{1,0:T(8,128)S(1)}, u32[]{:S(2)}, u32[]{:S(2)}) %collective-permute-start.20) | collective-permute-done | bytes 262176 | tf_op jit(solution)/shard_map/K5/ppermute | solution.py:117
  72.3 4.9 %collective-permute-done.19 = bf16[1024,512]{1,0:T(8,128)(2,1)S(1)} collective-permute-done((bf16[1024,512]{1,0:T(8,128)(2,1)S(1)}, bf16[1024,512]{1,0:T(8,128)(2,1)S(1)}, u32[]{:S(2)}, u32[]{:S(2)}) %collective-permute-start.19) | collective-permute-done | bytes 1048608 | tf_op jit(solution)/shard_map/ZBC/ppermute | solution.py:117
  77.2 0.4 convolution_add_fusion.2
  77.6 0.4 convolution_add_fusion.1
  78.1 0.4 convolution_add_fusion
  78.5 0.9 %multiply_convert_fusion = bf16[512,512]{1,0:T(8,128)(2,1)} fusion(f32[512,512]{1,0:T(8,128)S(1)} %convolution_add_fusion), kind=kLoop, calls=%fused_computation.23 | loop fusion | flops 524288 | bytes 1572864 | tf_op jit(solution)/shard_map/convert_element_type | solution.py:216
  79.7 2.1 %fusion = (f32[1,512,512]{2,1,0:T(8,128)}, f32[512,512]{1,0:T(8,128)}, f32[512,512]{1,0:T(8,128)}) fusion(f32[1,512,512]{2,1,0:T(8,128)S(1)} %copy-done.1, f32[512,512]{1,0:T(8,128)S(1)} %copy-done.2, f32[512,512]{1,0:T(8,128)S(1)} %pad_maximum_fusion.1, f32[512,512]{1,0:T(8,128)S(1)} %copy-done.3), kind=kLoop, calls=%fused_computation.18 | loop fusion | flops 2359296 | bytes 7340032 | tf_op jit(solution)/shard_map/add | solution.py:220
  (43 shorter events, 1.3 us)
Async XLA Ops:
  0.6 23.2 %copy-start = (f32[8192]{0:T(1024)S(1)}, f32[8192]{0:T(1024)}, u32[]{:S(2)}) copy-start(f32[8192]{0:T(1024)} %param.6) | copy-start | bytes 98308
  1.9 13.7 %collective-permute-start.4 = (bf16[512,512]{1,0:T(8,128)(2,1)S(1)}, bf16[512,512]{1,0:T(8,128)(2,1)}, u32[]{:S(2)}, u32[]{:S(2)}) collective-permute-start(bf16[512,512]{1,0:T(8,128)(2,1)S(1)} %bitcast_convert_fusion), channel_id=1, source_target_pairs={{0,4},{1,5},{2,6},{3,7},{4,0},{5,1},{6,2},{7,3},{8,12},{9,13},{10,... | collective-permute-start | bytes 1572872 | tf_op jit(solution)/shard_map/A0/ppermute | solution.py:117
  3.6 15.3 %collective-permute-start.3 = (bf16[512,512]{1,0:T(8,128)(2,1)S(1)}, bf16[512,512]{1,0:T(8,128)(2,1)S(1)}, u32[]{:S(2)}, u32[]{:S(2)}) collective-permute-start(bf16[512,512]{1,0:T(8,128)(2,1)S(1)} %bitcast_convert_fusion), channel_id=1, source_target_pairs={{0,12},{1,13},{2,14},{3,15},{4,8},{5,9},{6,10},{7,11},{8,4},{9,5},... | collective-permute-start | bytes 1572872 | tf_op jit(solution)/shard_map/B0/ppermute | solution.py:117
  5.8 13.1 %collective-permute-start.2 = (bf16[512,512]{1,0:T(8,128)(2,1)S(1)}, bf16[512,512]{1,0:T(8,128)(2,1)S(1)}, u32[]{:S(2)}, u32[]{:S(2)}) collective-permute-start(bf16[512,512]{1,0:T(8,128)(2,1)S(1)} %bitcast_convert_fusion), channel_id=1, source_target_pairs={{0,16},{1,2},{2,1},{3,19},{4,20},{5,6},{6,5},{7,23},{8,24},{9,10},... | collective-permute-start | bytes 1572872 | tf_op jit(solution)/shard_map/M1/ppermute | solution.py:117
  7.7 12.8 %collective-permute-start.1 = (bf16[512,512]{1,0:T(8,128)(2,1)S(1)}, bf16[512,512]{1,0:T(8,128)(2,1)}, u32[]{:S(2)}, u32[]{:S(2)}) collective-permute-start(bf16[512,512]{1,0:T(8,128)(2,1)S(1)} %bitcast_convert_fusion), channel_id=1, source_target_pairs={{0,1},{1,0},{2,3},{3,2},{4,5},{5,4},{6,7},{7,6},{8,9},{9,8},{10,11... | collective-permute-start | bytes 1572872 | tf_op jit(solution)/shard_map/Z1/ppermute | solution.py:117
  10.3 12.7 %collective-permute-start = (f32[256,512]{1,0:T(8,128)}, f32[256,512]{1,0:T(8,128)S(1)}, u32[]{:S(2)}, u32[]{:S(2)}) collective-permute-start(f32[256,512]{1,0:T(8,128)} %slice_select_fusion), channel_id=1, source_target_pairs={{0,16},{16,0},{32,48},{48,32},{64,80},{80,64},{96,112},{112,96},{1... | collective-permute-start | bytes 1572872 | tf_op jit(solution)/shard_map/K1/ppermute | solution.py:117
  15.6 15.6 %collective-permute-start.8 = (bf16[512,512]{1,0:T(8,128)(2,1)}, bf16[512,512]{1,0:T(8,128)(2,1)S(1)}, u32[]{:S(2)}, u32[]{:S(2)}) collective-permute-start(bf16[512,512]{1,0:T(8,128)(2,1)} %collective-permute-done.4), channel_id=1, source_target_pairs={{0,12},{1,13},{2,14},{3,15},{4,8},{5,9},{6,10},{7,11},{8,4},{9,5},... | collective-permute-start | bytes 1572872 | tf_op jit(solution)/shard_map/C0/ppermute | solution.py:117
  18.9 15.5 %collective-permute-start.9 = (bf16[512,512]{1,0:T(8,128)(2,1)S(1)}, bf16[512,512]{1,0:T(8,128)(2,1)S(1)}, u32[]{:S(2)}, u32[]{:S(2)}) collective-permute-start(bf16[512,512]{1,0:T(8,128)(2,1)S(1)} %collective-permute-done.2), channel_id=1, source_target_pairs={{0,1},{1,0},{2,3},{3,2},{4,5},{5,4},{6,7},{7,6},{8,9},{9,8},{10,11... | collective-permute-start | bytes 1572872 | tf_op jit(solution)/shard_map/E2/ppermute | solution.py:117
  20.5 13.9 %collective-permute-start.7 = (bf16[512,512]{1,0:T(8,128)(2,1)}, bf16[512,512]{1,0:T(8,128)(2,1)S(1)}, u32[]{:S(2)}, u32[]{:S(2)}) collective-permute-start(bf16[512,512]{1,0:T(8,128)(2,1)} %collective-permute-done.1), channel_id=1, source_target_pairs={{0,16},{1,2},{2,1},{3,19},{4,20},{5,6},{6,5},{7,23},{8,24},{9,10},... | collective-permute-start | bytes 1572872 | tf_op jit(solution)/shard_map/M2/ppermute | solution.py:117
  22.8 13.1 %collective-permute-start.6 = (bf16[512,512]{1,0:T(8,128)(2,1)}, bf16[512,512]{1,0:T(8,128)(2,1)S(1)}, u32[]{:S(2)}, u32[]{:S(2)}) collective-permute-start(bf16[512,512]{1,0:T(8,128)(2,1)} %collective-permute-done.1), channel_id=1, source_target_pairs={{0,4},{1,5},{2,6},{3,7},{4,0},{5,1},{6,2},{7,3},{8,12},{9,13},{10,... | collective-permute-start | bytes 1572872 | tf_op jit(solution)/shard_map/A1/ppermute | solution.py:117
  23.2 7.9 %collective-permute-start.5 = (f32[128,512]{1,0:T(8,128)S(1)}, f32[128,512]{1,0:T(8,128)S(1)}, u32[]{:S(2)}, u32[]{:S(2)}) collective-permute-start(f32[128,512]{1,0:T(8,128)S(1)} %slice_select_fusion.1), channel_id=1, source_target_pairs={{0,32},{16,48},{32,0},{48,16},{64,96},{80,112},{96,64},{112,80},{1... | collective-permute-start | bytes 786440 | tf_op jit(solution)/shard_map/K2/ppermute | solution.py:117
  34.4 14.5 %collective-permute-start.11 = (bf16[512,512]{1,0:T(8,128)(2,1)S(1)}, bf16[512,512]{1,0:T(8,128)(2,1)S(1)}, u32[]{:S(2)}, u32[]{:S(2)}) collective-permute-start(bf16[512,512]{1,0:T(8,128)(2,1)S(1)} %collective-permute-done.7), channel_id=1, source_target_pairs={{0,1},{1,0},{2,3},{3,2},{4,5},{5,4},{6,7},{7,6},{8,9},{9,8},{10,11... | collective-permute-start | bytes 1572872 | tf_op jit(solution)/shard_map/E3/ppermute | solution.py:117
  34.5 13.5 %collective-permute-start.12 = (bf16[512,512]{1,0:T(8,128)(2,1)S(1)}, bf16[512,512]{1,0:T(8,128)(2,1)S(1)}, u32[]{:S(2)}, u32[]{:S(2)}) collective-permute-start(bf16[512,512]{1,0:T(8,128)(2,1)S(1)} %broadcast_select_fusion.1), channel_id=1, source_target_pairs={{0,4},{1,5},{2,6},{3,7},{4,0},{5,1},{6,2},{7,3},{8,12},{9,13},{10,... | collective-permute-start | bytes 1572872 | tf_op jit(solution)/shard_map/A2/ppermute | solution.py:117
  35.3 22.4 %collective-permute-start.13 = (bf16[512,512]{1,0:T(8,128)(2,1)S(1)}, bf16[512,512]{1,0:T(8,128)(2,1)S(1)}, u32[]{:S(2)}, u32[]{:S(2)}) collective-permute-start(bf16[512,512]{1,0:T(8,128)(2,1)S(1)} %broadcast_select_fusion.1), channel_id=1, source_target_pairs={{0,12},{1,13},{2,14},{3,15},{4,8},{5,9},{6,10},{7,11},{8,4},{9,5},... | collective-permute-start | bytes 1572872 | tf_op jit(solution)/shard_map/B2/ppermute | solution.py:117
  35.9 6.5 %collective-permute-start.10 = (f32[64,512]{1,0:T(8,128)S(1)}, f32[64,512]{1,0:T(8,128)S(1)}, u32[]{:S(2)}, u32[]{:S(2)}) collective-permute-start(f32[64,512]{1,0:T(8,128)S(1)} %slice_select_fusion.2), channel_id=1, source_target_pairs={{0,64},{16,80},{32,96},{48,112},{64,0},{80,16},{96,32},{112,48},{1... | collective-permute-start | bytes 393224 | tf_op jit(solution)/shard_map/K3/ppermute | solution.py:117
  42.4 13.2 %collective-permute-start.14 = (f32[64,512]{1,0:T(8,128)S(1)}, f32[64,512]{1,0:T(8,128)S(1)}, u32[]{:S(2)}, u32[]{:S(2)}) collective-permute-start(f32[64,512]{1,0:T(8,128)S(1)} %select_add_fusion.2), channel_id=1, source_target_pairs={{0,128},{16,144},{32,160},{48,176},{64,192},{80,208},{96,224},{112... | collective-permute-start | bytes 393224 | tf_op jit(solution)/shard_map/HIGH/ppermute | solution.py:117
  49.0 17.2 %collective-permute-start.15 = (bf16[512,512]{1,0:T(8,128)(2,1)S(1)}, bf16[512,512]{1,0:T(8,128)(2,1)S(1)}, u32[]{:S(2)}, u32[]{:S(2)}) collective-permute-start(bf16[512,512]{1,0:T(8,128)(2,1)S(1)} %broadcast_select_fusion), channel_id=1, source_target_pairs={{0,4},{1,5},{2,6},{3,7},{4,0},{5,1},{6,2},{7,3},{8,12},{9,13},{10,... | collective-permute-start | bytes 1572872 | tf_op jit(solution)/shard_map/A3/ppermute | solution.py:117
  49.5 17.9 %collective-permute-start.17 = (bf16[512,512]{1,0:T(8,128)(2,1)S(1)}, bf16[512,512]{1,0:T(8,128)(2,1)S(1)}, u32[]{:S(2)}, u32[]{:S(2)}) collective-permute-start(bf16[512,512]{1,0:T(8,128)(2,1)S(1)} %collective-permute-done.12), channel_id=1, source_target_pairs={{0,12},{1,13},{2,14},{3,15},{4,8},{5,9},{6,10},{7,11},{8,4},{9,5},... | collective-permute-start | bytes 1572872 | tf_op jit(solution)/shard_map/C2/ppermute | solution.py:117
  50.6 17.2 %collective-permute-start.18 = (bf16[512,512]{1,0:T(8,128)(2,1)S(1)}, bf16[512,512]{1,0:T(8,128)(2,1)S(1)}, u32[]{:S(2)}, u32[]{:S(2)}) collective-permute-start(bf16[512,512]{1,0:T(8,128)(2,1)S(1)} %broadcast_select_fusion), channel_id=1, source_target_pairs={{0,12},{1,13},{2,14},{3,15},{4,8},{5,9},{6,10},{7,11},{8,4},{9,5},... | collective-permute-start | bytes 1572872 | tf_op jit(solution)/shard_map/B3/ppermute | solution.py:117
  55.5 21.7 %collective-permute-start.19 = (bf16[1024,512]{1,0:T(8,128)(2,1)S(1)}, bf16[1024,512]{1,0:T(8,128)(2,1)S(1)}, u32[]{:S(2)}, u32[]{:S(2)}) collective-permute-start(bf16[1024,512]{1,0:T(8,128)(2,1)S(1)} %pad_maximum_fusion), channel_id=1, source_target_pairs={{0,1},{1,0},{2,3},{3,2},{4,5},{5,4},{6,7},{7,6},{8,9},{9,8},{10,11... | collective-permute-start | bytes 3145736 | tf_op jit(solution)/shard_map/ZBC/ppermute | solution.py:117
  57.7 7.9 %collective-permute-start.16 = (f32[64,512]{1,0:T(8,128)S(1)}, f32[64,512]{1,0:T(8,128)S(1)}, u32[]{:S(2)}, u32[]{:S(2)}) collective-permute-start(f32[64,512]{1,0:T(8,128)S(1)} %add.210), channel_id=1, source_target_pairs={{0,64},{16,80},{32,96},{48,112},{64,0},{80,16},{96,32},{112,48},{1... | collective-permute-start | bytes 393224 | tf_op jit(solution)/shard_map/K4/ppermute | solution.py:117
  65.7 6.5 %collective-permute-start.20 = (f32[128,512]{1,0:T(8,128)S(1)}, f32[128,512]{1,0:T(8,128)S(1)}, u32[]{:S(2)}, u32[]{:S(2)}) collective-permute-start(f32[128,512]{1,0:T(8,128)S(1)} %pad_maximum_fusion.3), channel_id=1, source_target_pairs={{0,32},{16,48},{32,0},{48,16},{64,96},{80,112},{96,64},{112,80},{1... | collective-permute-start | bytes 786440 | tf_op jit(solution)/shard_map/K5/ppermute | solution.py:117
  66.2 11.9 %collective-permute-start.21 = (bf16[512,512]{1,0:T(8,128)(2,1)S(1)}, bf16[512,512]{1,0:T(8,128)(2,1)S(1)}, u32[]{:S(2)}, u32[]{:S(2)}) collective-permute-start(bf16[512,512]{1,0:T(8,128)(2,1)S(1)} %collective-permute-done.15), channel_id=1, source_target_pairs={{0,12},{1,13},{2,14},{3,15},{4,8},{5,9},{6,10},{7,11},{8,4},{9,5},... | collective-permute-start | bytes 1572872 | tf_op jit(solution)/shard_map/C3/ppermute | solution.py:117
  72.2 7.5 %copy-start.1 = (f32[1,512,512]{2,1,0:T(8,128)S(1)}, f32[1,512,512]{2,1,0:T(8,128)}, u32[]{:S(2)}) copy-start(f32[1,512,512]{2,1,0:T(8,128)} %param.9) | copy-start | bytes 3145732
  72.2 7.5 %copy-start.2 = (f32[512,512]{1,0:T(8,128)S(1)}, f32[512,512]{1,0:T(8,128)}, u32[]{:S(2)}) copy-start(f32[512,512]{1,0:T(8,128)} %param.7) | copy-start | bytes 3145732
  72.2 7.5 %copy-start.3 = (f32[512,512]{1,0:T(8,128)S(1)}, f32[512,512]{1,0:T(8,128)}, u32[]{:S(2)}) copy-start(f32[512,512]{1,0:T(8,128)} %param.8) | copy-start | bytes 3145732
  72.2 7.2 %collective-permute-start.22 = (f32[256,512]{1,0:T(8,128)S(1)}, f32[256,512]{1,0:T(8,128)S(1)}, u32[]{:S(2)}, u32[]{:S(2)}) collective-permute-start(f32[256,512]{1,0:T(8,128)S(1)} %pad_maximum_fusion.2), channel_id=1, source_target_pairs={{0,16},{16,0},{32,48},{48,32},{64,80},{80,64},{96,112},{112,96},{1... | collective-permute-start | bytes 1572872 | tf_op jit(solution)/shard_map/K6/ppermute | solution.py:117

commit v4 on v3

--- a/solution.py
+++ b/solution.py
@@ -206,12 +206,12 @@
     c3 = send("C3", a3, BOTH, second)
     add_product("dot3", a3, near_y, z ^ 3)
     add_product("dot2", order(c2), y ^ 2, z ^ 2)
-    add_product("dot3", order(b3), far_y, z ^ 3)
     total = order(join(total, order(k5), x % 2 == 1))
     k6 = send("K6", total, "island", swap(1))
     rest = order(rest)
     add_product("dot1", rest[:ROWS], far_y, z ^ 1)
     add_product("dot1", rest[ROWS:], y ^ 2, z ^ 1)
+    add_product("dot3", order(b3), far_y, z ^ 3)
     add_product("dot3", order(c3), y ^ 2, z ^ 3)
     keys = order((summed[0] * (1.0 / math.sqrt(D))).astype(jnp.bfloat16))
     total = order(join(total, order(k6), core == 1))

time: 82.6 us -> 82.1 us (level)
  transfers between devices with their start and end apart: 23 -> 23, of which waited for: 9 -> 11; matrix products, arithmetic and copies ran while one was open for 16% -> 16% of each run, Pallas kernels for 8% -> 8%
where the time goes in v4:
time: 82.1 us; the launch traced here: 81.9 us
  starting transfers between devices  30.8 us (38%)
  waiting for transfers between devices  26.8 us (33%)
  matrix products  9.12 us (11%)
  other arithmetic  7.67 us (9%)
  Pallas kernels  6.49 us (8%)
  between operations  0.95 us (1%)
    ppermute x23, starting transfers between devices, send(): return lax.ppermute(value, axis, pairs)  30.8 us
    ppermute x23, waiting for transfers between devices, send(): return lax.ppermute(value, axis, pairs)  26.8 us
    dot_general x16, matrix products, add_product(): jnp.dot(part, block, preferred_element_type=jnp.float32)  9.12 us
    pallas_call x1, Pallas kernels, normalise(): pl.pallas_call(norm_kernel, out_shape=jax.ShapeDtypeStruct(tokens.shape,...  6.49 us
    add x1, other arithmetic, body(): mixed = mix_share * local_weights + (1.0 - mix_share) * params_out[None]  2.06 us
    sub x1, other arithmetic, body(): keep, give = split(order(outer_params - own_copy), core == 1)  1.75 us
  transfers between devices with their start and end apart: 23, of which 11 were waited for; matrix products, arithmetic and copies ran while one was open for 16% of the time, Pallas kernels for 8%

profile of v4, /device:TPU:34, one launch (start us, length us, event | category | flops | bytes accessed | tf_op | source)
XLA Modules:
  0.0 81.9 jit_solution(2021186288820698124)
XLA Ops:
  0.6 1.3 %bitcast_convert_fusion = bf16[512,512]{1,0:T(8,128)(2,1)S(1)} fusion(f32[1,512,512]{2,1,0:T(8,128)} %param.9), kind=kLoop, calls=%fused_computation.19 | loop fusion | flops 262144 | bytes 1572864 | tf_op jit(solution)/shard_map/convert_element_type | solution.py:152
  1.9 1.7 %collective-permute-start.4 = (bf16[512,512]{1,0:T(8,128)(2,1)S(1)}, bf16[512,512]{1,0:T(8,128)(2,1)}, u32[]{:S(2)}, u32[]{:S(2)}) collective-permute-start(bf16[512,512]{1,0:T(8,128)(2,1)S(1)} %bitcast_convert_fusion), channel_id=1, source_target_pairs={{0,4},{1,5},{2,6},{3,7},{4,0},{5,1},{6,2},{7,3},{8,12},{9,13},{10,... | collective-permute-start | bytes 1572872 | tf_op jit(solution)/shard_map/A0/ppermute | solution.py:117
  3.6 2.2 %collective-permute-start.3 = (bf16[512,512]{1,0:T(8,128)(2,1)S(1)}, bf16[512,512]{1,0:T(8,128)(2,1)S(1)}, u32[]{:S(2)}, u32[]{:S(2)}) collective-permute-start(bf16[512,512]{1,0:T(8,128)(2,1)S(1)} %bitcast_convert_fusion), channel_id=1, source_target_pairs={{0,12},{1,13},{2,14},{3,15},{4,8},{5,9},{6,10},{7,11},{8,4},{9,5},... | collective-permute-start | bytes 1572872 | tf_op jit(solution)/shard_map/B0/ppermute | solution.py:117
  5.8 1.9 %collective-permute-start.2 = (bf16[512,512]{1,0:T(8,128)(2,1)S(1)}, bf16[512,512]{1,0:T(8,128)(2,1)S(1)}, u32[]{:S(2)}, u32[]{:S(2)}) collective-permute-start(bf16[512,512]{1,0:T(8,128)(2,1)S(1)} %bitcast_convert_fusion), channel_id=1, source_target_pairs={{0,16},{1,2},{2,1},{3,19},{4,20},{5,6},{6,5},{7,23},{8,24},{9,10},... | collective-permute-start | bytes 1572872 | tf_op jit(solution)/shard_map/M1/ppermute | solution.py:117
  7.7 1.7 %bitcast_subtract_fusion = f32[512,512]{1,0:T(8,128)S(1)} fusion(f32[512,512]{1,0:T(8,128)} %param.7, f32[1,512,512]{2,1,0:T(8,128)} %param.9), kind=kLoop, calls=%fused_computation.20 | loop fusion | flops 262144 | bytes 3145728 | tf_op jit(solution)/shard_map/sub | solution.py:157
  9.5 0.9 %slice_select_fusion = f32[256,512]{1,0:T(8,128)} fusion(f32[512,512]{1,0:T(8,128)S(1)} %bitcast_subtract_fusion, pred[]{:T(512)S(6)} %eq.29), kind=kLoop, calls=%fused_computation.47 | loop fusion | flops 131072 | bytes 1572865 | tf_op jit(solution)/shard_map/jit(_where)/select_n | solution.py:123
  10.3 5.3 %collective-permute-done.4 = bf16[512,512]{1,0:T(8,128)(2,1)} collective-permute-done((bf16[512,512]{1,0:T(8,128)(2,1)S(1)}, bf16[512,512]{1,0:T(8,128)(2,1)}, u32[]{:S(2)}, u32[]{:S(2)}) %collective-permute-start.4) | collective-permute-done | bytes 524320 | tf_op jit(solution)/shard_map/A0/ppermute | solution.py:117
  15.6 3.3 %collective-permute-start.8 = (bf16[512,512]{1,0:T(8,128)(2,1)}, bf16[512,512]{1,0:T(8,128)(2,1)S(1)}, u32[]{:S(2)}, u32[]{:S(2)}) collective-permute-start(bf16[512,512]{1,0:T(8,128)(2,1)} %collective-permute-done.4), channel_id=1, source_target_pairs={{0,12},{1,13},{2,14},{3,15},{4,8},{5,9},{6,10},{7,11},{8,4},{9,5},... | collective-permute-start | bytes 1572872 | tf_op jit(solution)/shard_map/C0/ppermute | solution.py:117
  19.0 1.5 %collective-permute-done.1 = bf16[512,512]{1,0:T(8,128)(2,1)} collective-permute-done((bf16[512,512]{1,0:T(8,128)(2,1)S(1)}, bf16[512,512]{1,0:T(8,128)(2,1)}, u32[]{:S(2)}, u32[]{:S(2)}) %collective-permute-start.1) | collective-permute-done | bytes 524320 | tf_op jit(solution)/shard_map/Z1/ppermute | solution.py:117
  20.5 2.2 %collective-permute-start.7 = (bf16[512,512]{1,0:T(8,128)(2,1)}, bf16[512,512]{1,0:T(8,128)(2,1)S(1)}, u32[]{:S(2)}, u32[]{:S(2)}) collective-permute-start(bf16[512,512]{1,0:T(8,128)(2,1)} %collective-permute-done.1), channel_id=1, source_target_pairs={{0,16},{1,2},{2,1},{3,19},{4,20},{5,6},{6,5},{7,23},{8,24},{9,10},... | collective-permute-start | bytes 1572872 | tf_op jit(solution)/shard_map/M2/ppermute | solution.py:117
  23.2 0.6 collective-permute-start.5
  23.8 6.5 %normalise.1 = bf16[512,8192]{1,0:T(8,128)(2,1)S(1)} custom-call(bf16[512,8192]{1,0:T(8,128)(2,1)} %tokens_ref.1, f32[1,8192]{1,0:T(1,128)S(1)} %bitcast.22), custom_call_target="tpu_custom_call" | custom-call | flops 25165824 | bytes 16777216 | tf_op jit(solution)/shard_map/normalise/pallas_call | solution.py:94
  30.3 0.4 fusion.18
  31.2 3.2 %collective-permute-done.7 = bf16[512,512]{1,0:T(8,128)(2,1)S(1)} collective-permute-done((bf16[512,512]{1,0:T(8,128)(2,1)}, bf16[512,512]{1,0:T(8,128)(2,1)S(1)}, u32[]{:S(2)}, u32[]{:S(2)}) %collective-permute-start.7) | collective-permute-done | bytes 524320 | tf_op jit(solution)/shard_map/M2/ppermute | solution.py:117
  34.5 0.8 collective-permute-start.12
  35.3 0.6 collective-permute-start.13
  35.9 2.1 %collective-permute-start.10 = (f32[64,512]{1,0:T(8,128)S(1)}, f32[64,512]{1,0:T(8,128)S(1)}, u32[]{:S(2)}, u32[]{:S(2)}) collective-permute-start(f32[64,512]{1,0:T(8,128)S(1)} %slice_select_fusion.2), channel_id=1, source_target_pairs={{0,64},{16,80},{32,96},{48,112},{64,0},{80,16},{96,32},{112,48},{1... | collective-permute-start | bytes 393224 | tf_op jit(solution)/shard_map/K3/ppermute | solution.py:117
  38.0 1.5 %convolution_add_fusion.14 = f32[512,512]{1,0:T(8,128)S(1)} fusion(f32[512,512]{1,0:T(8,128)S(1)} %fusion.18, bf16[512,512]{1,0:T(8,128)(2,1)} %collective-permute-done.4, bf16[512,8192]{1,0:T(8,128)(2,1)S(1)} %normalise.1, s32[]{:T(128)S(6)} %select_n.177), kind=kOutput, calls=%fused_computation.14 | convolution fusion | flops 268697600 | bytes 3145732 | tf_op jit(solution)/shard_map/dot0/dot_general | solution.py:146
  39.5 0.4 convolution_add_fusion.13
  40.0 2.3 %collective-permute-done.10 = f32[64,512]{1,0:T(8,128)S(1)} collective-permute-done((f32[64,512]{1,0:T(8,128)S(1)}, f32[64,512]{1,0:T(8,128)S(1)}, u32[]{:S(2)}, u32[]{:S(2)}) %collective-permute-start.10) | collective-permute-done | bytes 131104 | tf_op jit(solution)/shard_map/K3/ppermute | solution.py:117
  42.4 5.6 %collective-permute-start.14 = (f32[64,512]{1,0:T(8,128)S(1)}, f32[64,512]{1,0:T(8,128)S(1)}, u32[]{:S(2)}, u32[]{:S(2)}) collective-permute-start(f32[64,512]{1,0:T(8,128)S(1)} %select_add_fusion.2), channel_id=1, source_target_pairs={{0,128},{16,144},{32,160},{48,176},{64,192},{80,208},{96,224},{112... | collective-permute-start | bytes 393224 | tf_op jit(solution)/shard_map/HIGH/ppermute | solution.py:117
  48.0 0.9 %collective-permute-done.11 = bf16[512,512]{1,0:T(8,128)(2,1)S(1)} collective-permute-done((bf16[512,512]{1,0:T(8,128)(2,1)S(1)}, bf16[512,512]{1,0:T(8,128)(2,1)S(1)}, u32[]{:S(2)}, u32[]{:S(2)}) %collective-permute-start.11) | collective-permute-done | bytes 524320 | tf_op jit(solution)/shard_map/E3/ppermute | solution.py:117
  49.0 0.5 collective-permute-start.15
  49.5 1.1 %collective-permute-start.17 = (bf16[512,512]{1,0:T(8,128)(2,1)S(1)}, bf16[512,512]{1,0:T(8,128)(2,1)S(1)}, u32[]{:S(2)}, u32[]{:S(2)}) collective-permute-start(bf16[512,512]{1,0:T(8,128)(2,1)S(1)} %collective-permute-done.12), channel_id=1, source_target_pairs={{0,12},{1,13},{2,14},{3,15},{4,8},{5,9},{6,10},{7,11},{8,4},{9,5},... | collective-permute-start | bytes 1572872 | tf_op jit(solution)/shard_map/C2/ppermute | solution.py:117
  50.6 1.9 %collective-permute-start.18 = (bf16[1024,512]{1,0:T(8,128)(2,1)S(1)}, bf16[1024,512]{1,0:T(8,128)(2,1)S(1)}, u32[]{:S(2)}, u32[]{:S(2)}) collective-permute-start(bf16[1024,512]{1,0:T(8,128)(2,1)S(1)} %pad_maximum_fusion), channel_id=1, source_target_pairs={{0,1},{1,0},{2,3},{3,2},{4,5},{5,4},{6,7},{7,6},{8,9},{9,8},{10,11... | collective-permute-start | bytes 3145736 | tf_op jit(solution)/shard_map/ZBC/ppermute | solution.py:117
  52.5 0.4 convolution_add_fusion.12
  52.9 1.5 %convolution_add_fusion.11 = f32[512,512]{1,0:T(8,128)S(1)} fusion(f32[512,512]{1,0:T(8,128)S(1)} %convolution_add_fusion.12, bf16[512,512]{1,0:T(8,128)(2,1)} %collective-permute-done.1, bf16[512,8192]{1,0:T(8,128)(2,1)S(1)} %normalise.1, s32[]{:T(128)S(6)} %select_n.183), kind=kOutput, calls=%fused_computation.11 | convolution fusion | flops 268697600 | bytes 3145732 | tf_op jit(solution)/shard_map/dot1/dot_general | solution.py:146
  54.4 0.4 convolution_add_fusion.10
  54.9 0.4 convolution_add_fusion.9
  55.3 1.8 %collective-permute-done.14 = f32[64,512]{1,0:T(8,128)S(1)} collective-permute-done((f32[64,512]{1,0:T(8,128)S(1)}, f32[64,512]{1,0:T(8,128)S(1)}, u32[]{:S(2)}, u32[]{:S(2)}) %collective-permute-start.14) | collective-permute-done | bytes 131104 | tf_op jit(solution)/shard_map/HIGH/ppermute | solution.py:117
  57.2 0.7 collective-permute-start.20
  57.9 3.0 %collective-permute-start.16 = (f32[64,512]{1,0:T(8,128)S(1)}, f32[64,512]{1,0:T(8,128)S(1)}, u32[]{:S(2)}, u32[]{:S(2)}) collective-permute-start(f32[64,512]{1,0:T(8,128)S(1)} %add.210), channel_id=1, source_target_pairs={{0,64},{16,80},{32,96},{48,112},{64,0},{80,16},{96,32},{112,48},{1... | collective-permute-start | bytes 393224 | tf_op jit(solution)/shard_map/K4/ppermute | solution.py:117
  60.9 0.4 convolution_add_fusion.8
  61.3 0.4 convolution_add_fusion.7
  61.8 0.4 convolution_add_fusion.6
  62.2 3.7 %collective-permute-done.16 = f32[64,512]{1,0:T(8,128)S(1)} collective-permute-done((f32[64,512]{1,0:T(8,128)S(1)}, f32[64,512]{1,0:T(8,128)S(1)}, u32[]{:S(2)}, u32[]{:S(2)}) %collective-permute-start.16) | collective-permute-done | bytes 131104 | tf_op jit(solution)/shard_map/K4/ppermute | solution.py:117
  65.9 1.9 %collective-permute-start.19 = (f32[128,512]{1,0:T(8,128)S(1)}, f32[128,512]{1,0:T(8,128)S(1)}, u32[]{:S(2)}, u32[]{:S(2)}) collective-permute-start(f32[128,512]{1,0:T(8,128)S(1)} %pad_maximum_fusion.3), channel_id=1, source_target_pairs={{0,32},{16,48},{32,0},{48,16},{64,96},{80,112},{96,64},{112,80},{1... | collective-permute-start | bytes 786440 | tf_op jit(solution)/shard_map/K5/ppermute | solution.py:117
  68.1 0.4 convolution_add_fusion.5
  68.5 0.4 convolution_add_fusion.4
  69.0 3.4 %collective-permute-done.19 = f32[128,512]{1,0:T(8,128)S(1)} collective-permute-done((f32[128,512]{1,0:T(8,128)S(1)}, f32[128,512]{1,0:T(8,128)S(1)}, u32[]{:S(2)}, u32[]{:S(2)}) %collective-permute-start.19) | collective-permute-done | bytes 262176 | tf_op jit(solution)/shard_map/K5/ppermute | solution.py:117
  72.6 3.0 %collective-permute-done.18 = bf16[1024,512]{1,0:T(8,128)(2,1)S(1)} collective-permute-done((bf16[1024,512]{1,0:T(8,128)(2,1)S(1)}, bf16[1024,512]{1,0:T(8,128)(2,1)S(1)}, u32[]{:S(2)}, u32[]{:S(2)}) %collective-permute-start.18) | collective-permute-done | bytes 1048608 | tf_op jit(solution)/shard_map/ZBC/ppermute | solution.py:117
  75.6 0.4 convolution_add_fusion.3
  76.1 0.4 convolution_add_fusion.2
  76.6 0.4 convolution_add_fusion.1
  77.0 1.3 %collective-permute-done.21 = bf16[512,512]{1,0:T(8,128)(2,1)S(1)} collective-permute-done((bf16[512,512]{1,0:T(8,128)(2,1)S(1)}, bf16[512,512]{1,0:T(8,128)(2,1)S(1)}, u32[]{:S(2)}, u32[]{:S(2)}) %collective-permute-start.21) | collective-permute-done | bytes 524320 | tf_op jit(solution)/shard_map/C3/ppermute | solution.py:117
  78.3 0.4 convolution_add_fusion
  78.7 0.9 %multiply_convert_fusion = bf16[512,512]{1,0:T(8,128)(2,1)} fusion(f32[512,512]{1,0:T(8,128)S(1)} %convolution_add_fusion), kind=kLoop, calls=%fused_computation.23 | loop fusion | flops 524288 | bytes 1572864 | tf_op jit(solution)/shard_map/convert_element_type | solution.py:216
  79.8 2.1 %fusion = (f32[1,512,512]{2,1,0:T(8,128)}, f32[512,512]{1,0:T(8,128)}, f32[512,512]{1,0:T(8,128)}) fusion(f32[1,512,512]{2,1,0:T(8,128)S(1)} %copy-done.1, f32[512,512]{1,0:T(8,128)S(1)} %copy-done.2, f32[512,512]{1,0:T(8,128)S(1)} %pad_maximum_fusion.1, f32[512,512]{1,0:T(8,128)S(1)} %copy-done.3), kind=kLoop, calls=%fused_computation.18 | loop fusion | flops 2359296 | bytes 7340032 | tf_op jit(solution)/shard_map/add | solution.py:220
  (43 shorter events, 1.9 us)
Async XLA Ops:
  0.6 23.2 %copy-start = (f32[8192]{0:T(1024)S(1)}, f32[8192]{0:T(1024)}, u32[]{:S(2)}) copy-start(f32[8192]{0:T(1024)} %param.6) | copy-start | bytes 98308
  1.9 13.7 %collective-permute-start.4 = (bf16[512,512]{1,0:T(8,128)(2,1)S(1)}, bf16[512,512]{1,0:T(8,128)(2,1)}, u32[]{:S(2)}, u32[]{:S(2)}) collective-permute-start(bf16[512,512]{1,0:T(8,128)(2,1)S(1)} %bitcast_convert_fusion), channel_id=1, source_target_pairs={{0,4},{1,5},{2,6},{3,7},{4,0},{5,1},{6,2},{7,3},{8,12},{9,13},{10,... | collective-permute-start | bytes 1572872 | tf_op jit(solution)/shard_map/A0/ppermute | solution.py:117
  3.6 15.3 %collective-permute-start.3 = (bf16[512,512]{1,0:T(8,128)(2,1)S(1)}, bf16[512,512]{1,0:T(8,128)(2,1)S(1)}, u32[]{:S(2)}, u32[]{:S(2)}) collective-permute-start(bf16[512,512]{1,0:T(8,128)(2,1)S(1)} %bitcast_convert_fusion), channel_id=1, source_target_pairs={{0,12},{1,13},{2,14},{3,15},{4,8},{5,9},{6,10},{7,11},{8,4},{9,5},... | collective-permute-start | bytes 1572872 | tf_op jit(solution)/shard_map/B0/ppermute | solution.py:117
  5.8 13.1 %collective-permute-start.2 = (bf16[512,512]{1,0:T(8,128)(2,1)S(1)}, bf16[512,512]{1,0:T(8,128)(2,1)S(1)}, u32[]{:S(2)}, u32[]{:S(2)}) collective-permute-start(bf16[512,512]{1,0:T(8,128)(2,1)S(1)} %bitcast_convert_fusion), channel_id=1, source_target_pairs={{0,16},{1,2},{2,1},{3,19},{4,20},{5,6},{6,5},{7,23},{8,24},{9,10},... | collective-permute-start | bytes 1572872 | tf_op jit(solution)/shard_map/M1/ppermute | solution.py:117
  7.7 12.8 %collective-permute-start.1 = (bf16[512,512]{1,0:T(8,128)(2,1)S(1)}, bf16[512,512]{1,0:T(8,128)(2,1)}, u32[]{:S(2)}, u32[]{:S(2)}) collective-permute-start(bf16[512,512]{1,0:T(8,128)(2,1)S(1)} %bitcast_convert_fusion), channel_id=1, source_target_pairs={{0,1},{1,0},{2,3},{3,2},{4,5},{5,4},{6,7},{7,6},{8,9},{9,8},{10,11... | collective-permute-start | bytes 1572872 | tf_op jit(solution)/shard_map/Z1/ppermute | solution.py:117
  10.3 12.7 %collective-permute-start = (f32[256,512]{1,0:T(8,128)}, f32[256,512]{1,0:T(8,128)S(1)}, u32[]{:S(2)}, u32[]{:S(2)}) collective-permute-start(f32[256,512]{1,0:T(8,128)} %slice_select_fusion), channel_id=1, source_target_pairs={{0,16},{16,0},{32,48},{48,32},{64,80},{80,64},{96,112},{112,96},{1... | collective-permute-start | bytes 1572872 | tf_op jit(solution)/shard_map/K1/ppermute | solution.py:117
  15.6 15.6 %collective-permute-start.8 = (bf16[512,512]{1,0:T(8,128)(2,1)}, bf16[512,512]{1,0:T(8,128)(2,1)S(1)}, u32[]{:S(2)}, u32[]{:S(2)}) collective-permute-start(bf16[512,512]{1,0:T(8,128)(2,1)} %collective-permute-done.4), channel_id=1, source_target_pairs={{0,12},{1,13},{2,14},{3,15},{4,8},{5,9},{6,10},{7,11},{8,4},{9,5},... | collective-permute-start | bytes 1572872 | tf_op jit(solution)/shard_map/C0/ppermute | solution.py:117
  18.9 15.5 %collective-permute-start.9 = (bf16[512,512]{1,0:T(8,128)(2,1)S(1)}, bf16[512,512]{1,0:T(8,128)(2,1)S(1)}, u32[]{:S(2)}, u32[]{:S(2)}) collective-permute-start(bf16[512,512]{1,0:T(8,128)(2,1)S(1)} %collective-permute-done.2), channel_id=1, source_target_pairs={{0,1},{1,0},{2,3},{3,2},{4,5},{5,4},{6,7},{7,6},{8,9},{9,8},{10,11... | collective-permute-start | bytes 1572872 | tf_op jit(solution)/shard_map/E2/ppermute | solution.py:117
  20.5 13.9 %collective-permute-start.7 = (bf16[512,512]{1,0:T(8,128)(2,1)}, bf16[512,512]{1,0:T(8,128)(2,1)S(1)}, u32[]{:S(2)}, u32[]{:S(2)}) collective-permute-start(bf16[512,512]{1,0:T(8,128)(2,1)} %collective-permute-done.1), channel_id=1, source_target_pairs={{0,16},{1,2},{2,1},{3,19},{4,20},{5,6},{6,5},{7,23},{8,24},{9,10},... | collective-permute-start | bytes 1572872 | tf_op jit(solution)/shard_map/M2/ppermute | solution.py:117
  22.8 13.1 %collective-permute-start.6 = (bf16[512,512]{1,0:T(8,128)(2,1)}, bf16[512,512]{1,0:T(8,128)(2,1)S(1)}, u32[]{:S(2)}, u32[]{:S(2)}) collective-permute-start(bf16[512,512]{1,0:T(8,128)(2,1)} %collective-permute-done.1), channel_id=1, source_target_pairs={{0,4},{1,5},{2,6},{3,7},{4,0},{5,1},{6,2},{7,3},{8,12},{9,13},{10,... | collective-permute-start | bytes 1572872 | tf_op jit(solution)/shard_map/A1/ppermute | solution.py:117
  23.2 7.9 %collective-permute-start.5 = (f32[128,512]{1,0:T(8,128)S(1)}, f32[128,512]{1,0:T(8,128)S(1)}, u32[]{:S(2)}, u32[]{:S(2)}) collective-permute-start(f32[128,512]{1,0:T(8,128)S(1)} %slice_select_fusion.1), channel_id=1, source_target_pairs={{0,32},{16,48},{32,0},{48,16},{64,96},{80,112},{96,64},{112,80},{1... | collective-permute-start | bytes 786440 | tf_op jit(solution)/shard_map/K2/ppermute | solution.py:117
  34.4 14.5 %collective-permute-start.11 = (bf16[512,512]{1,0:T(8,128)(2,1)S(1)}, bf16[512,512]{1,0:T(8,128)(2,1)S(1)}, u32[]{:S(2)}, u32[]{:S(2)}) collective-permute-start(bf16[512,512]{1,0:T(8,128)(2,1)S(1)} %collective-permute-done.7), channel_id=1, source_target_pairs={{0,1},{1,0},{2,3},{3,2},{4,5},{5,4},{6,7},{7,6},{8,9},{9,8},{10,11... | collective-permute-start | bytes 1572872 | tf_op jit(solution)/shard_map/E3/ppermute | solution.py:117
  34.5 13.5 %collective-permute-start.12 = (bf16[512,512]{1,0:T(8,128)(2,1)S(1)}, bf16[512,512]{1,0:T(8,128)(2,1)S(1)}, u32[]{:S(2)}, u32[]{:S(2)}) collective-permute-start(bf16[512,512]{1,0:T(8,128)(2,1)S(1)} %broadcast_select_fusion.1), channel_id=1, source_target_pairs={{0,4},{1,5},{2,6},{3,7},{4,0},{5,1},{6,2},{7,3},{8,12},{9,13},{10,... | collective-permute-start | bytes 1572872 | tf_op jit(solution)/shard_map/A2/ppermute | solution.py:117
  35.3 22.6 %collective-permute-start.13 = (bf16[512,512]{1,0:T(8,128)(2,1)S(1)}, bf16[512,512]{1,0:T(8,128)(2,1)S(1)}, u32[]{:S(2)}, u32[]{:S(2)}) collective-permute-start(bf16[512,512]{1,0:T(8,128)(2,1)S(1)} %broadcast_select_fusion.1), channel_id=1, source_target_pairs={{0,12},{1,13},{2,14},{3,15},{4,8},{5,9},{6,10},{7,11},{8,4},{9,5},... | collective-permute-start | bytes 1572872 | tf_op jit(solution)/shard_map/B2/ppermute | solution.py:117
  35.9 6.5 %collective-permute-start.10 = (f32[64,512]{1,0:T(8,128)S(1)}, f32[64,512]{1,0:T(8,128)S(1)}, u32[]{:S(2)}, u32[]{:S(2)}) collective-permute-start(f32[64,512]{1,0:T(8,128)S(1)} %slice_select_fusion.2), channel_id=1, source_target_pairs={{0,64},{16,80},{32,96},{48,112},{64,0},{80,16},{96,32},{112,48},{1... | collective-permute-start | bytes 393224 | tf_op jit(solution)/shard_map/K3/ppermute | solution.py:117
  42.4 14.8 %collective-permute-start.14 = (f32[64,512]{1,0:T(8,128)S(1)}, f32[64,512]{1,0:T(8,128)S(1)}, u32[]{:S(2)}, u32[]{:S(2)}) collective-permute-start(f32[64,512]{1,0:T(8,128)S(1)} %select_add_fusion.2), channel_id=1, source_target_pairs={{0,128},{16,144},{32,160},{48,176},{64,192},{80,208},{96,224},{112... | collective-permute-start | bytes 393224 | tf_op jit(solution)/shard_map/HIGH/ppermute | solution.py:117
  49.0 18.9 %collective-permute-start.15 = (bf16[512,512]{1,0:T(8,128)(2,1)S(1)}, bf16[512,512]{1,0:T(8,128)(2,1)S(1)}, u32[]{:S(2)}, u32[]{:S(2)}) collective-permute-start(bf16[512,512]{1,0:T(8,128)(2,1)S(1)} %broadcast_select_fusion), channel_id=1, source_target_pairs={{0,4},{1,5},{2,6},{3,7},{4,0},{5,1},{6,2},{7,3},{8,12},{9,13},{10,... | collective-permute-start | bytes 1572872 | tf_op jit(solution)/shard_map/A3/ppermute | solution.py:117
  49.5 19.1 %collective-permute-start.17 = (bf16[512,512]{1,0:T(8,128)(2,1)S(1)}, bf16[512,512]{1,0:T(8,128)(2,1)S(1)}, u32[]{:S(2)}, u32[]{:S(2)}) collective-permute-start(bf16[512,512]{1,0:T(8,128)(2,1)S(1)} %collective-permute-done.12), channel_id=1, source_target_pairs={{0,12},{1,13},{2,14},{3,15},{4,8},{5,9},{6,10},{7,11},{8,4},{9,5},... | collective-permute-start | bytes 1572872 | tf_op jit(solution)/shard_map/C2/ppermute | solution.py:117
  50.6 25.1 %collective-permute-start.18 = (bf16[1024,512]{1,0:T(8,128)(2,1)S(1)}, bf16[1024,512]{1,0:T(8,128)(2,1)S(1)}, u32[]{:S(2)}, u32[]{:S(2)}) collective-permute-start(bf16[1024,512]{1,0:T(8,128)(2,1)S(1)} %pad_maximum_fusion), channel_id=1, source_target_pairs={{0,1},{1,0},{2,3},{3,2},{4,5},{5,4},{6,7},{7,6},{8,9},{9,8},{10,11... | collective-permute-start | bytes 3145736 | tf_op jit(solution)/shard_map/ZBC/ppermute | solution.py:117
  57.2 19.4 %collective-permute-start.20 = (bf16[512,512]{1,0:T(8,128)(2,1)S(1)}, bf16[512,512]{1,0:T(8,128)(2,1)S(1)}, u32[]{:S(2)}, u32[]{:S(2)}) collective-permute-start(bf16[512,512]{1,0:T(8,128)(2,1)S(1)} %broadcast_select_fusion), channel_id=1, source_target_pairs={{0,12},{1,13},{2,14},{3,15},{4,8},{5,9},{6,10},{7,11},{8,4},{9,5},... | collective-permute-start | bytes 1572872 | tf_op jit(solution)/shard_map/B3/ppermute | solution.py:117
  57.9 8.0 %collective-permute-start.16 = (f32[64,512]{1,0:T(8,128)S(1)}, f32[64,512]{1,0:T(8,128)S(1)}, u32[]{:S(2)}, u32[]{:S(2)}) collective-permute-start(f32[64,512]{1,0:T(8,128)S(1)} %add.210), channel_id=1, source_target_pairs={{0,64},{16,80},{32,96},{48,112},{64,0},{80,16},{96,32},{112,48},{1... | collective-permute-start | bytes 393224 | tf_op jit(solution)/shard_map/K4/ppermute | solution.py:117
  65.9 6.5 %collective-permute-start.19 = (f32[128,512]{1,0:T(8,128)S(1)}, f32[128,512]{1,0:T(8,128)S(1)}, u32[]{:S(2)}, u32[]{:S(2)}) collective-permute-start(f32[128,512]{1,0:T(8,128)S(1)} %pad_maximum_fusion.3), channel_id=1, source_target_pairs={{0,32},{16,48},{32,0},{48,16},{64,96},{80,112},{96,64},{112,80},{1... | collective-permute-start | bytes 786440 | tf_op jit(solution)/shard_map/K5/ppermute | solution.py:117
  67.9 10.4 %collective-permute-start.21 = (bf16[512,512]{1,0:T(8,128)(2,1)S(1)}, bf16[512,512]{1,0:T(8,128)(2,1)S(1)}, u32[]{:S(2)}, u32[]{:S(2)}) collective-permute-start(bf16[512,512]{1,0:T(8,128)(2,1)S(1)} %collective-permute-done.15), channel_id=1, source_target_pairs={{0,12},{1,13},{2,14},{3,15},{4,8},{5,9},{6,10},{7,11},{8,4},{9,5},... | collective-permute-start | bytes 1572872 | tf_op jit(solution)/shard_map/C3/ppermute | solution.py:117
  72.5 7.2 %collective-permute-start.22 = (f32[256,512]{1,0:T(8,128)S(1)}, f32[256,512]{1,0:T(8,128)S(1)}, u32[]{:S(2)}, u32[]{:S(2)}) collective-permute-start(f32[256,512]{1,0:T(8,128)S(1)} %pad_maximum_fusion.2), channel_id=1, source_target_pairs={{0,16},{16,0},{32,48},{48,32},{64,80},{80,64},{96,112},{112,96},{1... | collective-permute-start | bytes 1572872 | tf_op jit(solution)/shard_map/K6/ppermute | solution.py:117
  76.1 3.8 %copy-start.1 = (f32[1,512,512]{2,1,0:T(8,128)S(1)}, f32[1,512,512]{2,1,0:T(8,128)}, u32[]{:S(2)}) copy-start(f32[1,512,512]{2,1,0:T(8,128)} %param.9) | copy-start | bytes 3145732
  76.1 3.7 %copy-start.2 = (f32[512,512]{1,0:T(8,128)S(1)}, f32[512,512]{1,0:T(8,128)}, u32[]{:S(2)}) copy-start(f32[512,512]{1,0:T(8,128)} %param.7) | copy-start | bytes 3145732
  76.1 3.7 %copy-start.3 = (f32[512,512]{1,0:T(8,128)S(1)}, f32[512,512]{1,0:T(8,128)}, u32[]{:S(2)}) copy-start(f32[512,512]{1,0:T(8,128)} %param.8) | copy-start | bytes 3145732

commit v5 on v4

--- a/solution.py
+++ b/solution.py
@@ -212,8 +212,11 @@
     add_product("dot1", rest[:ROWS], far_y, z ^ 1)
     add_product("dot1", rest[ROWS:], y ^ 2, z ^ 1)
     add_product("dot3", order(b3), far_y, z ^ 3)
-    add_product("dot3", order(c3), y ^ 2, z ^ 3)
-    keys = order((summed[0] * (1.0 / math.sqrt(D))).astype(jnp.bfloat16))
+    part = lax.dynamic_slice(
+        normed, (0, ((y ^ 2) * 4 + (z ^ 3)) * ROWS), (normed.shape[0], ROWS)
+    )
+    last = jnp.dot(part, order(c3), preferred_element_type=jnp.float32)
+    keys = order(((summed[0] + last) * (1.0 / math.sqrt(D))).astype(jnp.bfloat16))
     total = order(join(total, order(k6), core == 1))
     islands = lax.axis_size("island")
     params_out, momentum_out = outer_update(outer_params, momentum, total / islands)

time: 82.1 us -> 82 us (level)
  other arithmetic: 7.67 us -> 6.75 us
    dot_general x0 -> x1, matrix products: none -> 1.24 us  [body(): last = jnp.dot(part, order(c3), preferred_element_type=jnp.float32)]
    convert_element_type x1 -> x0, other arithmetic: 0.92 us -> none  [body(): keys = order((summed[0] * (1.0 / math.sqrt(D))).astype(jnp.bfloat16))]
    dot_general x16 -> x15, matrix products: 9.12 us -> 8.69 us  [add_product(): jnp.dot(part, block, preferred_element_type=jnp.float32)]
where the time goes in v5:
time: 82 us; the launch traced here: 81.8 us
  starting transfers between devices  30.8 us (38%)
  waiting for transfers between devices  26.8 us (33%)
  matrix products  9.92 us (12%)
  other arithmetic  6.75 us (8%)
  Pallas kernels  6.49 us (8%)
  between operations  0.95 us (1%)
    ppermute x23, starting transfers between devices, send(): return lax.ppermute(value, axis, pairs)  30.8 us
    ppermute x23, waiting for transfers between devices, send(): return lax.ppermute(value, axis, pairs)  26.8 us
    dot_general x15, matrix products, add_product(): jnp.dot(part, block, preferred_element_type=jnp.float32)  8.69 us
    pallas_call x1, Pallas kernels, normalise(): pl.pallas_call(norm_kernel, out_shape=jax.ShapeDtypeStruct(tokens.shape,...  6.49 us
    add x1, other arithmetic, body(): mixed = mix_share * local_weights + (1.0 - mix_share) * params_out[None]  2.06 us
    sub x1, other arithmetic, body(): keep, give = split(order(outer_params - own_copy), core == 1)  1.75 us
  transfers between devices with their start and end apart: 23, of which 11 were waited for; matrix products, arithmetic and copies ran while one was open for 16% of the time, Pallas kernels for 8%

profile of v5, /device:TPU:34, one launch (start us, length us, event | category | flops | bytes accessed | tf_op | source)
XLA Modules:
  0.0 81.8 jit_solution(9193017125546136915)
XLA Ops:
  0.6 1.3 %bitcast_convert_fusion = bf16[512,512]{1,0:T(8,128)(2,1)S(1)} fusion(f32[1,512,512]{2,1,0:T(8,128)} %param.9), kind=kLoop, calls=%fused_computation.21 | loop fusion | flops 262144 | bytes 1572864 | tf_op jit(solution)/shard_map/convert_element_type | solution.py:152
  1.9 1.7 %collective-permute-start.4 = (bf16[512,512]{1,0:T(8,128)(2,1)S(1)}, bf16[512,512]{1,0:T(8,128)(2,1)}, u32[]{:S(2)}, u32[]{:S(2)}) collective-permute-start(bf16[512,512]{1,0:T(8,128)(2,1)S(1)} %bitcast_convert_fusion), channel_id=1, source_target_pairs={{0,4},{1,5},{2,6},{3,7},{4,0},{5,1},{6,2},{7,3},{8,12},{9,13},{10,... | collective-permute-start | bytes 1572872 | tf_op jit(solution)/shard_map/A0/ppermute | solution.py:117
  3.6 2.2 %collective-permute-start.3 = (bf16[512,512]{1,0:T(8,128)(2,1)S(1)}, bf16[512,512]{1,0:T(8,128)(2,1)S(1)}, u32[]{:S(2)}, u32[]{:S(2)}) collective-permute-start(bf16[512,512]{1,0:T(8,128)(2,1)S(1)} %bitcast_convert_fusion), channel_id=1, source_target_pairs={{0,12},{1,13},{2,14},{3,15},{4,8},{5,9},{6,10},{7,11},{8,4},{9,5},... | collective-permute-start | bytes 1572872 | tf_op jit(solution)/shard_map/B0/ppermute | solution.py:117
  5.8 1.9 %collective-permute-start.2 = (bf16[512,512]{1,0:T(8,128)(2,1)S(1)}, bf16[512,512]{1,0:T(8,128)(2,1)S(1)}, u32[]{:S(2)}, u32[]{:S(2)}) collective-permute-start(bf16[512,512]{1,0:T(8,128)(2,1)S(1)} %bitcast_convert_fusion), channel_id=1, source_target_pairs={{0,16},{1,2},{2,1},{3,19},{4,20},{5,6},{6,5},{7,23},{8,24},{9,10},... | collective-permute-start | bytes 1572872 | tf_op jit(solution)/shard_map/M1/ppermute | solution.py:117
  7.7 1.7 %bitcast_subtract_fusion = f32[512,512]{1,0:T(8,128)S(1)} fusion(f32[512,512]{1,0:T(8,128)} %param.7, f32[1,512,512]{2,1,0:T(8,128)} %param.9), kind=kLoop, calls=%fused_computation.22 | loop fusion | flops 262144 | bytes 3145728 | tf_op jit(solution)/shard_map/sub | solution.py:157
  9.5 0.9 %slice_select_fusion = f32[256,512]{1,0:T(8,128)} fusion(f32[512,512]{1,0:T(8,128)S(1)} %bitcast_subtract_fusion, pred[]{:T(512)S(6)} %eq.29), kind=kLoop, calls=%fused_computation.48 | loop fusion | flops 131072 | bytes 1572865 | tf_op jit(solution)/shard_map/jit(_where)/select_n | solution.py:123
  10.3 5.3 %collective-permute-done.4 = bf16[512,512]{1,0:T(8,128)(2,1)} collective-permute-done((bf16[512,512]{1,0:T(8,128)(2,1)S(1)}, bf16[512,512]{1,0:T(8,128)(2,1)}, u32[]{:S(2)}, u32[]{:S(2)}) %collective-permute-start.4) | collective-permute-done | bytes 524320 | tf_op jit(solution)/shard_map/A0/ppermute | solution.py:117
  15.6 3.3 %collective-permute-start.8 = (bf16[512,512]{1,0:T(8,128)(2,1)}, bf16[512,512]{1,0:T(8,128)(2,1)S(1)}, u32[]{:S(2)}, u32[]{:S(2)}) collective-permute-start(bf16[512,512]{1,0:T(8,128)(2,1)} %collective-permute-done.4), channel_id=1, source_target_pairs={{0,12},{1,13},{2,14},{3,15},{4,8},{5,9},{6,10},{7,11},{8,4},{9,5},... | collective-permute-start | bytes 1572872 | tf_op jit(solution)/shard_map/C0/ppermute | solution.py:117
  19.0 1.5 %collective-permute-done.1 = bf16[512,512]{1,0:T(8,128)(2,1)} collective-permute-done((bf16[512,512]{1,0:T(8,128)(2,1)S(1)}, bf16[512,512]{1,0:T(8,128)(2,1)}, u32[]{:S(2)}, u32[]{:S(2)}) %collective-permute-start.1) | collective-permute-done | bytes 524320 | tf_op jit(solution)/shard_map/Z1/ppermute | solution.py:117
  20.5 2.2 %collective-permute-start.7 = (bf16[512,512]{1,0:T(8,128)(2,1)}, bf16[512,512]{1,0:T(8,128)(2,1)S(1)}, u32[]{:S(2)}, u32[]{:S(2)}) collective-permute-start(bf16[512,512]{1,0:T(8,128)(2,1)} %collective-permute-done.1), channel_id=1, source_target_pairs={{0,16},{1,2},{2,1},{3,19},{4,20},{5,6},{6,5},{7,23},{8,24},{9,10},... | collective-permute-start | bytes 1572872 | tf_op jit(solution)/shard_map/M2/ppermute | solution.py:117
  23.2 0.6 collective-permute-start.5
  23.8 6.5 %normalise.1 = bf16[512,8192]{1,0:T(8,128)(2,1)S(1)} custom-call(bf16[512,8192]{1,0:T(8,128)(2,1)} %tokens_ref.1, f32[1,8192]{1,0:T(1,128)S(1)} %bitcast.22), custom_call_target="tpu_custom_call" | custom-call | flops 25165824 | bytes 16777216 | tf_op jit(solution)/shard_map/normalise/pallas_call | solution.py:94
  30.3 0.4 fusion.20
  30.8 0.4 collective-permute-done.5
  31.2 3.2 %collective-permute-done.7 = bf16[512,512]{1,0:T(8,128)(2,1)S(1)} collective-permute-done((bf16[512,512]{1,0:T(8,128)(2,1)}, bf16[512,512]{1,0:T(8,128)(2,1)S(1)}, u32[]{:S(2)}, u32[]{:S(2)}) %collective-permute-start.7) | collective-permute-done | bytes 524320 | tf_op jit(solution)/shard_map/M2/ppermute | solution.py:117
  34.5 0.8 collective-permute-start.12
  35.3 0.6 collective-permute-start.13
  35.9 2.1 %collective-permute-start.10 = (f32[64,512]{1,0:T(8,128)S(1)}, f32[64,512]{1,0:T(8,128)S(1)}, u32[]{:S(2)}, u32[]{:S(2)}) collective-permute-start(f32[64,512]{1,0:T(8,128)S(1)} %slice_select_fusion.2), channel_id=1, source_target_pairs={{0,64},{16,80},{32,96},{48,112},{64,0},{80,16},{96,32},{112,48},{1... | collective-permute-start | bytes 393224 | tf_op jit(solution)/shard_map/K3/ppermute | solution.py:117
  38.0 1.5 %convolution_add_fusion.14 = f32[512,512]{1,0:T(8,128)S(1)} fusion(f32[512,512]{1,0:T(8,128)S(1)} %fusion.20, bf16[512,512]{1,0:T(8,128)(2,1)} %collective-permute-done.4, bf16[512,8192]{1,0:T(8,128)(2,1)S(1)} %normalise.1, s32[]{:T(128)S(6)} %select_n.177), kind=kOutput, calls=%fused_computation.15 | convolution fusion | flops 268697600 | bytes 3145732 | tf_op jit(solution)/shard_map/dot0/dot_general | solution.py:146
  39.5 0.4 convolution_add_fusion.13
  40.0 2.3 %collective-permute-done.10 = f32[64,512]{1,0:T(8,128)S(1)} collective-permute-done((f32[64,512]{1,0:T(8,128)S(1)}, f32[64,512]{1,0:T(8,128)S(1)}, u32[]{:S(2)}, u32[]{:S(2)}) %collective-permute-start.10) | collective-permute-done | bytes 131104 | tf_op jit(solution)/shard_map/K3/ppermute | solution.py:117
  42.4 5.6 %collective-permute-start.14 = (f32[64,512]{1,0:T(8,128)S(1)}, f32[64,512]{1,0:T(8,128)S(1)}, u32[]{:S(2)}, u32[]{:S(2)}) collective-permute-start(f32[64,512]{1,0:T(8,128)S(1)} %select_add_fusion.2), channel_id=1, source_target_pairs={{0,128},{16,144},{32,160},{48,176},{64,192},{80,208},{96,224},{112... | collective-permute-start | bytes 393224 | tf_op jit(solution)/shard_map/HIGH/ppermute | solution.py:117
  48.0 0.9 %collective-permute-done.11 = bf16[512,512]{1,0:T(8,128)(2,1)S(1)} collective-permute-done((bf16[512,512]{1,0:T(8,128)(2,1)S(1)}, bf16[512,512]{1,0:T(8,128)(2,1)S(1)}, u32[]{:S(2)}, u32[]{:S(2)}) %collective-permute-start.11) | collective-permute-done | bytes 524320 | tf_op jit(solution)/shard_map/E3/ppermute | solution.py:117
  49.0 0.5 collective-permute-start.15
  49.5 1.1 %collective-permute-start.17 = (bf16[512,512]{1,0:T(8,128)(2,1)S(1)}, bf16[512,512]{1,0:T(8,128)(2,1)S(1)}, u32[]{:S(2)}, u32[]{:S(2)}) collective-permute-start(bf16[512,512]{1,0:T(8,128)(2,1)S(1)} %collective-permute-done.12), channel_id=1, source_target_pairs={{0,12},{1,13},{2,14},{3,15},{4,8},{5,9},{6,10},{7,11},{8,4},{9,5},... | collective-permute-start | bytes 1572872 | tf_op jit(solution)/shard_map/C2/ppermute | solution.py:117
  50.6 1.9 %collective-permute-start.18 = (bf16[1024,512]{1,0:T(8,128)(2,1)S(1)}, bf16[1024,512]{1,0:T(8,128)(2,1)S(1)}, u32[]{:S(2)}, u32[]{:S(2)}) collective-permute-start(bf16[1024,512]{1,0:T(8,128)(2,1)S(1)} %pad_maximum_fusion), channel_id=1, source_target_pairs={{0,1},{1,0},{2,3},{3,2},{4,5},{5,4},{6,7},{7,6},{8,9},{9,8},{10,11... | collective-permute-start | bytes 3145736 | tf_op jit(solution)/shard_map/ZBC/ppermute | solution.py:117
  52.5 0.4 convolution_add_fusion.12
  52.9 1.5 %convolution_add_fusion.11 = f32[512,512]{1,0:T(8,128)S(1)} fusion(f32[512,512]{1,0:T(8,128)S(1)} %convolution_add_fusion.12, bf16[512,512]{1,0:T(8,128)(2,1)} %collective-permute-done.1, bf16[512,8192]{1,0:T(8,128)(2,1)S(1)} %normalise.1, s32[]{:T(128)S(6)} %select_n.183), kind=kOutput, calls=%fused_computation.12 | convolution fusion | flops 268697600 | bytes 3145732 | tf_op jit(solution)/shard_map/dot1/dot_general | solution.py:146
  54.4 0.4 convolution_add_fusion.10
  54.9 0.4 convolution_add_fusion.9
  55.3 1.8 %collective-permute-done.14 = f32[64,512]{1,0:T(8,128)S(1)} collective-permute-done((f32[64,512]{1,0:T(8,128)S(1)}, f32[64,512]{1,0:T(8,128)S(1)}, u32[]{:S(2)}, u32[]{:S(2)}) %collective-permute-start.14) | collective-permute-done | bytes 131104 | tf_op jit(solution)/shard_map/HIGH/ppermute | solution.py:117
  57.2 0.7 collective-permute-start.20
  57.9 3.0 %collective-permute-start.16 = (f32[64,512]{1,0:T(8,128)S(1)}, f32[64,512]{1,0:T(8,128)S(1)}, u32[]{:S(2)}, u32[]{:S(2)}) collective-permute-start(f32[64,512]{1,0:T(8,128)S(1)} %add.210), channel_id=1, source_target_pairs={{0,64},{16,80},{32,96},{48,112},{64,0},{80,16},{96,32},{112,48},{1... | collective-permute-start | bytes 393224 | tf_op jit(solution)/shard_map/K4/ppermute | solution.py:117
  60.9 0.4 convolution_add_fusion.8
  61.3 0.4 convolution_add_fusion.7
  61.8 0.4 convolution_add_fusion.6
  62.2 3.7 %collective-permute-done.16 = f32[64,512]{1,0:T(8,128)S(1)} collective-permute-done((f32[64,512]{1,0:T(8,128)S(1)}, f32[64,512]{1,0:T(8,128)S(1)}, u32[]{:S(2)}, u32[]{:S(2)}) %collective-permute-start.16) | collective-permute-done | bytes 131104 | tf_op jit(solution)/shard_map/K4/ppermute | solution.py:117
  65.9 1.9 %collective-permute-start.19 = (f32[128,512]{1,0:T(8,128)S(1)}, f32[128,512]{1,0:T(8,128)S(1)}, u32[]{:S(2)}, u32[]{:S(2)}) collective-permute-start(f32[128,512]{1,0:T(8,128)S(1)} %pad_maximum_fusion.3), channel_id=1, source_target_pairs={{0,32},{16,48},{32,0},{48,16},{64,96},{80,112},{96,64},{112,80},{1... | collective-permute-start | bytes 786440 | tf_op jit(solution)/shard_map/K5/ppermute | solution.py:117
  68.1 0.4 convolution_add_fusion.5
  68.5 0.4 convolution_add_fusion.4
  69.0 3.4 %collective-permute-done.19 = f32[128,512]{1,0:T(8,128)S(1)} collective-permute-done((f32[128,512]{1,0:T(8,128)S(1)}, f32[128,512]{1,0:T(8,128)S(1)}, u32[]{:S(2)}, u32[]{:S(2)}) %collective-permute-start.19) | collective-permute-done | bytes 262176 | tf_op jit(solution)/shard_map/K5/ppermute | solution.py:117
  72.6 3.0 %collective-permute-done.18 = bf16[1024,512]{1,0:T(8,128)(2,1)S(1)} collective-permute-done((bf16[1024,512]{1,0:T(8,128)(2,1)S(1)}, bf16[1024,512]{1,0:T(8,128)(2,1)S(1)}, u32[]{:S(2)}, u32[]{:S(2)}) %collective-permute-start.18) | collective-permute-done | bytes 1048608 | tf_op jit(solution)/shard_map/ZBC/ppermute | solution.py:117
  75.6 0.4 convolution_add_fusion.3
  76.1 0.4 convolution_add_fusion.2
  76.5 0.4 convolution_add_fusion.1
  77.0 1.3 %collective-permute-done.21 = bf16[512,512]{1,0:T(8,128)(2,1)S(1)} collective-permute-done((bf16[512,512]{1,0:T(8,128)(2,1)S(1)}, bf16[512,512]{1,0:T(8,128)(2,1)S(1)}, u32[]{:S(2)}, u32[]{:S(2)}) %collective-permute-start.21) | collective-permute-done | bytes 524320 | tf_op jit(solution)/shard_map/C3/ppermute | solution.py:117
  78.3 1.2 %fusion.1 = bf16[512,512]{1,0:T(8,128)(2,1)} fusion(f32[512,512]{1,0:T(8,128)S(1)} %convolution_add_fusion.1, bf16[512,512]{1,0:T(8,128)(2,1)S(1)} %collective-permute-done.21, bf16[512,8192]{1,0:T(8,128)(2,1)S(1)} %normalise.1, s32[]{:T(128)S(6)} %select_n.198), kind=kOutput, calls=%fused_computation.16 | convolution fusion | flops 269221888 | bytes 2621444 | tf_op jit(solution)/shard_map/dot_general | solution.py:218
  79.7 2.1 %fusion.2 = (f32[1,512,512]{2,1,0:T(8,128)}, f32[512,512]{1,0:T(8,128)}, f32[512,512]{1,0:T(8,128)}) fusion(f32[1,512,512]{2,1,0:T(8,128)S(1)} %copy-done.1, f32[512,512]{1,0:T(8,128)S(1)} %copy-done.2, f32[512,512]{1,0:T(8,128)S(1)} %pad_maximum_fusion.1, f32[512,512]{1,0:T(8,128)S(1)} %copy-done.3), kind=kLoop, calls=%fused_computation.20 | loop fusion | flops 2359296 | bytes 7340032 | tf_op jit(solution)/shard_map/add | solution.py:223
  (42 shorter events, 1.5 us)
Async XLA Ops:
  0.6 23.2 %copy-start = (f32[8192]{0:T(1024)S(1)}, f32[8192]{0:T(1024)}, u32[]{:S(2)}) copy-start(f32[8192]{0:T(1024)} %param.6) | copy-start | bytes 98308
  1.9 13.7 %collective-permute-start.4 = (bf16[512,512]{1,0:T(8,128)(2,1)S(1)}, bf16[512,512]{1,0:T(8,128)(2,1)}, u32[]{:S(2)}, u32[]{:S(2)}) collective-permute-start(bf16[512,512]{1,0:T(8,128)(2,1)S(1)} %bitcast_convert_fusion), channel_id=1, source_target_pairs={{0,4},{1,5},{2,6},{3,7},{4,0},{5,1},{6,2},{7,3},{8,12},{9,13},{10,... | collective-permute-start | bytes 1572872 | tf_op jit(solution)/shard_map/A0/ppermute | solution.py:117
  3.6 15.3 %collective-permute-start.3 = (bf16[512,512]{1,0:T(8,128)(2,1)S(1)}, bf16[512,512]{1,0:T(8,128)(2,1)S(1)}, u32[]{:S(2)}, u32[]{:S(2)}) collective-permute-start(bf16[512,512]{1,0:T(8,128)(2,1)S(1)} %bitcast_convert_fusion), channel_id=1, source_target_pairs={{0,12},{1,13},{2,14},{3,15},{4,8},{5,9},{6,10},{7,11},{8,4},{9,5},... | collective-permute-start | bytes 1572872 | tf_op jit(solution)/shard_map/B0/ppermute | solution.py:117
  5.8 13.1 %collective-permute-start.2 = (bf16[512,512]{1,0:T(8,128)(2,1)S(1)}, bf16[512,512]{1,0:T(8,128)(2,1)S(1)}, u32[]{:S(2)}, u32[]{:S(2)}) collective-permute-start(bf16[512,512]{1,0:T(8,128)(2,1)S(1)} %bitcast_convert_fusion), channel_id=1, source_target_pairs={{0,16},{1,2},{2,1},{3,19},{4,20},{5,6},{6,5},{7,23},{8,24},{9,10},... | collective-permute-start | bytes 1572872 | tf_op jit(solution)/shard_map/M1/ppermute | solution.py:117
  7.7 12.8 %collective-permute-start.1 = (bf16[512,512]{1,0:T(8,128)(2,1)S(1)}, bf16[512,512]{1,0:T(8,128)(2,1)}, u32[]{:S(2)}, u32[]{:S(2)}) collective-permute-start(bf16[512,512]{1,0:T(8,128)(2,1)S(1)} %bitcast_convert_fusion), channel_id=1, source_target_pairs={{0,1},{1,0},{2,3},{3,2},{4,5},{5,4},{6,7},{7,6},{8,9},{9,8},{10,11... | collective-permute-start | bytes 1572872 | tf_op jit(solution)/shard_map/Z1/ppermute | solution.py:117
  10.3 12.7 %collective-permute-start = (f32[256,512]{1,0:T(8,128)}, f32[256,512]{1,0:T(8,128)S(1)}, u32[]{:S(2)}, u32[]{:S(2)}) collective-permute-start(f32[256,512]{1,0:T(8,128)} %slice_select_fusion), channel_id=1, source_target_pairs={{0,16},{16,0},{32,48},{48,32},{64,80},{80,64},{96,112},{112,96},{1... | collective-permute-start | bytes 1572872 | tf_op jit(solution)/shard_map/K1/ppermute | solution.py:117
  15.6 15.6 %collective-permute-start.8 = (bf16[512,512]{1,0:T(8,128)(2,1)}, bf16[512,512]{1,0:T(8,128)(2,1)S(1)}, u32[]{:S(2)}, u32[]{:S(2)}) collective-permute-start(bf16[512,512]{1,0:T(8,128)(2,1)} %collective-permute-done.4), channel_id=1, source_target_pairs={{0,12},{1,13},{2,14},{3,15},{4,8},{5,9},{6,10},{7,11},{8,4},{9,5},... | collective-permute-start | bytes 1572872 | tf_op jit(solution)/shard_map/C0/ppermute | solution.py:117
  18.9 15.5 %collective-permute-start.9 = (bf16[512,512]{1,0:T(8,128)(2,1)S(1)}, bf16[512,512]{1,0:T(8,128)(2,1)S(1)}, u32[]{:S(2)}, u32[]{:S(2)}) collective-permute-start(bf16[512,512]{1,0:T(8,128)(2,1)S(1)} %collective-permute-done.2), channel_id=1, source_target_pairs={{0,1},{1,0},{2,3},{3,2},{4,5},{5,4},{6,7},{7,6},{8,9},{9,8},{10,11... | collective-permute-start | bytes 1572872 | tf_op jit(solution)/shard_map/E2/ppermute | solution.py:117
  20.5 13.9 %collective-permute-start.7 = (bf16[512,512]{1,0:T(8,128)(2,1)}, bf16[512,512]{1,0:T(8,128)(2,1)S(1)}, u32[]{:S(2)}, u32[]{:S(2)}) collective-permute-start(bf16[512,512]{1,0:T(8,128)(2,1)} %collective-permute-done.1), channel_id=1, source_target_pairs={{0,16},{1,2},{2,1},{3,19},{4,20},{5,6},{6,5},{7,23},{8,24},{9,10},... | collective-permute-start | bytes 1572872 | tf_op jit(solution)/shard_map/M2/ppermute | solution.py:117
  22.8 13.1 %collective-permute-start.6 = (bf16[512,512]{1,0:T(8,128)(2,1)}, bf16[512,512]{1,0:T(8,128)(2,1)S(1)}, u32[]{:S(2)}, u32[]{:S(2)}) collective-permute-start(bf16[512,512]{1,0:T(8,128)(2,1)} %collective-permute-done.1), channel_id=1, source_target_pairs={{0,4},{1,5},{2,6},{3,7},{4,0},{5,1},{6,2},{7,3},{8,12},{9,13},{10,... | collective-permute-start | bytes 1572872 | tf_op jit(solution)/shard_map/A1/ppermute | solution.py:117
  23.2 7.9 %collective-permute-start.5 = (f32[128,512]{1,0:T(8,128)S(1)}, f32[128,512]{1,0:T(8,128)S(1)}, u32[]{:S(2)}, u32[]{:S(2)}) collective-permute-start(f32[128,512]{1,0:T(8,128)S(1)} %slice_select_fusion.1), channel_id=1, source_target_pairs={{0,32},{16,48},{32,0},{48,16},{64,96},{80,112},{96,64},{112,80},{1... | collective-permute-start | bytes 786440 | tf_op jit(solution)/shard_map/K2/ppermute | solution.py:117
  34.4 14.5 %collective-permute-start.11 = (bf16[512,512]{1,0:T(8,128)(2,1)S(1)}, bf16[512,512]{1,0:T(8,128)(2,1)S(1)}, u32[]{:S(2)}, u32[]{:S(2)}) collective-permute-start(bf16[512,512]{1,0:T(8,128)(2,1)S(1)} %collective-permute-done.7), channel_id=1, source_target_pairs={{0,1},{1,0},{2,3},{3,2},{4,5},{5,4},{6,7},{7,6},{8,9},{9,8},{10,11... | collective-permute-start | bytes 1572872 | tf_op jit(solution)/shard_map/E3/ppermute | solution.py:117
  34.5 13.5 %collective-permute-start.12 = (bf16[512,512]{1,0:T(8,128)(2,1)S(1)}, bf16[512,512]{1,0:T(8,128)(2,1)S(1)}, u32[]{:S(2)}, u32[]{:S(2)}) collective-permute-start(bf16[512,512]{1,0:T(8,128)(2,1)S(1)} %broadcast_select_fusion.1), channel_id=1, source_target_pairs={{0,4},{1,5},{2,6},{3,7},{4,0},{5,1},{6,2},{7,3},{8,12},{9,13},{10,... | collective-permute-start | bytes 1572872 | tf_op jit(solution)/shard_map/A2/ppermute | solution.py:117
  35.3 22.6 %collective-permute-start.13 = (bf16[512,512]{1,0:T(8,128)(2,1)S(1)}, bf16[512,512]{1,0:T(8,128)(2,1)S(1)}, u32[]{:S(2)}, u32[]{:S(2)}) collective-permute-start(bf16[512,512]{1,0:T(8,128)(2,1)S(1)} %broadcast_select_fusion.1), channel_id=1, source_target_pairs={{0,12},{1,13},{2,14},{3,15},{4,8},{5,9},{6,10},{7,11},{8,4},{9,5},... | collective-permute-start | bytes 1572872 | tf_op jit(solution)/shard_map/B2/ppermute | solution.py:117
  35.9 6.5 %collective-permute-start.10 = (f32[64,512]{1,0:T(8,128)S(1)}, f32[64,512]{1,0:T(8,128)S(1)}, u32[]{:S(2)}, u32[]{:S(2)}) collective-permute-start(f32[64,512]{1,0:T(8,128)S(1)} %slice_select_fusion.2), channel_id=1, source_target_pairs={{0,64},{16,80},{32,96},{48,112},{64,0},{80,16},{96,32},{112,48},{1... | collective-permute-start | bytes 393224 | tf_op jit(solution)/shard_map/K3/ppermute | solution.py:117
  42.4 14.8 %collective-permute-start.14 = (f32[64,512]{1,0:T(8,128)S(1)}, f32[64,512]{1,0:T(8,128)S(1)}, u32[]{:S(2)}, u32[]{:S(2)}) collective-permute-start(f32[64,512]{1,0:T(8,128)S(1)} %select_add_fusion.2), channel_id=1, source_target_pairs={{0,128},{16,144},{32,160},{48,176},{64,192},{80,208},{96,224},{112... | collective-permute-start | bytes 393224 | tf_op jit(solution)/shard_map/HIGH/ppermute | solution.py:117
  49.0 18.9 %collective-permute-start.15 = (bf16[512,512]{1,0:T(8,128)(2,1)S(1)}, bf16[512,512]{1,0:T(8,128)(2,1)S(1)}, u32[]{:S(2)}, u32[]{:S(2)}) collective-permute-start(bf16[512,512]{1,0:T(8,128)(2,1)S(1)} %broadcast_select_fusion), channel_id=1, source_target_pairs={{0,4},{1,5},{2,6},{3,7},{4,0},{5,1},{6,2},{7,3},{8,12},{9,13},{10,... | collective-permute-start | bytes 1572872 | tf_op jit(solution)/shard_map/A3/ppermute | solution.py:117
  49.5 19.1 %collective-permute-start.17 = (bf16[512,512]{1,0:T(8,128)(2,1)S(1)}, bf16[512,512]{1,0:T(8,128)(2,1)S(1)}, u32[]{:S(2)}, u32[]{:S(2)}) collective-permute-start(bf16[512,512]{1,0:T(8,128)(2,1)S(1)} %collective-permute-done.12), channel_id=1, source_target_pairs={{0,12},{1,13},{2,14},{3,15},{4,8},{5,9},{6,10},{7,11},{8,4},{9,5},... | collective-permute-start | bytes 1572872 | tf_op jit(solution)/shard_map/C2/ppermute | solution.py:117
  50.6 25.1 %collective-permute-start.18 = (bf16[1024,512]{1,0:T(8,128)(2,1)S(1)}, bf16[1024,512]{1,0:T(8,128)(2,1)S(1)}, u32[]{:S(2)}, u32[]{:S(2)}) collective-permute-start(bf16[1024,512]{1,0:T(8,128)(2,1)S(1)} %pad_maximum_fusion), channel_id=1, source_target_pairs={{0,1},{1,0},{2,3},{3,2},{4,5},{5,4},{6,7},{7,6},{8,9},{9,8},{10,11... | collective-permute-start | bytes 3145736 | tf_op jit(solution)/shard_map/ZBC/ppermute | solution.py:117
  57.2 19.3 %collective-permute-start.20 = (bf16[512,512]{1,0:T(8,128)(2,1)S(1)}, bf16[512,512]{1,0:T(8,128)(2,1)S(1)}, u32[]{:S(2)}, u32[]{:S(2)}) collective-permute-start(bf16[512,512]{1,0:T(8,128)(2,1)S(1)} %broadcast_select_fusion), channel_id=1, source_target_pairs={{0,12},{1,13},{2,14},{3,15},{4,8},{5,9},{6,10},{7,11},{8,4},{9,5},... | collective-permute-start | bytes 1572872 | tf_op jit(solution)/shard_map/B3/ppermute | solution.py:117
  57.9 8.0 %collective-permute-start.16 = (f32[64,512]{1,0:T(8,128)S(1)}, f32[64,512]{1,0:T(8,128)S(1)}, u32[]{:S(2)}, u32[]{:S(2)}) collective-permute-start(f32[64,512]{1,0:T(8,128)S(1)} %add.210), channel_id=1, source_target_pairs={{0,64},{16,80},{32,96},{48,112},{64,0},{80,16},{96,32},{112,48},{1... | collective-permute-start | bytes 393224 | tf_op jit(solution)/shard_map/K4/ppermute | solution.py:117
  65.9 6.5 %collective-permute-start.19 = (f32[128,512]{1,0:T(8,128)S(1)}, f32[128,512]{1,0:T(8,128)S(1)}, u32[]{:S(2)}, u32[]{:S(2)}) collective-permute-start(f32[128,512]{1,0:T(8,128)S(1)} %pad_maximum_fusion.3), channel_id=1, source_target_pairs={{0,32},{16,48},{32,0},{48,16},{64,96},{80,112},{96,64},{112,80},{1... | collective-permute-start | bytes 786440 | tf_op jit(solution)/shard_map/K5/ppermute | solution.py:117
  67.9 10.4 %collective-permute-start.21 = (bf16[512,512]{1,0:T(8,128)(2,1)S(1)}, bf16[512,512]{1,0:T(8,128)(2,1)S(1)}, u32[]{:S(2)}, u32[]{:S(2)}) collective-permute-start(bf16[512,512]{1,0:T(8,128)(2,1)S(1)} %collective-permute-done.15), channel_id=1, source_target_pairs={{0,12},{1,13},{2,14},{3,15},{4,8},{5,9},{6,10},{7,11},{8,4},{9,5},... | collective-permute-start | bytes 1572872 | tf_op jit(solution)/shard_map/C3/ppermute | solution.py:117
  72.5 7.2 %copy-start.1 = (f32[1,512,512]{2,1,0:T(8,128)S(1)}, f32[1,512,512]{2,1,0:T(8,128)}, u32[]{:S(2)}) copy-start(f32[1,512,512]{2,1,0:T(8,128)} %param.9) | copy-start | bytes 3145732
  72.5 7.2 %copy-start.2 = (f32[512,512]{1,0:T(8,128)S(1)}, f32[512,512]{1,0:T(8,128)}, u32[]{:S(2)}) copy-start(f32[512,512]{1,0:T(8,128)} %param.7) | copy-start | bytes 3145732
  72.5 7.2 %copy-start.3 = (f32[512,512]{1,0:T(8,128)S(1)}, f32[512,512]{1,0:T(8,128)}, u32[]{:S(2)}) copy-start(f32[512,512]{1,0:T(8,128)} %param.8) | copy-start | bytes 3145732
  72.5 7.0 %collective-permute-start.22 = (f32[256,512]{1,0:T(8,128)S(1)}, f32[256,512]{1,0:T(8,128)S(1)}, u32[]{:S(2)}, u32[]{:S(2)}) collective-permute-start(f32[256,512]{1,0:T(8,128)S(1)} %pad_maximum_fusion.2), channel_id=1, source_target_pairs={{0,16},{16,0},{32,48},{48,32},{64,80},{80,64},{96,112},{112,96},{1... | collective-permute-start | bytes 1572872 | tf_op jit(solution)/shard_map/K6/ppermute | solution.py:117
